TPU v7x, 32 devices: a whole 2x2x4 slice. The times are simulated.
32 devices in a mesh: dp: 4 (over z), expert: 8 (over y, x, core).
Axes of the slice: x: 2, y: 2, z: 4, core: 2. Of those that a mesh axis runs over, the one named last changes fastest.
Arguments:
- tokens: bfloat16 [32, 1024, 768], P(('dp', 'expert')), may hold values from -6 to 6
- token_ids: int32 [32, 1024], P(('dp', 'expert')), may hold values from 0 to 8191, as said below
- hash_table: int32 [8192], replicated, may hold values from 0 to 7, as said below
- gain_one: float32 [768], replicated, may hold values from 0.5 to 1.5
- w_qkv: bfloat16 [768, 2304], replicated, may hold values from -0.21875 to 0.21875
- w_proj: bfloat16 [768, 768], replicated, may hold values from -0.875 to 0.875
- gain_two: float32 [768], replicated, may hold values from 0.5 to 1.5
- w_in: bfloat16 [8, 768, 3072], P('expert'), may hold values from -0.21875 to 0.21875
- w_out: bfloat16 [8, 768, 3072], P('expert'), may hold values from -0.109375 to 0.109375
- cotangent: bfloat16 [32, 1024, 768], P(('dp', 'expert')), may hold values from -10 to 10
Outputs:
- outputs: bfloat16 [32, 1024, 768], P(('dp', 'expert'))
- grad_tokens: float32 [32, 1024, 768], P(('dp', 'expert'))
- grad_gain_one: float32 [768], replicated
- grad_qkv: float32 [768, 2304], replicated
- grad_proj: float32 [768, 768], replicated
- grad_gain_two: float32 [768], replicated
- grad_w_in: float32 [8, 768, 3072], P('expert', None, 'dp')
- grad_w_out: float32 [8, 768, 3072], P('expert', None, 'dp')
Inputs may be any that keep to these rules, and one draw needn't show every extreme that they name: `token_ids`: among the 1024 tokens of one device, at most 256 have an id that hash_table gives to one expert; in every draw, in each dp group, every device has exactly 256 tokens of one common expert. `hash_table`: every expert is given exactly 1024 ids.
All inputs are finite; a program needn't handle non-finite values.
Results may differ from a plain program's by a relative error of at most 0.011.
Values may be sent and summed in bfloat16 or wider, within the bound.
No kernel may reach another device: no remote copies, remote signals or barrier semaphores. Data moves between devices by JAX's collectives and lax.ppermute only.
A program may use at most 256 MiB of HBM per device.

v0:
```python
import jax
import jax.numpy as jnp
from jax import lax
from jax.sharding import PartitionSpec as P

HEADS = 12
HEAD_DIM = 64


EPSILON = 1e-05
NEGATIVE = -1e30


def layer_norm(values, norm_gain):
    centred = values - jnp.mean(values, axis=-1, keepdims=True)
    spread = jnp.mean(centred * centred, axis=-1, keepdims=True)
    return centred * lax.rsqrt(spread + EPSILON) * norm_gain


def norm_back(values, norm_gain, upstream):
    _, pullback = jax.vjp(layer_norm, values, norm_gain)
    return pullback(upstream)


def smooth_unit(values):
    return jax.nn.gelu(values, approximate=True)


def unit_back(values, upstream):
    _, pullback = jax.vjp(smooth_unit, values)
    return pullback(upstream)[0]


def contract_rows(left_side, right_side):
    return lax.dot_general(
        left_side, right_side, (((0,), (0,)), ((), ())), preferred_element_type=jnp.float32
    )


def contract_last(left_side, right_side):
    return lax.dot_general(
        left_side, right_side, (((1,), (1,)), ((), ())), preferred_element_type=jnp.float32
    )


def heads_view(packed, head_count):
    model_width = packed.shape[1] // 3
    length = packed.shape[0]
    queries = packed[:, :model_width].reshape(length, head_count, -1)
    key_rows = packed[:, model_width : 2 * model_width].reshape(length, head_count, -1)
    value_rows = packed[:, 2 * model_width :].reshape(length, head_count, -1)
    return (queries, key_rows, value_rows)


def block_scores(queries, key_rows, begin_row, block_rows, score_scale):
    end_row = begin_row + block_rows
    scores = (
        jnp.einsum(
            "qhd,khd->hqk",
            queries[begin_row:end_row],
            key_rows[:end_row],
            preferred_element_type=jnp.float32,
        )
        * score_scale
    )
    allowed = jnp.arange(end_row)[None, :] <= (begin_row + jnp.arange(block_rows))[:, None]
    return jnp.where(allowed[None], scores, NEGATIVE)


def attend_forward(packed, head_count, block_rows, score_scale):
    queries, key_rows, value_rows = heads_view(packed, head_count)
    length = packed.shape[0]
    pieces = []
    totals = []
    for begin_row in range(0, length, block_rows):
        scores = block_scores(queries, key_rows, begin_row, block_rows, score_scale)
        highest = jnp.max(scores, axis=-1, keepdims=True)
        exponent = jnp.exp(scores - highest)
        summed = jnp.sum(exponent, axis=-1, keepdims=True)
        weights = (exponent / summed).astype(jnp.bfloat16)
        blended = jnp.einsum(
            "hqk,khd->qhd",
            weights,
            value_rows[: begin_row + block_rows],
            preferred_element_type=jnp.float32,
        )
        pieces.append(blended.reshape(block_rows, -1).astype(jnp.bfloat16))
        totals.append((highest + jnp.log(summed))[:, :, 0])
    return (jnp.concatenate(pieces, axis=0), jnp.concatenate(totals, axis=1))


def attend_back(packed, log_totals, grad_attended, head_count, block_rows, score_scale):
    queries, key_rows, value_rows = heads_view(packed, head_count)
    length = packed.shape[0]
    grad_heads = grad_attended.reshape(length, head_count, -1)
    grad_keys = jnp.zeros(key_rows.shape, jnp.float32)
    grad_values = jnp.zeros(value_rows.shape, jnp.float32)
    grad_queries = []
    for begin_row in range(0, length, block_rows):
        end_row = begin_row + block_rows
        scores = block_scores(queries, key_rows, begin_row, block_rows, score_scale)
        probabilities = jnp.exp(scores - log_totals[:, begin_row:end_row, None])
        weights = probabilities.astype(jnp.bfloat16)
        grad_here = grad_heads[begin_row:end_row]
        grad_probs = jnp.einsum(
            "qhd,khd->hqk", grad_here, value_rows[:end_row], preferred_element_type=jnp.float32
        )
        row_inner = jnp.sum(probabilities * grad_probs, axis=-1, keepdims=True)
        grad_scores = (probabilities * (grad_probs - row_inner)).astype(jnp.bfloat16)
        grad_block = jnp.einsum(
            "hqk,khd->qhd", grad_scores, key_rows[:end_row], preferred_element_type=jnp.float32
        )
        grad_queries.append((grad_block * score_scale).reshape(block_rows, -1))
        grad_keys = grad_keys.at[:end_row].add(
            jnp.einsum(
                "hqk,qhd->khd",
                grad_scores,
                queries[begin_row:end_row],
                preferred_element_type=jnp.float32,
            )
            * score_scale
        )
        grad_values = grad_values.at[:end_row].add(
            jnp.einsum("hqk,qhd->khd", weights, grad_here, preferred_element_type=jnp.float32)
        )
    joined = jnp.concatenate(
        [
            jnp.concatenate(grad_queries, axis=0),
            grad_keys.reshape(length, -1),
            grad_values.reshape(length, -1),
        ],
        axis=1,
    )
    return joined.astype(jnp.bfloat16)


def local(tokens, token_ids, hash_table, gain_one, w_qkv, w_proj, gain_two, w_in, w_out, cotangent):
    seq_count, length, model_width = tokens.shape
    row_count = seq_count * length
    head_count = HEADS
    score_scale = HEAD_DIM ** (-0.5)
    block_rows = min(512, length)
    inputs = tokens.reshape(row_count, model_width).astype(jnp.float32)
    normed_one = layer_norm(inputs, gain_one).astype(jnp.bfloat16)
    packed = jnp.dot(normed_one, w_qkv, preferred_element_type=jnp.float32).astype(jnp.bfloat16)
    packed_seq = packed.reshape(seq_count, length, -1)
    attended, log_totals = lax.map(
        lambda one_seq: attend_forward(one_seq, head_count, block_rows, score_scale), packed_seq
    )
    attended = attended.reshape(row_count, model_width)
    residual = inputs + jnp.dot(attended, w_proj, preferred_element_type=jnp.float32)
    normed_two = layer_norm(residual, gain_two).astype(jnp.bfloat16)
    experts_here = lax.axis_size("expert")
    capacity = 2 * row_count // experts_here
    choose = jnp.take(hash_table, token_ids.reshape(row_count))
    onehot_expert = (choose[:, None] == jnp.arange(experts_here)[None, :]).astype(jnp.int32)
    ranking = jnp.sum((jnp.cumsum(onehot_expert, axis=0) - 1) * onehot_expert, axis=1)
    target = choose * capacity + ranking
    placer = (jnp.arange(experts_here * capacity)[:, None] == target[None, :]).astype(jnp.bfloat16)
    outgoing = jnp.dot(placer, normed_two, preferred_element_type=jnp.float32).astype(jnp.bfloat16)
    outgoing = outgoing.reshape(experts_here, capacity, model_width)
    inner_weight = w_in[0]
    outer_weight = w_out[0]
    arrived = lax.all_to_all(outgoing, "expert", split_axis=0, concat_axis=0, tiled=True)
    hidden = jnp.dot(
        arrived.reshape(-1, model_width), inner_weight, preferred_element_type=jnp.float32
    )
    active = smooth_unit(hidden).astype(jnp.bfloat16)
    result = contract_last(active, outer_weight).astype(jnp.bfloat16).reshape(arrived.shape)
    returned = lax.all_to_all(result, "expert", split_axis=0, concat_axis=0, tiled=True)
    expert_part = contract_rows(placer, returned.reshape(-1, model_width))
    outputs = (residual + expert_part).astype(jnp.bfloat16).reshape(tokens.shape)
    upstream = cotangent.reshape(row_count, model_width)
    grad_send = jnp.dot(placer, upstream, preferred_element_type=jnp.float32).astype(jnp.bfloat16)
    grad_arrived = lax.all_to_all(
        grad_send.reshape(experts_here, capacity, model_width),
        "expert",
        split_axis=0,
        concat_axis=0,
        tiled=True,
    )
    flat_in = arrived.reshape(-1, model_width)
    flat_grad = grad_arrived.reshape(-1, model_width)
    hidden = jnp.dot(flat_in, inner_weight, preferred_element_type=jnp.float32)
    active = smooth_unit(hidden).astype(jnp.bfloat16)
    grad_active = jnp.dot(flat_grad, outer_weight, preferred_element_type=jnp.float32)
    grad_hidden = unit_back(hidden, grad_active).astype(jnp.bfloat16)
    grad_flat = contract_last(grad_hidden, inner_weight).astype(jnp.bfloat16)
    grad_back = lax.all_to_all(
        grad_flat.reshape(arrived.shape), "expert", split_axis=0, concat_axis=0, tiled=True
    )
    grad_inner = contract_rows(flat_in, grad_hidden)
    grad_outer = contract_rows(flat_grad, active)
    grad_w_in, grad_w_out = (
        lax.psum_scatter(
            grad_inner[None].astype(jnp.bfloat16), "dp", scatter_dimension=2, tiled=True
        ).astype(jnp.float32),
        lax.psum_scatter(
            grad_outer[None].astype(jnp.bfloat16), "dp", scatter_dimension=2, tiled=True
        ).astype(jnp.float32),
    )
    grad_normed_two = contract_rows(placer, grad_back.reshape(-1, model_width))
    grad_res_part, grad_gain_two = norm_back(residual, gain_two, grad_normed_two)
    grad_residual = upstream.astype(jnp.float32) + grad_res_part
    grad_attn = grad_residual.astype(jnp.bfloat16)
    grad_proj = contract_rows(attended, grad_attn)
    grad_attended = contract_last(grad_attn, w_proj).astype(jnp.bfloat16)
    grad_packed = lax.map(
        lambda scanned: attend_back(
            scanned[0], scanned[1], scanned[2], head_count, block_rows, score_scale
        ),
        (packed_seq, log_totals, grad_attended.reshape(seq_count, length, model_width)),
    )
    grad_packed = grad_packed.reshape(row_count, -1)
    grad_qkv = contract_rows(normed_one, grad_packed)
    grad_normed_one = contract_last(grad_packed, w_qkv)
    grad_in_part, grad_gain_one = norm_back(inputs, gain_one, grad_normed_one)
    grad_tokens = (grad_residual + grad_in_part).reshape(tokens.shape)
    grad_qkv, grad_proj, grad_gain_one, grad_gain_two = lax.psum(
        (grad_qkv, grad_proj, grad_gain_one, grad_gain_two), ("dp", "expert")
    )
    return (
        outputs,
        grad_tokens,
        grad_gain_one,
        grad_qkv,
        grad_proj,
        grad_gain_two,
        grad_w_in,
        grad_w_out,
    )


def solution(mesh):
    in_specs = (
        P(("dp", "expert"), None, None),
        P(("dp", "expert"), None),
        P(),
        P(),
        P(),
        P(),
        P(),
        P("expert", None, None),
        P("expert", None, None),
        P(("dp", "expert"), None, None),
    )
    out_specs = (
        P(("dp", "expert"), None, None),
        P(("dp", "expert"), None, None),
        P(),
        P(),
        P(),
        P(),
        P("expert", None, "dp"),
        P("expert", None, "dp"),
    )
    return jax.shard_map(local, mesh=mesh, in_specs=in_specs, out_specs=out_specs, check_vma=False)
```

profile of v0, /device:TPU:0, one launch (start us, length us, event | category | flops | bytes accessed | tf_op | source)
XLA Modules:
  0.0 640.9 jit_solution(8525737237297518981)
XLA Ops:
  24.2 5.8 gather_fusion
  30.7 5.0 reduce-window.6
  64.1 6.2 fusion.74
  70.3 10.7 %fusion.15 = (f32[12,512]{1,0:T(8,128)S(1)}, f32[12,512,1024]{2,1,0:T(8,128)}) fusion(pred[512,1024]{1,0:T(8,128)(4,1)S(1)} %copy-done.14, bf16[512,12,64]{0,2,1:T(8,128)(2,1)S(1)} %bitcast.175, bf16[1024,12,64]{0,2,1:T(8,128)(2,1)S(1)} %bitcast.171), kind=kOutput, calls=%fused_computation.30 | convolution fusion | flops 824174592 | bytes 28073984 | tf_op jit(solution)/shard_map/while/body/eval_jaxpr/qhd,khd->hqk/dot_general | solution.py:58
  81.0 12.3 %fusion.7 = f32[12,512]{1,0:T(8,128)S(1)} fusion(f32[12,512]{1,0:T(8,128)S(1)} %get-tuple-element.153, f32[12,512,1024]{2,1,0:T(8,128)} %get-tuple-element.154, pred[512,1024]{1,0:T(8,128)(4,1)S(1)} %copy-done.15), kind=kLoop, calls=%fused_computation.17 | loop fusion | flops 25159680 | bytes 25739264 | tf_op jit(solution)/shard_map/while/body/eval_jaxpr/reduce_sum | solution.py:79
  96.5 9.8 %fusion.75 = bf16[12,64,512]{2,1,0:T(8,128)(2,1)} fusion(bf16[1024,12,64]{0,2,1:T(8,128)(2,1)} %bitcast.179, f32[12,512]{1,0:T(8,128)S(1)} %fusion.7, f32[12,512]{1,0:T(8,128)S(1)} %get-tuple-element.153, f32[12,512,1024]{2,1,0:T(8,128)S(1)} %copy-done.1, pred[512,1024]{1,0:T(8,128)(4,1)} %iota_compare_fusion.9), kind=kOutput, calls=%fused_computation.103 | convolution fusion | flops 837156864 | bytes 28098560 | tf_op jit(solution)/shard_map/while/body/eval_jaxpr/hqk,khd->qhd/dot_general | solution.py:81
  110.6 5.5 fusion.55
  116.1 5.4 all-to-all-start
  125.5 6.5 %fusion.56 = bf16[2048,768]{1,0:T(8,128)(2,1)} fusion(s32[1024]{0:T(1024)S(1)} %bitcast.204, bf16[1,1024,768]{2,1,0:T(8,128)(2,1)} %param.31), kind=kOutput, calls=%fused_computation.73 | convolution fusion | flops 3224895488 | bytes 4722688 | tf_op jit(solution)/shard_map/dot_general | solution.py:174
  132.0 27.4 %all-to-all-done = bf16[8,256,768]{2,1,0:T(8,128)(2,1)} async-done(((bf16[8,256,768]{2,1,0:T(8,128)(2,1)}), bf16[8,256,768]{2,1,0:T(8,128)(2,1)}, u32[]{:S(2)}, u32[]{:S(2)}) %all-to-all-start) | async-done | bytes 3145760 | tf_op jit(solution)/shard_map/all_to_all | solution.py:164
  165.3 24.0 %multiply_convert_fusion.1 = (bf16[2048,3072]{1,0:T(8,128)(2,1)}, f32[2048,3072]{1,0:T(8,128)}) fusion(bf16[2048,768]{1,0:T(8,128)(2,1)} %bitcast.21, bf16[1,768,3072]{2,1,0:T(8,128)(2,1)} %param.29), kind=kOutput, calls=%fused_computation.13 | convolution fusion | flops 9720299520 | bytes 45613056 | tf_op jit(solution)/shard_map/dot_general | solution.py:165
  189.3 12.4 %all-to-all-done.2 = bf16[8,256,768]{2,1,0:T(8,128)(2,1)} async-done(((bf16[8,256,768]{2,1,0:T(8,128)(2,1)}), bf16[8,256,768]{2,1,0:T(8,128)(2,1)}, u32[]{:S(2)}, u32[]{:S(2)}) %all-to-all-start.2) | async-done | bytes 3145760 | tf_op jit(solution)/shard_map/all_to_all | solution.py:175
  201.8 15.4 %fusion.35 = bf16[1,768,3072]{2,1,0:T(8,128)(2,1)} fusion(bf16[2048,768]{1,0:T(8,128)(2,1)} %bitcast.29, bf16[2048,3072]{1,0:T(8,128)(2,1)} %get-tuple-element.159), kind=kOutput, calls=%fused_computation.54 | convolution fusion | flops 9666035712 | bytes 20447232 | tf_op jit(solution)/shard_map/dot_general | solution.py:35
  217.2 27.5 %fusion.6 = bf16[2048,3072]{1,0:T(8,128)(2,1)S(1)} fusion(f32[2048,3072]{1,0:T(8,128)} %get-tuple-element.160, bf16[2048,768]{1,0:T(8,128)(2,1)} %bitcast.29, bf16[1,768,3072]{2,1,0:T(8,128)(2,1)} %param.30), kind=kOutput, calls=%fused_computation.9 | convolution fusion | flops 9789505536 | bytes 45613056 | tf_op jit(solution)/shard_map/dot_general | solution.py:186
  244.6 14.9 %fusion.49 = bf16[2048,768]{1,0:T(8,128)(2,1)} fusion(bf16[2048,3072]{1,0:T(8,128)(2,1)S(1)} %fusion.6, bf16[1,768,3072]{2,1,0:T(8,128)(2,1)} %param.29), kind=kOutput, calls=%fused_computation.70 | convolution fusion | flops 9665249280 | bytes 20447232 | tf_op jit(solution)/shard_map/dot_general | solution.py:41
  264.1 15.8 %fusion.34 = bf16[1,768,3072]{2,1,0:T(8,128)(2,1)} fusion(bf16[2048,768]{1,0:T(8,128)(2,1)} %bitcast.21, bf16[2048,3072]{1,0:T(8,128)(2,1)} %copy-done.69), kind=kOutput, calls=%fused_computation.53 | convolution fusion | flops 9666035712 | bytes 20447232 | tf_op jit(solution)/shard_map/dot_general | solution.py:35
  279.9 15.5 %fusion.52 = bf16[2048,768]{1,0:T(8,128)(2,1)} fusion(bf16[2048,3072]{1,0:T(8,128)(2,1)} %get-tuple-element.159, bf16[1,768,3072]{2,1,0:T(8,128)(2,1)} %param.30), kind=kOutput, calls=%fused_computation.71 | convolution fusion | flops 9665249280 | bytes 20447232 | tf_op jit(solution)/shard_map/dot_general | solution.py:41
  295.4 6.5 %all-to-all-done.3 = bf16[8,256,768]{2,1,0:T(8,128)(2,1)} async-done(((bf16[8,256,768]{2,1,0:T(8,128)(2,1)}), bf16[8,256,768]{2,1,0:T(8,128)(2,1)}, u32[]{:S(2)}, u32[]{:S(2)}) %all-to-all-start.3) | async-done | bytes 3145760 | tf_op jit(solution)/shard_map/all_to_all | solution.py:189
  306.9 7.9 %multiply_reduce_fusion.2 = (f32[768]{0:T(1024)}, f32[1024]{0:T(1024)S(1)}, f32[1024,768]{0,1:T(8,128)S(1)}) fusion(f32[1024,768]{0,1:T(8,128)} %copy-done.17, f32[1024]{0:T(1024)S(1)} %copy-done.58, f32[1024]{0:T(1024)S(1)} %copy-done.50, f32[768]{0:T(1024)S(1)} %copy-done.61, bf16[2048,768]{1,0:T(8,128)(2,1)} %bitcast.31, s32[1024]{0:T(1024)S(1)} %bitcast.206), kind=kOutput, calls=%fused_computation.82 | convolution fusion | flops 3228825856 | bytes 9459712 | tf_op jit(solution)/shard_map/dot_general | solution.py:35
  323.0 7.7 %multiply_reduce_fusion.1 = (f32[12,512]{1,0:T(8,128)}, f32[12,512,512]{1,2,0:T(8,128)}) fusion(f32[12,512]{1,0:T(8,128)S(1)} %copy-done.38, f32[12,512,512]{1,2,0:T(8,128)S(1)} %bitcast.170, pred[512,512]{0,1:T(8,128)(4,1)S(1)} %copy-done.23, bf16[512,12,64]{0,2,1:T(8,128)(2,1)S(1)} %bitcast.183, bf16[512,12,64]{0,2,1:T(8,128)(2,1)S(1)} %bitcast.182), kind=kOutput, calls=%fused_computation.22 | convolution fusion | flops 418375680 | bytes 27049984 | tf_op jit(solution)/shard_map/while/body/eval_jaxpr/qhd,khd->hqk/dot_general | solution.py:105
  330.7 18.9 %multiply_reduce_fusion = (f32[12,512]{1,0:T(8,128)}, f32[12,512,1024]{2,1,0:T(8,128)}) fusion(f32[12,512]{1,0:T(8,128)} %log_add_fusion, f32[12,512,1024]{2,1,0:T(8,128)} %get-tuple-element.154, pred[512,1024]{1,0:T(8,128)(4,1)} %iota_compare_fusion.9, bf16[512,12,64]{0,2,1:T(8,128)(2,1)} %bitcast.189, bf16[1024,12,64]{0,2,1:T(8,128)(2,1)} %bitcast.180), kind=kOutput, calls=%fused_computation.11 | convolution fusion | flops 836757504 | bytes 53264384 | tf_op jit(solution)/shard_map/while/body/eval_jaxpr/qhd,khd->hqk/dot_general | solution.py:105
  349.6 10.2 %multiply_convert_fusion.2 = bf16[12,512,512]{1,2,0:T(8,128)(2,1)S(1)} fusion(f32[12,512,512]{1,2,0:T(8,128)} %get-tuple-element.163, f32[12,512]{1,0:T(8,128)} %get-tuple-element.162, f32[12,512]{1,0:T(8,128)} %log_add_fusion.1, f32[12,512,512]{1,2,0:T(8,128)} %copy-done.2, pred[512,512]{0,1:T(8,128)(4,1)} %iota_compare_fusion.14), kind=kLoop, calls=%fused_computation.21 | loop fusion | flops 18874368 | bytes 31768576 | tf_op jit(solution)/shard_map/while/body/eval_jaxpr/convert_element_type | solution.py:109
  361.9 17.4 %multiply_convert_fusion = bf16[12,512,1024]{2,1,0:T(8,128)(2,1)S(1)} fusion(f32[12,512,1024]{2,1,0:T(8,128)} %get-tuple-element.165, f32[12,512]{1,0:T(8,128)S(1)} %copy-done.40, f32[12,512]{1,0:T(8,128)S(1)} %copy-done.35, f32[12,512,1024]{2,1,0:T(8,128)} %get-tuple-element.154, pred[512,1024]{1,0:T(8,128)(4,1)S(1)} %copy-done.16), kind=kLoop, calls=%fused_computation.10 | loop fusion | flops 37748736 | bytes 63488000 | tf_op jit(solution)/shard_map/while/body/eval_jaxpr/convert_element_type | solution.py:109
  387.3 9.6 %multiply_convert_fusion.5 = bf16[12,64,512]{2,1,0:T(8,128)(2,1)} fusion(bf16[1024,12,64]{0,2,1:T(8,128)(2,1)S(1)} %bitcast.172, bf16[12,512,1024]{2,1,0:T(8,128)(2,1)} %copy-done.3), kind=kOutput, calls=%fused_computation.95 | convolution fusion | flops 806092800 | bytes 14942208 | tf_op jit(solution)/shard_map/while/body/eval_jaxpr/hqk,khd->qhd/dot_general | solution.py:110
  396.9 7.5 %fusion.71 = f32[512,12,64]{0,2,1:T(8,128)} fusion(bf16[512,12,64]{0,2,1:T(8,128)(2,1)S(1)} %bitcast.184, f32[12,512]{1,0:T(8,128)S(1)} %copy-done.39, f32[12,512,512]{1,2,0:T(8,128)} %copy-done.2, pred[512,512]{0,1:T(8,128)(4,1)S(1)} %copy-done.24), kind=kOutput, calls=%fused_computation.101 | convolution fusion | flops 415236096 | bytes 15228928 | tf_op jit(solution)/shard_map/while/body/eval_jaxpr/hqk,qhd->khd/dot_general | solution.py:124
  404.4 13.9 %fusion.61 = bf16[1024,12,64]{0,2,1:T(8,128)(2,1)} fusion(f32[512,12,64]{0,2,1:T(8,128)} %fusion.71, bf16[512,12,64]{0,2,1:T(8,128)(2,1)S(1)} %bitcast.190, f32[12,512]{1,0:T(8,128)S(1)} %copy-done.35, f32[12,512,1024]{2,1,0:T(8,128)} %get-tuple-element.154, pred[512,1024]{1,0:T(8,128)(4,1)S(1)} %copy-done.16), kind=kOutput, calls=%fused_computation.79 | convolution fusion | flops 832045056 | bytes 29646848 | tf_op jit(solution)/shard_map/while/body/eval_jaxpr/hqk,qhd->khd/dot_general | solution.py:124
  424.0 6.9 %fusion.77 = f32[768,2304]{1,0:T(8,128)} fusion(bf16[1024,768]{0,1:T(8,128)(2,1)S(1)} %bitcast.208, bf16[1024,768]{0,1:T(8,128)(2,1)S(1)} %bitcast.192, bf16[512,768]{0,1:T(8,128)(2,1)S(1)} %bitcast.196, bf16[512,768]{0,1:T(8,128)(2,1)S(1)} %bitcast.193, bf16[1,1024,768]{1,2,0:T(8,128)(2,1)S(1)} %copy-done.6, f32[768]{0:T(1024)S(1)} %copy-done.56, ...), kind=kOutput, calls=%fused_computation.106 | convolution fusion | flops 3646685184 | bytes 13380608 | tf_op jit(solution)/shard_map/dot_general | solution.py:35
  431.0 7.1 %fusion.70 = bf16[1,1024,768]{1,2,0:T(8,128)(2,1)} fusion(f32[1024,768]{0,1:T(8,128)} %copy-done.17, bf16[2048,768]{1,0:T(8,128)(2,1)} %bitcast.25, s32[1024]{0:T(1024)} %bitcast.205), kind=kOutput, calls=%fused_computation.100 | convolution fusion | flops 3224895488 | bytes 7868416 | tf_op jit(solution)/shard_map/dot_general | solution.py:35
  441.2 6.8 %fusion.60 = (f32[1024]{0:T(1024)S(1)}, f32[1024,768]{0,1:T(8,128)S(1)}) fusion(bf16[1,1024,768]{1,2,0:T(8,128)(2,1)} %copy.39, f32[768]{0:T(1024)S(1)} %copy-done.56, f32[1024]{0:T(1024)S(1)} %copy-done.45, bf16[768,2304]{1,0:T(8,128)(2,1)S(1)} %copy-done, bf16[1024,768]{0,1:T(8,128)(2,1)} %bitcast.207, bf16[1024,768]{0,1:T(8,128)(2,1)} %bitcast.191, ...), kind=kOutput, calls=%fused_computation.77 | convolution fusion | flops 3646684160 | bytes 12987392 | tf_op jit(solution)/shard_map/dot_general | solution.py:41
  457.3 42.5 %all-reduce.2 = (f32[768]{0:T(1024)}, f32[768]{0:T(1024)}) all-reduce(f32[768]{0:T(1024)S(1)} %copy-done.59, f32[768]{0:T(1024)S(1)} %copy-done.62), channel_id=1, replica_groups=mesh['dp'=4,'expert'=8] {'dp','expert'}, use_global_device_ids=true, to_apply=%region_18.19 | all-reduce | flops 1536 | bytes 12288 | tf_op jit(solution)/shard_map/psum | solution.py:219
  505.5 119.8 %all-reduce.6.cloned.1.call-done = (f32[768,2304]{1,0:T(8,128)}, f32[768,768]{1,0:T(8,128)}) async-done(((f32[768,2304]{1,0:T(8,128)}, f32[768,768]{1,0:T(8,128)}), (f32[768,2304]{1,0:T(8,128)}, f32[768,768]{1,0:T(8,128)})) %all-reduce.6.cloned.1.call-update) | async-done | bytes 9437200 | tf_op jit(solution)/shard_map/psum | solution.py:219
  625.3 6.6 %copy.63 = f32[768,2304]{1,0:T(8,128)} copy(f32[768,2304]{1,0:T(8,128)} %get-tuple-element.171) | data formatting | bytes 14155776
  (214 shorter events, 115.2 us)
Async XLA Ops:
  8.0 8.2 %copy-start = (bf16[768,2304]{1,0:T(8,128)(2,1)S(1)}, bf16[768,2304]{1,0:T(8,128)(2,1)}, u32[]{:S(2)}) copy-start(bf16[768,2304]{1,0:T(8,128)(2,1)} %param.26) | copy-start | bytes 10616836
  9.4 6.9 %copy-start.55 = (f32[768]{0:T(1024)S(1)}, f32[768]{0:T(1024)}, u32[]{:S(2)}) copy-start(f32[768]{0:T(1024)} %param.25) | copy-start | bytes 9220
  13.8 6.9 %copy-start.44 = (f32[1024]{0:T(1024)}, f32[1024]{0:T(1024)S(1)}, u32[]{:S(2)}) copy-start(f32[1024]{0:T(1024)S(1)} %broadcast_multiply_fusion.1) | copy-start | bytes 12292
  63.1 7.2 %copy-start.42 = (f32[12,512]{1,0:T(8,128)}, f32[12,512]{1,0:T(8,128)S(1)}, u32[]{:S(2)}) copy-start(f32[12,512]{1,0:T(8,128)S(1)} %fusion.13) | copy-start | bytes 73732
  70.3 10.7 %copy-start.15 = (pred[512,1024]{1,0:T(8,128)(4,1)S(1)}, pred[512,1024]{1,0:T(8,128)(4,1)}, u32[]{:S(2)}) copy-start(pred[512,1024]{1,0:T(8,128)(4,1)} %iota_compare_fusion.9) | copy-start | bytes 1572868
  81.0 12.4 %copy-start.36 = (f32[12,512]{1,0:T(8,128)}, f32[12,512]{1,0:T(8,128)S(1)}, u32[]{:S(2)}) copy-start(f32[12,512]{1,0:T(8,128)S(1)} %get-tuple-element.153) | copy-start | bytes 73732
  81.0 15.4 %copy-start.1 = (f32[12,512,1024]{2,1,0:T(8,128)S(1)}, f32[12,512,1024]{2,1,0:T(8,128)}, u32[]{:S(2)}) copy-start(f32[12,512,1024]{2,1,0:T(8,128)} %get-tuple-element.154) | copy-start | bytes 75497472
  93.4 12.9 %copy-start.41 = (f32[12,512]{1,0:T(8,128)}, f32[12,512]{1,0:T(8,128)S(1)}, u32[]{:S(2)}) copy-start(f32[12,512]{1,0:T(8,128)S(1)} %fusion.7) | copy-start | bytes 73732
  96.4 9.8 %copy-start.5 = (bf16[1,1024,768]{1,2,0:T(8,128)(2,1)S(1)}, bf16[1,1024,768]{1,2,0:T(8,128)(2,1)}, u32[]{:S(2)}) copy-start(bf16[1,1024,768]{1,2,0:T(8,128)(2,1)} %copy.39) | copy-start | bytes 4718596
  110.6 14.9 %copy-start.63 = (s32[1,1024]{1,0:T(1,128)}, s32[1,1024]{1,0:T(1,128)S(1)}, u32[]{:S(2)}) copy-start(s32[1,1024]{1,0:T(1,128)S(1)} %multiply_add_fusion.1) | copy-start | bytes 12292
  116.1 43.4 %all-to-all-start = ((bf16[8,256,768]{2,1,0:T(8,128)(2,1)}), bf16[8,256,768]{2,1,0:T(8,128)(2,1)}, u32[]{:S(2)}, u32[]{:S(2)}) async-start(bf16[8,256,768]{2,1,0:T(8,128)(2,1)} %bitcast.188), calls=%async_computation | async-start | bytes 6291456 | tf_op jit(solution)/shard_map/all_to_all | solution.py:164
  159.4 42.3 %all-to-all-start.2 = ((bf16[8,256,768]{2,1,0:T(8,128)(2,1)}), bf16[8,256,768]{2,1,0:T(8,128)(2,1)}, u32[]{:S(2)}, u32[]{:S(2)}) async-start(bf16[8,256,768]{2,1,0:T(8,128)(2,1)} %bitcast.187), calls=%async_computation.2 | async-start | bytes 6291456 | tf_op jit(solution)/shard_map/all_to_all | solution.py:175
  163.9 335.9 %reduce-scatter.5.cloned.1.call-start = ((), (), s32[]{:S(2)}) async-start(), calls=%async_computation.7 | async-start | bytes 5898240 | tf_op jit(solution)/shard_map/reduce_scatter | solution.py:198
  244.6 14.9 %copy-start.69 = (bf16[2048,3072]{1,0:T(8,128)(2,1)}, bf16[2048,3072]{1,0:T(8,128)(2,1)S(1)}, u32[]{:S(2)}) copy-start(bf16[2048,3072]{1,0:T(8,128)(2,1)S(1)} %fusion.6) | copy-start | bytes 37748740
  259.6 42.4 %all-to-all-start.3 = ((bf16[8,256,768]{2,1,0:T(8,128)(2,1)}), bf16[8,256,768]{2,1,0:T(8,128)(2,1)}, u32[]{:S(2)}, u32[]{:S(2)}) async-start(bf16[8,256,768]{2,1,0:T(8,128)(2,1)} %bitcast.186), calls=%async_computation.3 | async-start | bytes 6291456 | tf_op jit(solution)/shard_map/all_to_all | solution.py:189
  264.1 238.6 %reduce-scatter.3.cloned.1.call-start = ((), (), s32[]{:S(2)}) async-start(), calls=%async_computation.6 | async-start | bytes 5898240 | tf_op jit(solution)/shard_map/reduce_scatter | solution.py:195
  302.0 129.0 %all-to-all-start.1 = ((bf16[8,256,768]{2,1,0:T(8,128)(2,1)}), bf16[8,256,768]{2,1,0:T(8,128)(2,1)}, u32[]{:S(2)}, u32[]{:S(2)}) async-start(bf16[8,256,768]{2,1,0:T(8,128)(2,1)} %bitcast.185), calls=%async_computation.1 | async-start | bytes 6291456 | tf_op jit(solution)/shard_map/all_to_all | solution.py:170
  306.6 318.7 %all-reduce.6.cloned.1.call-start = ((), (), s32[]{:S(2)}) async-start(), calls=%async_computation.8 | async-start | bytes 18874368 | tf_op jit(solution)/shard_map/psum | solution.py:219
  306.8 7.9 %copy-start.54 = (f32[1024]{0:T(1024)S(1)}, f32[1024]{0:T(1024)}, u32[]{:S(2)}) copy-start(f32[1024]{0:T(1024)} %copy-done.53) | copy-start | bytes 12292
  306.9 7.9 %copy-start.18 = (f32[1024,768]{0,1:T(8,128)S(1)}, f32[1024,768]{0,1:T(8,128)}, u32[]{:S(2)}) copy-start(f32[1024,768]{0,1:T(8,128)} %copy-done.17) | copy-start | bytes 9437188
  321.3 9.4 %copy-start.26 = (bf16[512,768]{0,1:T(8,128)(2,1)}, bf16[512,768]{0,1:T(8,128)(2,1)S(1)}, u32[]{:S(2)}) copy-start(bf16[512,768]{0,1:T(8,128)(2,1)S(1)} %get-tuple-element.152) | copy-start | bytes 2359300
  349.6 10.2 %copy-start.22 = (bf16[512,768]{0,1:T(8,128)(2,1)S(1)}, bf16[512,768]{0,1:T(8,128)(2,1)}, u32[]{:S(2)}) copy-start(bf16[512,768]{0,1:T(8,128)(2,1)} %copy.41) | copy-start | bytes 2359300
  361.9 22.0 %copy-start.21 = (bf16[512,768]{0,1:T(8,128)(2,1)S(1)}, bf16[512,768]{0,1:T(8,128)(2,1)}, u32[]{:S(2)}) copy-start(bf16[512,768]{0,1:T(8,128)(2,1)} %copy.45) | copy-start | bytes 2359300
  387.3 9.6 %copy-start.24 = (pred[512,512]{0,1:T(8,128)(4,1)S(1)}, pred[512,512]{0,1:T(8,128)(4,1)}, u32[]{:S(2)}) copy-start(pred[512,512]{0,1:T(8,128)(4,1)} %iota_compare_fusion.14) | copy-start | bytes 786436
  387.3 9.6 %copy-start.27 = (bf16[512,768]{0,1:T(8,128)(2,1)S(1)}, bf16[512,768]{0,1:T(8,128)(2,1)}, u32[]{:S(2)}) copy-start(bf16[512,768]{0,1:T(8,128)(2,1)} %copy-done.26) | copy-start | bytes 2359300
  387.3 9.6 %copy-start.39 = (f32[12,512]{1,0:T(8,128)S(1)}, f32[12,512]{1,0:T(8,128)}, u32[]{:S(2)}) copy-start(f32[12,512]{1,0:T(8,128)} %log_add_fusion.1) | copy-start | bytes 73732
  396.9 7.5 %copy-start.28 = (bf16[512,768]{0,1:T(8,128)(2,1)S(1)}, bf16[512,768]{0,1:T(8,128)(2,1)}, u32[]{:S(2)}) copy-start(bf16[512,768]{0,1:T(8,128)(2,1)} %get-tuple-element.151) | copy-start | bytes 2359300
  404.4 13.9 %copy-start.33 = (bf16[1024,768]{0,1:T(8,128)(2,1)S(1)}, bf16[1024,768]{0,1:T(8,128)(2,1)}, u32[]{:S(2)}) copy-start(bf16[1024,768]{0,1:T(8,128)(2,1)} %copy-done.32) | copy-start | bytes 4718596
  404.4 13.9 %copy-start.67 = (bf16[12,64,512]{2,1,0:T(8,128)(2,1)S(1)}, bf16[12,64,512]{2,1,0:T(8,128)(2,1)}, u32[]{:S(2)}) copy-start(bf16[12,64,512]{2,1,0:T(8,128)(2,1)} %fusion.74) | copy-start | bytes 2359300
  404.4 13.9 %copy-start.68 = (bf16[12,64,512]{2,1,0:T(8,128)(2,1)S(1)}, bf16[12,64,512]{2,1,0:T(8,128)(2,1)}, u32[]{:S(2)}) copy-start(bf16[12,64,512]{2,1,0:T(8,128)(2,1)} %fusion.75) | copy-start | bytes 2359300
  441.2 6.8 %copy-start.52 = (f32[1024]{0:T(1024)S(1)}, f32[1024]{0:T(1024)}, u32[]{:S(2)}) copy-start(f32[1024]{0:T(1024)} %copy-done.51) | copy-start | bytes 12292
  441.2 6.9 %copy-start.7 = (bf16[1,1024,768]{1,2,0:T(8,128)(2,1)S(1)}, bf16[1,1024,768]{1,2,0:T(8,128)(2,1)}, u32[]{:S(2)}) copy-start(bf16[1,1024,768]{1,2,0:T(8,128)(2,1)} %copy.39) | copy-start | bytes 4718596
  (48 other events, 160.6 us)
Sparse Core Ops, SparseCore 0:
  217.3 85.2 reduce-scatter.4
  305.0 85.7 reduce-scatter.2
Sparse Core Ops, SparseCore 1:
  431.1 194.2 all-reduce.5
where the time goes:
time: 651 us; the launch traced here: 641 us
  matrix products  260 us (40%)
  waiting for transfers between devices  166 us (25%)
  other arithmetic  73.9 us (11%)
  local copies, waits for them, and re-layouts  62.7 us (10%)
  blocking collectives  42.5 us (7%)
  starting transfers between devices  19.2 us (3%)
  between operations  16.4 us (3%)
    psum x1, waiting for transfers between devices, local(): lax.psum((grad_qkv, grad_proj, grad_gain_one, grad_gain_two), ('dp', 'exp...  120 us
    dot_general x6, matrix products, contract_rows(): lax.dot_general(left_side, right_side, (((0,), (0,)), ((), ())), preferre...  55.9 us
    psum x1, blocking collectives, local(): lax.psum((grad_qkv, grad_proj, grad_gain_one, grad_gain_two), ('dp', 'exp...  42.5 us
    dot_general x4, matrix products, contract_last(): lax.dot_general(left_side, right_side, (((1,), (1,)), ((), ())), preferre...  38.6 us
    unnamed x152, local copies, waits for them, and re-layouts  36.4 us
    convert_element_type x2, other arithmetic, attend_back(): (probabilities * (grad_probs - row_inner)).astype(jnp.bfloat16)  27.5 us
    dot_general x1, matrix products, local(): jnp.dot(flat_grad, outer_weight, preferred_element_type=jnp.float32)  27.5 us
    all_to_all x1, waiting for transfers between devices, local(): lax.all_to_all(outgoing, 'expert', split_axis=0, concat_axis=0, tiled=True)  27.4 us
  transfers between devices with their start and end apart: 7, of which 4 were waited for; matrix products, arithmetic and copies ran while one was open for 40% of the time, Pallas kernels for 0%

commit v1 on v0

v1 whole, which is shorter than its diff:
```python
import functools
import math

import jax
import jax.numpy as jnp
from jax import lax
from jax.experimental import pallas as pl
from jax.experimental.pallas import tpu as pltpu
from jax.sharding import Mesh, PartitionSpec as P

HEADS = 12
HEAD_DIM = 64
EPSILON = 1e-05
NEGATIVE = -1e30
SCALE = HEAD_DIM ** (-0.5)
BF = jnp.bfloat16
F32 = jnp.float32
PLANE = ("y", "x", "core")


def nn(a, b):
    return lax.dot_general(a, b, (((1,), (0,)), ((), ())), preferred_element_type=F32)


def nt(a, b):
    return lax.dot_general(a, b, (((1,), (1,)), ((), ())), preferred_element_type=F32)


def tn(a, b):
    return lax.dot_general(a, b, (((0,), (0,)), ((), ())), preferred_element_type=F32)


def iota(shape, dim):
    return lax.broadcasted_iota(jnp.int32, shape, dim)


def call(body, flops=0, moved=0, limit=40, **kw):
    return pl.pallas_call(
        body,
        compiler_params=pltpu.CompilerParams(vmem_limit_bytes=limit << 20),
        cost_estimate=pl.CostEstimate(
            flops=int(flops), bytes_accessed=int(moved), transcendentals=0
        ),
        **kw,
    )


def whole(shape):
    return pl.BlockSpec(shape, lambda *i: (0,) * len(shape))


def norm_parts(v):
    centred = v - jnp.mean(v, axis=-1, keepdims=True)
    rate = lax.rsqrt(jnp.mean(centred * centred, axis=-1, keepdims=True) + EPSILON)
    return centred * rate, rate


def norm_grad(x_hat, rate, u):
    return rate * (
        u
        - jnp.mean(u, axis=-1, keepdims=True)
        - x_hat * jnp.mean(u * x_hat, axis=-1, keepdims=True)
    )


def route_body(ids_ref, table_ref, cot_ref, row_ref, col_ref, send_ref, *, experts, capacity):
    step = pl.program_id(0)
    count = ids_ref.shape[1]
    block = send_ref.shape[0]

    @pl.when(step == 0)
    def _():
        ids = ids_ref[...]
        table = table_ref[...].astype(BF)
        high = (iota((table.shape[0], count), 0) == (ids >> 7)).astype(BF)
        picked = tn(table, high)
        low = iota((128, count), 0) == (ids & 127)
        chosen = jnp.sum(jnp.where(low, picked, 0.0), axis=0, keepdims=True)
        slots = max(16, experts)
        member = iota((slots, count), 0).astype(F32) == chosen
        before = (iota((count, count), 0) < iota((count, count), 1)).astype(BF)
        earlier = nn(member.astype(BF), before)
        rank = jnp.sum(jnp.where(member, earlier, 0.0), axis=0, keepdims=True)
        target = chosen * capacity + rank
        row_ref[...] = target.astype(jnp.int32)
        turned = jnp.transpose(jnp.broadcast_to(target, (8, count)))
        col_ref[...] = turned[:, :1].astype(jnp.int32)

    placer = (iota((block, count), 0) + step * block == row_ref[...]).astype(BF)
    send_ref[...] = nn(placer, cot_ref[...]).astype(BF)


def route(ids, table, cot, experts, capacity):
    count, width = cot.shape
    slots = experts * capacity
    block = min(512, slots)
    return call(
        functools.partial(route_body, experts=experts, capacity=capacity),
        flops=2 * slots * count * width,
        moved=2 * (count + slots) * width,
        grid=(slots // block,),
        in_specs=[whole(ids.shape), whole(table.shape), whole(cot.shape)],
        out_specs=[
            whole((1, count)),
            whole((count, 1)),
            pl.BlockSpec((block, width), lambda i: (i, 0)),
        ],
        out_shape=[
            jax.ShapeDtypeStruct((1, count), jnp.int32),
            jax.ShapeDtypeStruct((count, 1), jnp.int32),
            jax.ShapeDtypeStruct((slots, width), BF),
        ],
    )(ids, table, cot)


def packed_body(x_ref, gain_ref, w_ref, packed_ref, turned_ref):
    x_hat, _ = norm_parts(x_ref[...].astype(F32))
    normed = (x_hat * gain_ref[...]).astype(BF)
    packed_ref[...] = nn(normed, w_ref[...]).astype(BF)
    turned_ref[...] = jnp.transpose(normed)


def make_packed(x, gain, w):
    count, width = x.shape
    wide = w.shape[1]
    block = 256
    return call(
        packed_body,
        flops=2 * count * width * wide,
        moved=2 * (count * (2 * width + wide) + width * wide),
        grid=(count // block,),
        in_specs=[
            pl.BlockSpec((block, width), lambda i: (i, 0)),
            whole(gain.shape),
            whole(w.shape),
        ],
        out_specs=[
            pl.BlockSpec((block, wide), lambda i: (i, 0)),
            pl.BlockSpec((width, block), lambda i: (0, i)),
        ],
        out_shape=[
            jax.ShapeDtypeStruct((count, wide), BF),
            jax.ShapeDtypeStruct((width, count), BF),
        ],
    )(x, gain, w)


def attend_body(q_ref, k_ref, v_ref, o_ref, total_ref, *, block):
    length = q_ref.shape[0]
    lane = iota((1, 128), 1)
    v_turned = jnp.transpose(v_ref[...])
    allowed = iota((block, block), 0) <= iota((block, block), 1)
    for row in range(length // block):
        end = (row + 1) * block
        outs = []
        for head in range(2):
            q = jnp.where(lane // 64 == head, q_ref[row * block : end, :] * BF(SCALE), BF(0))
            s = nt(k_ref[:end, :], q)
            last = jnp.where(allowed, s[end - block :], NEGATIVE)
            s = jnp.concatenate([s[: end - block], last], 0) if row else last
            highest = jnp.max(s, 0, keepdims=True)
            p = jnp.exp(s - highest)
            summed = jnp.sum(p, 0, keepdims=True)
            out = nn(v_turned[head * 64 : (head + 1) * 64, :end], p.astype(BF))
            outs.append(out * (1.0 / summed))
            total_ref[0, head : head + 1, row * block : end] = highest + jnp.log(summed)
        o_ref[row * block : end, :] = jnp.transpose(jnp.concatenate(outs, 0)).astype(BF)


def attend(packed):
    length = packed.shape[0]
    pairs = packed.shape[1] // 384
    part = lambda o: pl.BlockSpec((length, 128), lambda i: (0, o * pairs + i))
    return call(
        functools.partial(attend_body, block=min(512, length)),
        flops=1.2e10,
        moved=2 * length * pairs * 512,
        grid=(pairs,),
        in_specs=[part(0), part(1), part(2)],
        out_specs=[part(0), pl.BlockSpec((1, 2, length), lambda i: (i, 0, 0))],
        out_shape=[
            jax.ShapeDtypeStruct((length, pairs * 128), BF),
            jax.ShapeDtypeStruct((pairs, 2, length), F32),
        ],
    )(packed, packed, packed)


def attend_back_body(
    q_ref, k_ref, v_ref, o_ref, up_ref, total_ref, dq_ref, dk_ref, dv_ref, acc_ref, *, block
):
    length = q_ref.shape[0]
    count = length // block
    lane = iota((1, 128), 1)
    inner = jnp.transpose(o_ref[...].astype(F32) * up_ref[...].astype(F32))
    inner = [jnp.sum(inner[:64], 0, keepdims=True), jnp.sum(inner[64:], 0, keepdims=True)]
    allowed = iota((block, block), 0) <= iota((block, block), 1)
    for part in range(count):
        begin, end = part * block, (part + 1) * block
        k = k_ref[begin:end, :]
        v = v_ref[begin:end, :]
        dk, dv = [], []
        for head in range(2):
            mine = lane // 64 == head
            q = jnp.where(mine, q_ref[begin:, :] * BF(SCALE), BF(0))
            up = jnp.where(mine, up_ref[begin:, :], BF(0))
            s = nt(k, q) - total_ref[0, head : head + 1, begin:]
            first = jnp.where(allowed, s[:, :block], NEGATIVE)
            s = jnp.concatenate([first, s[:, block:]], 1) if part < count - 1 else first
            p = jnp.exp(s)
            ds = (p * (nt(v, up) - inner[head][:, begin:])).astype(BF)
            dv.append(nn(p.astype(BF), up))
            dk.append(nn(ds, q))
            dq = tn(ds, jnp.where(mine, k * BF(SCALE), BF(0)))
            if part == 0 and head == 0:
                acc_ref[...] = dq
            else:
                acc_ref[begin:, :] += dq
        dk_ref[begin:end, :] = (dk[0] + dk[1]).astype(BF)
        dv_ref[begin:end, :] = (dv[0] + dv[1]).astype(BF)
    dq_ref[...] = acc_ref[...].astype(BF)


def attend_back(packed, attended, totals, upstream):
    length = packed.shape[0]
    pairs = packed.shape[1] // 384
    part = lambda o: pl.BlockSpec((length, 128), lambda i: (0, o * pairs + i))
    return call(
        functools.partial(attend_back_body, block=min(256, length)),
        flops=3e10,
        moved=2 * length * pairs * 1024,
        grid=(pairs,),
        in_specs=[
            part(0), part(1), part(2), part(0), part(0),
            pl.BlockSpec((1, 2, length), lambda i: (i, 0, 0)),
        ],
        out_specs=[part(0)] * 3,
        out_shape=[jax.ShapeDtypeStruct((length, pairs * 128), BF)] * 3,
        scratch_shapes=[pltpu.VMEM((length, 128), F32)],
    )(packed, packed, packed, attended, upstream, totals)


def dispatch_body(att_ref, w_ref, x_ref, gain_ref, row_ref, res_ref, send_ref, normed_ref):
    step = pl.program_id(0)
    count = att_ref.shape[0]
    block = send_ref.shape[0]

    @pl.when(step == 0)
    def _():
        for begin in range(0, count, 256):
            rows = slice(begin, begin + 256)
            residual = x_ref[rows, :].astype(F32) + nn(att_ref[rows, :], w_ref[...])
            res_ref[rows, :] = residual
            x_hat, _ = norm_parts(residual)
            normed_ref[rows, :] = (x_hat * gain_ref[...]).astype(BF)

    placer = (iota((block, count), 0) + step * block == row_ref[...]).astype(BF)
    send_ref[...] = nn(placer, normed_ref[...]).astype(BF)


def dispatch(attended, w, x, gain, row, slots):
    count, width = x.shape
    block = min(512, slots)
    return call(
        dispatch_body,
        flops=2 * count * width * (slots + width),
        moved=2 * width * (5 * count + slots),
        grid=(slots // block,),
        in_specs=[whole(a.shape) for a in (attended, w, x, gain, row)],
        out_specs=[
            whole((count, width)),
            pl.BlockSpec((block, width), lambda i: (i, 0)),
        ],
        out_shape=[
            jax.ShapeDtypeStruct((count, width), F32),
            jax.ShapeDtypeStruct((slots, width), BF),
        ],
        scratch_shapes=[pltpu.VMEM((count, width), BF)],
    )(attended, w, x, gain, row)


def expert_body(x_ref, g_ref, w_ref, ga_ref, act_ref, gh_ref, dw_ref, turned_ref):
    @pl.when(pl.program_id(0) == 0)
    def _():
        turned_ref[...] = jnp.transpose(g_ref[...])

    c1 = 2.0 * math.sqrt(2.0 / math.pi)
    c2 = c1 * 0.044715
    for begin in range(0, x_ref.shape[0], 512):
        rows = slice(begin, begin + 512)
        h = nn(x_ref[rows, :], w_ref[...])
        square = h * h
        half = jnp.tanh(h * (0.5 * c1 + (0.5 * c2) * square)) * 0.5 + 0.5
        act = h * half
        slope = half + (act * (1.0 - half)) * (c1 + (3.0 * c2) * square)
        act_ref[rows, :] = act.astype(BF)
        gh_ref[rows, :] = (ga_ref[rows, :].astype(F32) * slope).astype(BF)
    dw_ref[...] = nn(turned_ref[...], act_ref[...]).astype(BF)


def expert(x, g, w, ga):
    rows, width = x.shape
    units = w.shape[1]
    block = min(512, units)
    column = pl.BlockSpec((rows, block), lambda i: (0, i))
    weight = pl.BlockSpec((width, block), lambda i: (0, i))
    return call(
        expert_body,
        flops=4 * rows * width * units,
        moved=2 * (2 * rows * width + 2 * width * units + 3 * rows * units),
        limit=48,
        grid=(units // block,),
        in_specs=[whole(x.shape), whole(g.shape), weight, column],
        out_specs=[column, column, weight],
        out_shape=[
            jax.ShapeDtypeStruct((rows, units), BF),
            jax.ShapeDtypeStruct((rows, units), BF),
            jax.ShapeDtypeStruct((width, units), BF),
        ],
        scratch_shapes=[pltpu.VMEM((width, rows), BF)],
    )(x, g, w, ga)


def collect_back_body(
    back_ref, col_ref, res_ref, cot_ref, gain_ref, w_ref, att_ref,
    gres_ref, gatt_ref, gproj_ref, ggain_ref, acc_ref,
):
    step = pl.program_id(0)
    block = col_ref.shape[0]
    slots = back_ref.shape[0]
    placer = (iota((block, slots), 1) == col_ref[...]).astype(BF)
    grad = nn(placer, back_ref[...])
    x_hat, rate = norm_parts(res_ref[...])
    gres = cot_ref[...].astype(F32) + norm_grad(x_hat, rate, grad * gain_ref[...])
    gres_ref[...] = gres
    gain_part = jnp.sum(grad * x_hat, axis=0, keepdims=True)
    gattn = gres.astype(BF)
    gatt_ref[...] = nt(gattn, w_ref[...]).astype(BF)
    part = tn(att_ref[...], gattn)

    @pl.when(step == 0)
    def _():
        acc_ref[...] = part
        ggain_ref[...] = gain_part

    @pl.when(step > 0)
    def _():
        acc_ref[...] += part
        ggain_ref[...] += gain_part

    @pl.when(step == pl.num_programs(0) - 1)
    def _():
        gproj_ref[...] = acc_ref[...].astype(BF)


def collect_back(back, col, residual, cot, gain, w, attended):
    count, width = cot.shape
    slots = back.shape[0]
    block = 256
    row = pl.BlockSpec((block, width), lambda i: (i, 0))
    return call(
        collect_back_body,
        flops=2 * count * width * (slots + 2 * width),
        moved=2 * width * (slots + 8 * count),
        grid=(count // block,),
        in_specs=[
            whole(back.shape), pl.BlockSpec((block, 1), lambda i: (i, 0)), row, row,
            whole(gain.shape), whole(w.shape), row,
        ],
        out_specs=[row, row, whole((width, width)), whole((1, width))],
        out_shape=[
            jax.ShapeDtypeStruct((count, width), F32),
            jax.ShapeDtypeStruct((count, width), BF),
            jax.ShapeDtypeStruct((width, width), BF),
            jax.ShapeDtypeStruct((1, width), F32),
        ],
        scratch_shapes=[pltpu.VMEM((width, width), F32)],
    )(back, col, residual, cot, gain, w, attended)


def collect_body(back_ref, col_ref, res_ref, out_ref):
    block, slots = col_ref.shape[0], back_ref.shape[0]
    placer = (iota((block, slots), 1) == col_ref[...]).astype(BF)
    out_ref[...] = (res_ref[...] + nn(placer, back_ref[...])).astype(BF)


def collect(back, col, residual):
    count, width = residual.shape
    block = 256
    row = pl.BlockSpec((block, width), lambda i: (i, 0))
    return call(
        collect_body,
        flops=2 * count * width * back.shape[0],
        moved=2 * width * (back.shape[0] + 3 * count),
        grid=(count // block,),
        in_specs=[whole(back.shape), pl.BlockSpec((block, 1), lambda i: (i, 0)), row],
        out_specs=row,
        out_shape=jax.ShapeDtypeStruct((count, width), BF),
    )(back, col, residual)


def grad_qkv_body(turned_ref, g_ref, out_ref):
    out_ref[...] = nn(turned_ref[...], g_ref[...]).astype(BF)


def weight_grad(turned, g):
    width, count = turned.shape
    wide = g.shape[1]
    block = min(384, wide)
    return call(
        grad_qkv_body,
        flops=2 * width * count * wide,
        moved=2 * (width * count + count * wide + width * wide),
        grid=(wide // block,),
        in_specs=[whole(turned.shape), pl.BlockSpec((count, block), lambda i: (0, i))],
        out_specs=pl.BlockSpec((width, block), lambda i: (0, i)),
        out_shape=jax.ShapeDtypeStruct((width, wide), BF),
    )(turned, g)


def grad_in_body(x_ref, gain_ref, w_ref, dq_ref, dk_ref, dv_ref, gres_ref, out_ref, ggain_ref):
    step = pl.program_id(0)
    width = x_ref.shape[1]
    x_hat, rate = norm_parts(x_ref[...].astype(F32))
    grad = nt(dq_ref[...], w_ref[:, :width])
    grad += nt(dk_ref[...], w_ref[:, width : 2 * width])
    grad += nt(dv_ref[...], w_ref[:, 2 * width :])
    out_ref[...] = gres_ref[...] + norm_grad(x_hat, rate, grad * gain_ref[...])
    part = jnp.sum(grad * x_hat, axis=0, keepdims=True)

    @pl.when(step == 0)
    def _():
        ggain_ref[...] = part

    @pl.when(step > 0)
    def _():
        ggain_ref[...] += part


def grad_in(x, gain, w, dq, dk, dv, gres):
    count, width = x.shape
    block = 256
    row = pl.BlockSpec((block, width), lambda i: (i, 0))
    return call(
        grad_in_body,
        flops=6 * count * width * width,
        moved=2 * width * 9 * count,
        grid=(count // block,),
        in_specs=[row, whole(gain.shape), whole(w.shape), row, row, row, row],
        out_specs=[row, whole((1, width))],
        out_shape=[
            jax.ShapeDtypeStruct((count, width), F32),
            jax.ShapeDtypeStruct((1, width), F32),
        ],
    )(x, gain, w, dq, dk, dv, gres)


def shift(a, axis, k):
    n = lax.axis_size(axis)
    return lax.ppermute(a, axis, [(i, (i + k) % n) for i in range(n)])


def cut(a, index, pieces, dim):
    size = a.shape[dim] // pieces
    return lax.dynamic_slice_in_dim(a, index * size, size, dim)


def scatter_sum(a, axis, dim):
    n = lax.axis_size(axis)
    me = lax.axis_index(axis)
    total = cut(a, me, n, dim).astype(F32)
    for k in range(1, n):
        total += shift(cut(a, lax.rem(me + k, n), n, dim), axis, k).astype(F32)
    return total.astype(a.dtype)


def gather_all(a, axis, dim):
    n = lax.axis_size(axis)
    me = lax.axis_index(axis)
    size = a.shape[dim]
    shape = a.shape[:dim] + (n * size,) + a.shape[dim + 1 :]
    out = lax.dynamic_update_slice_in_dim(jnp.zeros(shape, a.dtype), a, me * size, dim)
    for k in range(1, n):
        got = shift(a, axis, k)
        out = lax.dynamic_update_slice_in_dim(out, got, lax.rem(me - k + n, n) * size, dim)
    return out


def sum_all(a):
    a = scatter_sum(a, "core", 1)
    half = a.shape[0] // 2
    top = scatter_sum(scatter_sum(a[:half], "x", 0), "y", 0)
    low = scatter_sum(scatter_sum(a[half:], "y", 0), "x", 0)
    both = scatter_sum(jnp.stack([top, low]), "dp", 1)
    both = gather_all(both, "dp", 1)
    top = gather_all(gather_all(both[0], "y", 0), "x", 0)
    low = gather_all(gather_all(both[1], "x", 0), "y", 0)
    return gather_all(jnp.concatenate([top, low], 0), "core", 1)


def sum_small(a):
    for axis in ("core", "x", "y", "dp"):
        total = a
        for k in range(1, lax.axis_size(axis)):
            total = total + shift(a, axis, k)
        a = total
    return a


def local(tokens, token_ids, hash_table, gain_one, w_qkv, w_proj, gain_two, w_in, w_out, cotangent):
    width = tokens.shape[-1]
    x = tokens.reshape(-1, width)
    cot = cotangent.reshape(-1, width)
    count = x.shape[0]
    experts = lax.axis_size(PLANE)
    capacity = 2 * count // experts
    slots = experts * capacity
    first_gain = gain_one.reshape(1, width)
    second_gain = gain_two.reshape(1, width)
    inner, outer = w_in[0], w_out[0]

    def exchange(rows):
        moved = lax.all_to_all(
            rows.reshape(experts, capacity, width), PLANE, split_axis=0, concat_axis=0, tiled=True
        )
        return moved.reshape(slots, width)

    row, col, grad_send = route(
        token_ids.reshape(1, count), hash_table.reshape(-1, 128), cot, experts, capacity
    )
    flat_grad = exchange(grad_send)
    packed, turned = make_packed(x, first_gain, w_qkv)
    attended, totals = attend(packed)
    residual, outgoing = dispatch(attended, w_proj, x, second_gain, row, slots)
    flat_in = exchange(outgoing)
    grad_active = nn(flat_grad, outer).astype(BF)
    active, grad_hidden, grad_outer = expert(flat_in, flat_grad, inner, grad_active)
    grad_w_out = lax.psum_scatter(
        grad_outer[None], "dp", scatter_dimension=2, tiled=True
    ).astype(F32)
    grad_flat = nt(grad_hidden, inner).astype(BF)
    grad_back = exchange(grad_flat)
    grad_inner = tn(flat_in, grad_hidden).astype(BF)
    grad_w_in = lax.psum_scatter(
        grad_inner[None], "dp", scatter_dimension=2, tiled=True
    ).astype(F32)
    result = nt(active, outer).astype(BF)
    returned = exchange(result)

    grad_residual, grad_attended, grad_proj, grad_gain_two = collect_back(
        grad_back, col, residual, cot, second_gain, w_proj, attended
    )
    dq, dk, dv = attend_back(packed, attended, totals, grad_attended)
    grad_qkv = jnp.concatenate([weight_grad(turned, g) for g in (dq, dk, dv)], axis=1)
    grad_tokens, grad_gain_one = grad_in(x, first_gain, w_qkv, dq, dk, dv, grad_residual)
    outputs = collect(returned, col, residual)

    grad_proj = sum_all(grad_proj).astype(F32)
    grad_qkv = sum_all(grad_qkv).astype(F32)
    gains = sum_small(jnp.concatenate([grad_gain_one, grad_gain_two], 0))
    return (
        outputs.reshape(tokens.shape),
        grad_tokens.reshape(tokens.shape),
        gains[0],
        grad_qkv,
        grad_proj,
        gains[1],
        grad_w_in,
        grad_w_out,
    )


def solution(mesh):
    dp, experts = mesh.devices.shape
    side = math.isqrt(experts // 2)
    parts = Mesh(mesh.devices.reshape(dp, side, experts // 2 // side, 2), ("dp", "y", "x", "core"))
    rows = ("dp",) + PLANE
    in_specs = (
        P(rows, None, None),
        P(rows, None),
        P(),
        P(),
        P(),
        P(),
        P(),
        P(PLANE, None, None),
        P(PLANE, None, None),
        P(rows, None, None),
    )
    out_specs = (
        P(rows, None, None),
        P(rows, None, None),
        P(),
        P(),
        P(),
        P(),
        P(PLANE, None, "dp"),
        P(PLANE, None, "dp"),
    )
    return jax.shard_map(local, mesh=parts, in_specs=in_specs, out_specs=out_specs, check_vma=False)
```

time: 651 us -> 471 us (0.72)
  matrix products: 260 us -> 58 us
  Pallas kernels: 0 us -> 126 us
  other arithmetic: 73.9 us -> 16.8 us
  blocking collectives: 42.5 us -> 0 us
  starting transfers between devices: 19.2 us -> 57.9 us
  local copies, waits for them, and re-layouts: 62.7 us -> 32.8 us
  waiting for transfers between devices: 166 us -> 157 us
    dot_general x28 -> x4, matrix products: 260 us -> 58 us  [the longest x2 26.8 us: nt(): lax.dot_general(a, b, (((1,), (1,)), ((), ())), preferred_element_type=F32)]
    pallas_call x0 -> x12, Pallas kernels: none -> 126 us  [the longest x1 34.2 us: expert(): call(expert_body, flops=4 * rows * width * units, moved=2 * (2 * rows * w...]
    psum x1 -> x0, waiting for transfers between devices: 120 us -> none  [local(): lax.psum((grad_qkv, grad_proj, grad_gain_one, grad_gain_two), ('dp', 'exp...]
    ppermute x0 -> x38, waiting for transfers between devices: none -> 108 us  [shift(): return lax.ppermute(a, axis, [(i, (i + k) % n) for i in range(n)])]
    psum x1 -> x0, blocking collectives: 42.5 us -> none  [local(): lax.psum((grad_qkv, grad_proj, grad_gain_one, grad_gain_two), ('dp', 'exp...]
    ppermute x0 -> x38, starting transfers between devices: none -> 40.9 us  [shift(): return lax.ppermute(a, axis, [(i, (i + k) % n) for i in range(n)])]
    reduce_sum x8 -> x0, other arithmetic: 22.8 us -> none  [the longest x2 16.1 us: attend_forward(): summed = jnp.sum(exponent, axis=-1, keepdims=True)]
    convert_element_type x6 -> x10, other arithmetic: 34.5 us -> 13.7 us  [the longest x1 3.48 us: local(): grad_qkv = sum_all(grad_qkv).astype(F32)]
  transfers between devices with their start and end apart: 7 -> 44, of which waited for: 4 -> 23; matrix products, arithmetic and copies ran while one was open for 40% -> 14% of each run, Pallas kernels for 0% -> 19%
where the time goes in v1:
time: 471 us; the launch traced here: 464 us
  waiting for transfers between devices  157 us (33%)
  Pallas kernels  126 us (27%)
  matrix products  58 us (12%)
  starting transfers between devices  57.9 us (12%)
  local copies, waits for them, and re-layouts  32.8 us (7%)
  other arithmetic  16.8 us (4%)
  between operations  15.4 us (3%)
    ppermute x38, waiting for transfers between devices, shift(): return lax.ppermute(a, axis, [(i, (i + k) % n) for i in range(n)])  108 us
    all_to_all x4, waiting for transfers between devices, exchange(): lax.all_to_all(rows.reshape(experts, capacity, width), PLANE, split_axis=...  48 us
    ppermute x38, starting transfers between devices, shift(): return lax.ppermute(a, axis, [(i, (i + k) % n) for i in range(n)])  40.9 us
    pallas_call x1, Pallas kernels, expert(): call(expert_body, flops=4 * rows * width * units, moved=2 * (2 * rows * w...  34.2 us
    pallas_call x1, Pallas kernels, attend_back(): call(functools.partial(attend_back_body, block=min(256, length)), flops=3...  28.8 us
    dot_general x2, matrix products, nt(): lax.dot_general(a, b, (((1,), (1,)), ((), ())), preferred_element_type=F32)  26.8 us
    unnamed x76, local copies, waits for them, and re-layouts  25.8 us
    all_to_all x4, starting transfers between devices, exchange(): lax.all_to_all(rows.reshape(experts, capacity, width), PLANE, split_axis=...  16.7 us
  transfers between devices with their start and end apart: 44, of which 23 were waited for; matrix products, arithmetic and copies ran while one was open for 14% of the time, Pallas kernels for 19%

profile of v1, /device:TPU:0, one launch (start us, length us, event | category | flops | bytes accessed | tf_op | source)
XLA Modules:
  0.0 464.3 jit_solution(643581521271721182)
XLA Ops:
  10.0 5.5 %shard_map.163 = (s32[1,1024]{1,0:T(1,128)S(1)}, s32[1024,1]{1,0:T(8,128)S(1)}, bf16[2048,768]{1,0:T(8,128)(2,1)}) custom-call(s32[1,1024]{1,0:T(1,128)S(1)} %copy-done.11, s32[64,128]{1,0:T(8,128)S(1)} %bitcast.65, bf16[1024,768]{1,0:T(8,128)(2,1)S(1)} %bitcast.60), custom_call_target="tpu_custom_call" | custom-call | flops 3221225472 | bytes 4718592 | tf_op jit(solution)/shard_map/pallas_call | solution.py:97
  16.4 5.3 %all-to-all-start.1 = ((bf16[8,256,768]{2,1,0:T(8,128)(2,1)}), bf16[8,256,768]{2,1,0:T(8,128)(2,1)}, u32[]{:S(2)}, u32[]{:S(2)}) async-start(bf16[8,256,768]{2,1,0:T(8,128)(2,1)} %bitcast.5), calls=%async_computation.1 | async-start | bytes 6291456 | tf_op jit(solution)/shard_map/all_to_all | solution.py:522
  23.7 5.4 %shard_map.161 = (bf16[1024,2304]{1,0:T(8,128)(2,1)S(1)}, bf16[768,1024]{1,0:T(8,128)(2,1)S(1)}) custom-call(bf16[1024,768]{1,0:T(8,128)(2,1)S(1)} %bitcast.62, f32[1,768]{1,0:T(1,128)S(1)} %reshape.62.gain_ref, bf16[768,2304]{1,0:T(8,128)(2,1)S(1)} %copy-done.2), custom_call_target="tpu_custom_call" | custom-call | flops 3623878656 | bytes 11403264 | tf_op jit(solution)/shard_map/pallas_call | solution.py:127
  29.2 16.3 %shard_map.162 = (bf16[1024,768]{1,0:T(8,128)(2,1)S(1)}, f32[6,2,1024]{2,1,0:T(2,128)S(1)}) custom-call(bf16[1024,2304]{1,0:T(8,128)(2,1)S(1)} %get-tuple-element.29.q_ref.k_ref.v_ref, bf16[1024,2304]{1,0:T(8,128)(2,1)S(1)} %get-tuple-element.29.q_ref.k_ref.v_ref, bf16[1024,2304]{1,0:T(8,128)(2,1)S(1)} %get-tuple-element.29.q_ref.k_ref.v_ref), custom_call_target="tpu_custom_call" | custom-call | flops 12000000000 | bytes 6291456 | tf_op jit(solution)/shard_map/pallas_call | solution.py:174
  45.5 5.8 %shard_map.164 = (f32[1024,768]{1,0:T(8,128)S(1)}, bf16[2048,768]{1,0:T(8,128)(2,1)S(1)}) custom-call(bf16[1024,768]{1,0:T(8,128)(2,1)S(1)} %get-tuple-element.30.att_ref.o_ref, bf16[768,768]{1,0:T(8,128)(2,1)S(1)} %copy-done.8, bf16[1024,768]{1,0:T(8,128)(2,1)S(1)} %bitcast.63, f32[1,768]{1,0:T(1,128)S(1)} %reshape.63.gain_ref, ...), custom_call_target="tpu_custom_call" | custom-call | flops 4429185024 | bytes 11010048 | tf_op jit(solution)/shard_map/pallas_call | solution.py:263
  55.8 3.8 all-to-all-done.1
  59.7 4.1 all-to-all-start
  63.8 15.6 %convolution_convert_fusion.ga_ref = bf16[2048,3072]{1,0:T(8,128)(2,1)} fusion(bf16[2048,768]{1,0:T(8,128)(2,1)} %bitcast.6.g_ref, bf16[1,768,3072]{2,1,0:T(8,128)(2,1)} %param.18), kind=kOutput, calls=%fused_computation | convolution fusion | flops 9669967872 | bytes 20447232 | tf_op jit(solution)/shard_map/dot_general | solution.py:22
  79.4 22.2 %all-to-all-done = bf16[8,256,768]{2,1,0:T(8,128)(2,1)S(1)} async-done(((bf16[8,256,768]{2,1,0:T(8,128)(2,1)}), bf16[8,256,768]{2,1,0:T(8,128)(2,1)S(1)}, u32[]{:S(2)}, u32[]{:S(2)}) %all-to-all-start) | async-done | bytes 3145760 | tf_op jit(solution)/shard_map/all_to_all | solution.py:522
  101.6 34.2 %shard_map.165 = (bf16[2048,3072]{1,0:T(8,128)(2,1)}, bf16[2048,3072]{1,0:T(8,128)(2,1)}, bf16[768,3072]{1,0:T(8,128)(2,1)}) custom-call(bf16[2048,768]{1,0:T(8,128)(2,1)S(1)} %bitcast.57, bf16[2048,768]{1,0:T(8,128)(2,1)} %bitcast.6.g_ref, bf16[768,3072]{1,0:T(8,128)(2,1)} %bitcast.69, bf16[2048,3072]{1,0:T(8,128)(2,1)} %convolution_convert_fusion.ga_ref), custom_call_target="tpu_custom_call" | custom-call | flops 19327352832 | bytes 53477376 | tf_op jit(solution)/shard_map/pallas_call | solution.py:306
  135.8 15.4 %convolution_convert_fusion.2 = bf16[2048,768]{1,0:T(8,128)(2,1)} fusion(bf16[2048,3072]{1,0:T(8,128)(2,1)} %get-tuple-element.37, bf16[1,768,3072]{2,1,0:T(8,128)(2,1)} %param.17), kind=kOutput, calls=%fused_computation.9 | convolution fusion | flops 9665249280 | bytes 20447232 | tf_op jit(solution)/shard_map/dot_general | solution.py:26
  151.3 3.7 all-to-all-start.3
  155.2 15.5 %fusion.3 = bf16[1,768,3072]{2,1,0:T(8,128)(2,1)} fusion(bf16[2048,768]{1,0:T(8,128)(2,1)} %bitcast.58, bf16[2048,3072]{1,0:T(8,128)(2,1)} %get-tuple-element.37), kind=kOutput, calls=%fused_computation.5 | convolution fusion | flops 9666035712 | bytes 20447232 | tf_op jit(solution)/shard_map/dot_general | solution.py:30
  170.8 22.0 %all-to-all-done.3 = bf16[8,256,768]{2,1,0:T(8,128)(2,1)S(1)} async-done(((bf16[8,256,768]{2,1,0:T(8,128)(2,1)}), bf16[8,256,768]{2,1,0:T(8,128)(2,1)S(1)}, u32[]{:S(2)}, u32[]{:S(2)}) %all-to-all-start.3) | async-done | bytes 3145760 | tf_op jit(solution)/shard_map/all_to_all | solution.py:522
  197.9 11.8 %shard_map.167 = (f32[1024,768]{1,0:T(8,128)S(1)}, bf16[1024,768]{1,0:T(8,128)(2,1)S(1)}, bf16[768,768]{1,0:T(8,128)(2,1)S(1)}, f32[1,768]{1,0:T(1,128)S(1)}) custom-call(bf16[2048,768]{1,0:T(8,128)(2,1)S(1)} %bitcast.56, s32[1024,1]{1,0:T(8,128)S(1)} %copy-done.21, f32[1024,768]{1,0:T(8,128)} %copy-done.16, bf16[1024,768]{1,0:T(8,128)(2,1)S(1)} %bitcast.61, ...), custom_call_target="tpu_custom_call" | custom-call | flops 5637144576 | bytes 15728640 | tf_op jit(solution)/shard_map/pallas_call | solution.py:360
  215.2 28.8 %shard_map.168 = (bf16[1024,768]{1,0:T(8,128)(2,1)S(1)}, bf16[1024,768]{1,0:T(8,128)(2,1)S(1)}, bf16[1024,768]{1,0:T(8,128)(2,1)S(1)}) custom-call(bf16[1024,2304]{1,0:T(8,128)(2,1)S(1)} %copy-done.19, bf16[1024,2304]{1,0:T(8,128)(2,1)S(1)} %copy-done.19, bf16[1024,2304]{1,0:T(8,128)(2,1)S(1)} %copy-done.19, bf16[1024,768]{1,0:T(8,128)(2,1)S(1)} %copy-done.25, ...), custom_call_target="tpu_custom_call" | custom-call | flops 30000001024 | bytes 12582912 | tf_op jit(solution)/shard_map/pallas_call | solution.py:227
  244.1 6.8 %shard_map.169 = (f32[1024,768]{1,0:T(8,128)}, f32[1,768]{1,0:T(1,128)S(1)}) custom-call(bf16[1024,768]{1,0:T(8,128)(2,1)S(1)} %bitcast.64, f32[1,768]{1,0:T(1,128)S(1)} %reshape.62.gain_ref, bf16[768,2304]{1,0:T(8,128)(2,1)S(1)} %copy-done.3, bf16[1024,768]{1,0:T(8,128)(2,1)S(1)} %get-tuple-element.40.dq_ref.g_ref, ...), custom_call_target="tpu_custom_call" | custom-call | flops 3623878656 | bytes 14155776 | tf_op jit(solution)/shard_map/pallas_call | solution.py:443
  273.5 4.3 collective-permute-start.29
  283.7 11.4 %fusion.4 = bf16[2048,768]{1,0:T(8,128)(2,1)} fusion(bf16[2048,3072]{1,0:T(8,128)(2,1)S(1)} %bitcast.75, bf16[1,768,3072]{2,1,0:T(8,128)(2,1)S(1)} %bitcast.71), kind=kOutput, calls=%fused_computation.8 | convolution fusion | flops 9665249280 | bytes 20447232 | tf_op jit(solution)/shard_map/dot_general | solution.py:26
  295.1 3.6 all-to-all-start.2
  299.6 3.9 collective-permute-start.5
  312.7 32.5 %collective-permute-done.7 = bf16[192,1152]{1,0:T(8,128)(2,1)S(1)} collective-permute-done((bf16[192,1152]{1,0:T(8,128)(2,1)S(1)}, bf16[192,1152]{1,0:T(8,128)(2,1)S(1)}, u32[]{:S(2)}, u32[]{:S(2)}) %collective-permute-start.7) | collective-permute-done | bytes 442400 | tf_op jit(solution)/shard_map/ppermute | solution.py:459
  347.7 4.8 %collective-permute-done.8 = bf16[96,1152]{1,0:T(8,128)(2,1)S(1)} collective-permute-done((bf16[96,1152]{1,0:T(8,128)(2,1)S(1)}, bf16[96,1152]{1,0:T(8,128)(2,1)S(1)}, u32[]{:S(2)}, u32[]{:S(2)}) %collective-permute-start.8) | collective-permute-done | bytes 221216 | tf_op jit(solution)/shard_map/ppermute | solution.py:459
  354.0 3.8 collective-permute-start.13
  358.5 6.5 %collective-permute-done.13 = bf16[2,24,1152]{2,1,0:T(8,128)(2,1)S(1)} collective-permute-done((bf16[2,24,1152]{2,1,0:T(8,128)(2,1)S(1)}, bf16[2,24,1152]{2,1,0:T(8,128)(2,1)S(1)}, u32[]{:S(2)}, u32[]{:S(2)}) %collective-permute-start.13) | collective-permute-done | bytes 110624 | tf_op jit(solution)/shard_map/ppermute | solution.py:459
  365.0 17.0 %collective-permute-done.12 = bf16[2,24,1152]{2,1,0:T(8,128)(2,1)S(1)} collective-permute-done((bf16[2,24,1152]{2,1,0:T(8,128)(2,1)S(1)}, bf16[2,24,1152]{2,1,0:T(8,128)(2,1)S(1)}, u32[]{:S(2)}, u32[]{:S(2)}) %collective-permute-start.12) | collective-permute-done | bytes 110624 | tf_op jit(solution)/shard_map/ppermute | solution.py:459
  383.2 8.3 %collective-permute-done.14 = bf16[2,24,1152]{2,1,0:T(8,128)(2,1)S(1)} collective-permute-done((bf16[2,24,1152]{2,1,0:T(8,128)(2,1)S(1)}, bf16[2,24,1152]{2,1,0:T(8,128)(2,1)S(1)}, u32[]{:S(2)}, u32[]{:S(2)}) %collective-permute-start.14) | collective-permute-done | bytes 110624 | tf_op jit(solution)/shard_map/ppermute | solution.py:459
  391.8 8.4 %collective-permute-done.15 = bf16[2,24,1152]{2,1,0:T(8,128)(2,1)S(1)} collective-permute-done((bf16[2,24,1152]{2,1,0:T(8,128)(2,1)S(1)}, bf16[2,24,1152]{2,1,0:T(8,128)(2,1)S(1)}, u32[]{:S(2)}, u32[]{:S(2)}) %collective-permute-start.15) | collective-permute-done | bytes 110624 | tf_op jit(solution)/shard_map/ppermute | solution.py:459
  404.3 3.6 collective-permute-done.19
  411.6 7.5 %collective-permute-done.20 = bf16[192,1152]{1,0:T(8,128)(2,1)S(1)} collective-permute-done((bf16[192,1152]{1,0:T(8,128)(2,1)S(1)}, bf16[192,1152]{1,0:T(8,128)(2,1)S(1)}, u32[]{:S(2)}, u32[]{:S(2)}) %collective-permute-start.20) | collective-permute-done | bytes 442400 | tf_op jit(solution)/shard_map/ppermute | solution.py:459
  437.5 4.9 %shard_map.166 = bf16[1024,768]{1,0:T(8,128)(2,1)} custom-call(bf16[2048,768]{1,0:T(8,128)(2,1)S(1)} %bitcast.55, s32[1024,1]{1,0:T(8,128)S(1)} %copy-done.22, f32[1024,768]{1,0:T(8,128)S(1)} %copy-done.17), custom_call_target="tpu_custom_call" | custom-call | flops 3221225472 | bytes 7864320 | tf_op jit(solution)/shard_map/pallas_call | solution.py:390
  447.8 3.5 convert_element_type.167
  (231 shorter events, 102.5 us)
Async XLA Ops:
  16.4 43.3 %all-to-all-start.1 = ((bf16[8,256,768]{2,1,0:T(8,128)(2,1)}), bf16[8,256,768]{2,1,0:T(8,128)(2,1)}, u32[]{:S(2)}, u32[]{:S(2)}) async-start(bf16[8,256,768]{2,1,0:T(8,128)(2,1)} %bitcast.5), calls=%async_computation.1 | async-start | bytes 6291456 | tf_op jit(solution)/shard_map/all_to_all | solution.py:522
  59.7 41.9 %all-to-all-start = ((bf16[8,256,768]{2,1,0:T(8,128)(2,1)}), bf16[8,256,768]{2,1,0:T(8,128)(2,1)S(1)}, u32[]{:S(2)}, u32[]{:S(2)}) async-start(bf16[8,256,768]{2,1,0:T(8,128)(2,1)} %bitcast.59), calls=%async_computation | async-start | bytes 6291456 | tf_op jit(solution)/shard_map/all_to_all | solution.py:522
  151.3 41.5 %all-to-all-start.3 = ((bf16[8,256,768]{2,1,0:T(8,128)(2,1)}), bf16[8,256,768]{2,1,0:T(8,128)(2,1)S(1)}, u32[]{:S(2)}, u32[]{:S(2)}) async-start(bf16[8,256,768]{2,1,0:T(8,128)(2,1)} %bitcast.68), calls=%async_computation.3 | async-start | bytes 6291456 | tf_op jit(solution)/shard_map/all_to_all | solution.py:522
  154.9 296.4 %reduce-scatter.3.cloned.1.call-start = ((), (), s32[]{:S(2)}) async-start(), calls=%async_computation.6 | async-start | bytes 5898240 | tf_op jit(solution)/shard_map/reduce_scatter | solution.py:543
  250.9 11.1 %collective-permute-start = (f32[2,768]{1,0:T(2,128)S(1)}, f32[2,768]{1,0:T(2,128)S(1)}, u32[]{:S(2)}, u32[]{:S(2)}) collective-permute-start(f32[2,768]{1,0:T(2,128)S(1)} %pad_maximum_fusion.3), channel_id=1, source_target_pairs={{0,1},{1,0},{2,3},{3,2},{4,5},{5,4},{6,7},{7,6},{8,9},{9,8},{10,11... | collective-permute-start | bytes 18440 | tf_op jit(solution)/shard_map/ppermute | solution.py:459
  251.0 9.1 %collective-permute-start.22 = (bf16[768,384]{1,0:T(8,128)(2,1)S(1)}, bf16[768,384]{1,0:T(8,128)(2,1)S(1)}, u32[]{:S(2)}, u32[]{:S(2)}) collective-permute-start(bf16[768,384]{1,0:T(8,128)(2,1)S(1)} %constant_dynamic-slice_fusion.4), channel_id=1, source_target_pairs={{0,1},{1,0},{2,3},{3,2},{4,5},{5,4},{6,7},{7,6},{8,9},{9,8},{10,11... | collective-permute-start | bytes 1769480 | tf_op jit(solution)/shard_map/ppermute | solution.py:459
  260.1 46.3 %collective-permute-start.6 = (bf16[768,1152]{1,0:T(8,128)(2,1)}, bf16[768,1152]{1,0:T(8,128)(2,1)}, u32[]{:S(2)}, u32[]{:S(2)}) collective-permute-start(bf16[768,1152]{1,0:T(8,128)(2,1)} %constant_dynamic-slice_fusion.9), channel_id=1, source_target_pairs={{0,1},{1,0},{2,3},{3,2},{4,5},{5,4},{6,7},{7,6},{8,9},{9,8},{10,11... | collective-permute-start | bytes 5308424 | tf_op jit(solution)/shard_map/ppermute | solution.py:459
  262.1 16.7 %collective-permute-start.1 = (f32[2,768]{1,0:T(2,128)S(1)}, f32[2,768]{1,0:T(2,128)S(1)}, u32[]{:S(2)}, u32[]{:S(2)}) collective-permute-start(f32[2,768]{1,0:T(2,128)S(1)} %fusion.20), channel_id=1, source_target_pairs={{0,2},{2,0},{1,3},{3,1},{4,6},{6,4},{5,7},{7,5},{8,10},{10,8},{9,1... | collective-permute-start | bytes 18440 | tf_op jit(solution)/shard_map/ppermute | solution.py:459
  278.8 20.7 %collective-permute-start.2 = (f32[2,768]{1,0:T(2,128)S(1)}, f32[2,768]{1,0:T(2,128)S(1)}, u32[]{:S(2)}, u32[]{:S(2)}) collective-permute-start(f32[2,768]{1,0:T(2,128)S(1)} %fusion.28), channel_id=1, source_target_pairs={{0,4},{4,0},{1,5},{5,1},{2,6},{6,2},{3,7},{7,3},{8,12},{12,8},{9,1... | collective-permute-start | bytes 18440 | tf_op jit(solution)/shard_map/ppermute | solution.py:459
  283.6 22.7 %collective-permute-start.30 = (bf16[2,24,384]{2,1,0:T(8,128)(2,1)S(1)}, bf16[2,24,384]{2,1,0:T(8,128)(2,1)S(1)}, u32[]{:S(2)}, u32[]{:S(2)}) collective-permute-start(bf16[2,24,384]{2,1,0:T(8,128)(2,1)S(1)} %get-tuple-element.53), channel_id=1, source_target_pairs={{0,8},{8,16},{16,24},{24,0},{1,9},{9,17},{17,25},{25,1},{2,10},{10... | collective-permute-start | bytes 110600 | tf_op jit(solution)/shard_map/ppermute | solution.py:459
  295.1 139.4 %all-to-all-start.2 = ((bf16[8,256,768]{2,1,0:T(8,128)(2,1)}), bf16[8,256,768]{2,1,0:T(8,128)(2,1)S(1)}, u32[]{:S(2)}, u32[]{:S(2)}) async-start(bf16[8,256,768]{2,1,0:T(8,128)(2,1)} %bitcast.67), calls=%async_computation.2 | async-start | bytes 6291456 | tf_op jit(solution)/shard_map/all_to_all | solution.py:522
  298.8 155.4 %reduce-scatter.5.cloned.1.call-start = ((), (), s32[]{:S(2)}) async-start(), calls=%async_computation.7 | async-start | bytes 5898240 | tf_op jit(solution)/shard_map/reduce_scatter | solution.py:537
  299.6 142.8 %collective-permute-start.5 = (f32[2,768]{1,0:T(2,128)S(1)}, f32[2,768]{1,0:T(2,128)S(1)}, u32[]{:S(2)}, u32[]{:S(2)}) collective-permute-start(f32[2,768]{1,0:T(2,128)S(1)} %add.112), channel_id=1, source_target_pairs={{0,24},{8,0},{16,8},{24,16},{1,25},{9,1},{17,9},{25,17},{2,26},{10... | collective-permute-start | bytes 18440 | tf_op jit(solution)/shard_map/ppermute | solution.py:459
  303.4 139.0 %collective-permute-start.4 = (f32[2,768]{1,0:T(2,128)S(1)}, f32[2,768]{1,0:T(2,128)S(1)}, u32[]{:S(2)}, u32[]{:S(2)}) collective-permute-start(f32[2,768]{1,0:T(2,128)S(1)} %add.112), channel_id=1, source_target_pairs={{0,16},{8,24},{16,0},{24,8},{1,17},{9,25},{17,1},{25,9},{2,18},{10... | collective-permute-start | bytes 18440 | tf_op jit(solution)/shard_map/ppermute | solution.py:459
  303.4 7.6 %collective-permute-start.31 = (bf16[2,24,384]{2,1,0:T(8,128)(2,1)S(1)}, bf16[2,24,384]{2,1,0:T(8,128)(2,1)S(1)}, u32[]{:S(2)}, u32[]{:S(2)}) collective-permute-start(bf16[2,24,384]{2,1,0:T(8,128)(2,1)S(1)} %get-tuple-element.53), channel_id=1, source_target_pairs={{0,16},{8,24},{16,0},{24,8},{1,17},{9,25},{17,1},{25,9},{2,18},{10... | collective-permute-start | bytes 110600 | tf_op jit(solution)/shard_map/ppermute | solution.py:459
  309.1 36.1 %collective-permute-start.7 = (bf16[192,1152]{1,0:T(8,128)(2,1)S(1)}, bf16[192,1152]{1,0:T(8,128)(2,1)S(1)}, u32[]{:S(2)}, u32[]{:S(2)}) collective-permute-start(bf16[192,1152]{1,0:T(8,128)(2,1)S(1)} %constant_dynamic-slice_fusion.8), channel_id=1, source_target_pairs={{0,2},{2,0},{1,3},{3,1},{4,6},{6,4},{5,7},{7,5},{8,10},{10,8},{9,1... | collective-permute-start | bytes 1327112 | tf_op jit(solution)/shard_map/ppermute | solution.py:459
  311.1 35.8 %collective-permute-start.9 = (bf16[192,1152]{1,0:T(8,128)(2,1)S(1)}, bf16[192,1152]{1,0:T(8,128)(2,1)S(1)}, u32[]{:S(2)}, u32[]{:S(2)}) collective-permute-start(bf16[192,1152]{1,0:T(8,128)(2,1)S(1)} %constant_dynamic-slice_fusion.6), channel_id=1, source_target_pairs={{0,4},{4,0},{1,5},{5,1},{2,6},{6,2},{3,7},{7,3},{8,12},{12,8},{9,1... | collective-permute-start | bytes 1327112 | tf_op jit(solution)/shard_map/ppermute | solution.py:459
  345.4 7.1 %collective-permute-start.8 = (bf16[96,1152]{1,0:T(8,128)(2,1)S(1)}, bf16[96,1152]{1,0:T(8,128)(2,1)S(1)}, u32[]{:S(2)}, u32[]{:S(2)}) collective-permute-start(bf16[96,1152]{1,0:T(8,128)(2,1)S(1)} %constant_dynamic-slice_fusion.7), channel_id=1, source_target_pairs={{0,4},{4,0},{1,5},{5,1},{2,6},{6,2},{3,7},{7,3},{8,12},{12,8},{9,1... | collective-permute-start | bytes 663560 | tf_op jit(solution)/shard_map/ppermute | solution.py:459
  347.1 6.9 %collective-permute-start.10 = (bf16[96,1152]{1,0:T(8,128)(2,1)S(1)}, bf16[96,1152]{1,0:T(8,128)(2,1)S(1)}, u32[]{:S(2)}, u32[]{:S(2)}) collective-permute-start(bf16[96,1152]{1,0:T(8,128)(2,1)S(1)} %constant_dynamic-slice_fusion.5), channel_id=1, source_target_pairs={{0,2},{2,0},{1,3},{3,1},{4,6},{6,4},{5,7},{7,5},{8,10},{10,8},{9,1... | collective-permute-start | bytes 663560 | tf_op jit(solution)/shard_map/ppermute | solution.py:459
  354.0 11.0 %collective-permute-start.13 = (bf16[2,24,1152]{2,1,0:T(8,128)(2,1)S(1)}, bf16[2,24,1152]{2,1,0:T(8,128)(2,1)S(1)}, u32[]{:S(2)}, u32[]{:S(2)}) collective-permute-start(bf16[2,24,1152]{2,1,0:T(8,128)(2,1)S(1)} %get-tuple-element.68), channel_id=1, source_target_pairs={{0,24},{8,0},{16,8},{24,16},{1,25},{9,1},{17,9},{25,17},{2,26},{10... | collective-permute-start | bytes 331784 | tf_op jit(solution)/shard_map/ppermute | solution.py:459
  357.9 24.2 %collective-permute-start.12 = (bf16[2,24,1152]{2,1,0:T(8,128)(2,1)S(1)}, bf16[2,24,1152]{2,1,0:T(8,128)(2,1)S(1)}, u32[]{:S(2)}, u32[]{:S(2)}) collective-permute-start(bf16[2,24,1152]{2,1,0:T(8,128)(2,1)S(1)} %get-tuple-element.67), channel_id=1, source_target_pairs={{0,16},{8,24},{16,0},{24,8},{1,17},{9,25},{17,1},{25,9},{2,18},{10... | collective-permute-start | bytes 331784 | tf_op jit(solution)/shard_map/ppermute | solution.py:459
  357.9 24.2 %collective-permute-start.11 = (bf16[2,24,1152]{2,1,0:T(8,128)(2,1)S(1)}, bf16[2,24,1152]{2,1,0:T(8,128)(2,1)S(1)}, u32[]{:S(2)}, u32[]{:S(2)}) collective-permute-start(bf16[2,24,1152]{2,1,0:T(8,128)(2,1)S(1)} %get-tuple-element.66), channel_id=1, source_target_pairs={{0,8},{8,16},{16,24},{24,0},{1,9},{9,17},{17,25},{25,1},{2,10},{10... | collective-permute-start | bytes 331784 | tf_op jit(solution)/shard_map/ppermute | solution.py:459
  382.2 9.4 %collective-permute-start.14 = (bf16[2,24,1152]{2,1,0:T(8,128)(2,1)S(1)}, bf16[2,24,1152]{2,1,0:T(8,128)(2,1)S(1)}, u32[]{:S(2)}, u32[]{:S(2)}) collective-permute-start(bf16[2,24,1152]{2,1,0:T(8,128)(2,1)S(1)} %get-tuple-element.55), channel_id=1, source_target_pairs={{0,8},{8,16},{16,24},{24,0},{1,9},{9,17},{17,25},{25,1},{2,10},{10... | collective-permute-start | bytes 331784 | tf_op jit(solution)/shard_map/ppermute | solution.py:459
  382.3 41.4 %collective-permute-start.35 = (bf16[96,384]{1,0:T(8,128)(2,1)S(1)}, bf16[96,384]{1,0:T(8,128)(2,1)S(1)}, u32[]{:S(2)}, u32[]{:S(2)}) collective-permute-start(bf16[96,384]{1,0:T(8,128)(2,1)S(1)} %get-tuple-element.70), channel_id=1, source_target_pairs={{0,2},{2,0},{1,3},{3,1},{4,6},{6,4},{5,7},{7,5},{8,10},{10,8},{9,1... | collective-permute-start | bytes 221192 | tf_op jit(solution)/shard_map/ppermute | solution.py:459
  382.4 17.9 %collective-permute-start.15 = (bf16[2,24,1152]{2,1,0:T(8,128)(2,1)S(1)}, bf16[2,24,1152]{2,1,0:T(8,128)(2,1)S(1)}, u32[]{:S(2)}, u32[]{:S(2)}) collective-permute-start(bf16[2,24,1152]{2,1,0:T(8,128)(2,1)S(1)} %get-tuple-element.55), channel_id=1, source_target_pairs={{0,16},{8,24},{16,0},{24,8},{1,17},{9,25},{17,1},{25,9},{2,18},{10... | collective-permute-start | bytes 331784 | tf_op jit(solution)/shard_map/ppermute | solution.py:459
  391.5 10.3 %collective-permute-start.16 = (bf16[2,24,1152]{2,1,0:T(8,128)(2,1)S(1)}, bf16[2,24,1152]{2,1,0:T(8,128)(2,1)S(1)}, u32[]{:S(2)}, u32[]{:S(2)}) collective-permute-start(bf16[2,24,1152]{2,1,0:T(8,128)(2,1)S(1)} %get-tuple-element.55), channel_id=1, source_target_pairs={{0,24},{8,0},{16,8},{24,16},{1,25},{9,1},{17,9},{25,17},{2,26},{10... | collective-permute-start | bytes 331784 | tf_op jit(solution)/shard_map/ppermute | solution.py:459
  403.0 7.0 %collective-permute-start.17 = (bf16[96,1152]{1,0:T(8,128)(2,1)S(1)}, bf16[96,1152]{1,0:T(8,128)(2,1)S(1)}, u32[]{:S(2)}, u32[]{:S(2)}) collective-permute-start(bf16[96,1152]{1,0:T(8,128)(2,1)S(1)} %get-tuple-element.64), channel_id=1, source_target_pairs={{0,4},{4,0},{1,5},{5,1},{2,6},{6,2},{3,7},{7,3},{8,12},{12,8},{9,1... | collective-permute-start | bytes 663560 | tf_op jit(solution)/shard_map/ppermute | solution.py:459
  408.0 11.1 %collective-permute-start.20 = (bf16[192,1152]{1,0:T(8,128)(2,1)S(1)}, bf16[192,1152]{1,0:T(8,128)(2,1)S(1)}, u32[]{:S(2)}, u32[]{:S(2)}) collective-permute-start(bf16[192,1152]{1,0:T(8,128)(2,1)S(1)} %constant_dynamic-update-slice_fusion.18), channel_id=1, source_target_pairs={{0,4},{4,0},{1,5},{5,1},{2,6},{6,2},{3,7},{7,3},{8,12},{12,8},{9,1... | collective-permute-start | bytes 1327112 | tf_op jit(solution)/shard_map/ppermute | solution.py:459
  410.0 10.3 %collective-permute-start.18 = (bf16[192,1152]{1,0:T(8,128)(2,1)S(1)}, bf16[192,1152]{1,0:T(8,128)(2,1)S(1)}, u32[]{:S(2)}, u32[]{:S(2)}) collective-permute-start(bf16[192,1152]{1,0:T(8,128)(2,1)S(1)} %constant_dynamic-update-slice_fusion.22), channel_id=1, source_target_pairs={{0,2},{2,0},{1,3},{3,1},{4,6},{6,4},{5,7},{7,5},{8,10},{10,8},{9,1... | collective-permute-start | bytes 1327112 | tf_op jit(solution)/shard_map/ppermute | solution.py:459
  422.1 24.0 %collective-permute-start.21 = (bf16[768,1152]{1,0:T(8,128)(2,1)}, bf16[768,1152]{1,0:T(8,128)(2,1)}, u32[]{:S(2)}, u32[]{:S(2)}) collective-permute-start(bf16[768,1152]{1,0:T(8,128)(2,1)} %get-tuple-element.56), channel_id=1, source_target_pairs={{0,1},{1,0},{2,3},{3,2},{4,5},{5,4},{6,7},{7,6},{8,9},{9,8},{10,11... | collective-permute-start | bytes 5308424 | tf_op jit(solution)/shard_map/ppermute | solution.py:459
  430.0 12.3 %collective-permute-start.3 = (f32[2,768]{1,0:T(2,128)S(1)}, f32[2,768]{1,0:T(2,128)S(1)}, u32[]{:S(2)}, u32[]{:S(2)}) collective-permute-start(f32[2,768]{1,0:T(2,128)S(1)} %add.112), channel_id=1, source_target_pairs={{0,8},{8,16},{16,24},{24,0},{1,9},{9,17},{17,25},{25,1},{2,10},{10... | collective-permute-start | bytes 18440 | tf_op jit(solution)/shard_map/ppermute | solution.py:459
  434.5 8.5 %collective-permute-start.37 = (bf16[768,384]{1,0:T(8,128)(2,1)}, bf16[768,384]{1,0:T(8,128)(2,1)}, u32[]{:S(2)}, u32[]{:S(2)}) collective-permute-start(bf16[768,384]{1,0:T(8,128)(2,1)} %get-tuple-element.60), channel_id=1, source_target_pairs={{0,1},{1,0},{2,3},{3,2},{4,5},{5,4},{6,7},{7,6},{8,9},{9,8},{10,11... | collective-permute-start | bytes 1769480 | tf_op jit(solution)/shard_map/ppermute | solution.py:459
  (50 other events, 440.8 us)
Sparse Core Ops, SparseCore 0:
  170.9 87.5 reduce-scatter.2
  301.9 100.4 reduce-scatter.4

commit v2 on v1

v2 whole, which is shorter than its diff:
```python
import functools
import math

import jax
import jax.numpy as jnp
from jax import lax
from jax.experimental import pallas as pl
from jax.experimental.pallas import tpu as pltpu
from jax.sharding import Mesh, PartitionSpec as P

HEADS = 12
HEAD_DIM = 64
EPSILON = 1e-05
NEGATIVE = -1e30
SCALE = HEAD_DIM ** (-0.5)
BF = jnp.bfloat16
F32 = jnp.float32
PLANE = ("y", "x", "core")


def nn(a, b):
    return lax.dot_general(a, b, (((1,), (0,)), ((), ())), preferred_element_type=F32)


def nt(a, b):
    return lax.dot_general(a, b, (((1,), (1,)), ((), ())), preferred_element_type=F32)


def tn(a, b):
    return lax.dot_general(a, b, (((0,), (0,)), ((), ())), preferred_element_type=F32)


def iota(shape, dim):
    return lax.broadcasted_iota(jnp.int32, shape, dim)


def call(body, flops=0, moved=0, limit=60, **kw):
    return pl.pallas_call(
        body,
        compiler_params=pltpu.CompilerParams(vmem_limit_bytes=limit << 20),
        cost_estimate=pl.CostEstimate(
            flops=int(flops), bytes_accessed=int(moved), transcendentals=0
        ),
        **kw,
    )


def whole(shape):
    return pl.BlockSpec(shape, lambda *i: (0,) * len(shape))


def norm_parts(v):
    centred = v - jnp.mean(v, axis=-1, keepdims=True)
    rate = lax.rsqrt(jnp.mean(centred * centred, axis=-1, keepdims=True) + EPSILON)
    return centred * rate, rate


def norm_grad(x_hat, rate, u):
    return rate * (
        u
        - jnp.mean(u, axis=-1, keepdims=True)
        - x_hat * jnp.mean(u * x_hat, axis=-1, keepdims=True)
    )


def route_body(
    ids_ref, table_ref, cot_ref, row_ref, col_ref, first_ref, send_ref, *, sides, capacity
):
    high_side, low_side = sides
    count = ids_ref.shape[1]
    ids = ids_ref[...]
    table = table_ref[...].astype(BF)
    high = (iota((table.shape[0], count), 0) == (ids >> 7)).astype(BF)
    picked = tn(table, high)
    low = iota((128, count), 0) == (ids & 127)
    chosen = jnp.sum(jnp.where(low, picked, 0.0), axis=0, keepdims=True).astype(jnp.int32)
    bits = low_side.bit_length()
    here = [lax.axis_index(axis) for axis in PLANE]
    part_y = ((chosen >> bits) - here[0]) & (high_side - 1)
    part_x = ((chosen >> 1) - here[1]) & (low_side - 1)
    part_core = (chosen - here[2]) & 1
    relative = (part_y * low_side + part_x) * 2 + part_core
    slots = max(16, send_ref.shape[0])
    member = iota((slots, count), 0) == relative
    before = (iota((count, count), 0) < iota((count, count), 1)).astype(BF)
    earlier = nn(member.astype(BF), before)
    rank = jnp.sum(jnp.where(member, earlier, 0.0), axis=0, keepdims=True)
    target = relative.astype(F32) * capacity + rank
    row = target.astype(jnp.int32)
    row_ref[...] = row
    first = chosen.astype(F32) * capacity + rank
    turned = jnp.transpose(jnp.concatenate([target, first] * 4, 0))
    col_ref[...] = turned[:, :1].astype(jnp.int32)
    first_ref[...] = turned[:, 1:2].astype(jnp.int32)
    first = first.astype(jnp.int32)
    place([send_ref.at[part] for part in range(send_ref.shape[0])], first, cot_ref, capacity)


def place(send_refs, row, rows_ref, capacity):
    for part, send_ref in enumerate(send_refs):
        placer = (iota((capacity, row.shape[1]), 0) + part * capacity == row).astype(BF)
        send_ref[...] = nn(placer, rows_ref[...]).astype(BF)


def route(ids, table, cot, sides, capacity):
    count, width = cot.shape
    experts = 2 * sides[0] * sides[1]
    slots = experts * capacity
    return call(
        functools.partial(route_body, sides=sides, capacity=capacity),
        flops=2 * slots * count * width,
        moved=2 * (count + slots) * width,
        out_shape=[
            jax.ShapeDtypeStruct((1, count), jnp.int32),
            jax.ShapeDtypeStruct((count, 1), jnp.int32),
            jax.ShapeDtypeStruct((count, 1), jnp.int32),
            jax.ShapeDtypeStruct((experts, capacity, width), BF),
        ],
    )(ids, table, cot)


def packed_body(x_ref, gain_ref, w_ref, packed_ref, normed_ref):
    x_hat, _ = norm_parts(x_ref[...].astype(F32))
    normed = (x_hat * gain_ref[...]).astype(BF)
    packed_ref[...] = nn(normed, w_ref[...]).astype(BF)
    normed_ref[...] = normed


def make_packed(x, gain, w):
    count, width = x.shape
    wide = w.shape[1]
    block = 256
    return call(
        packed_body,
        flops=2 * count * width * wide,
        moved=2 * (count * (2 * width + wide) + width * wide),
        grid=(count // block,),
        in_specs=[
            pl.BlockSpec((block, width), lambda i: (i, 0)),
            whole(gain.shape),
            whole(w.shape),
        ],
        out_specs=[
            pl.BlockSpec((block, wide), lambda i: (i, 0)),
            pl.BlockSpec((block, width), lambda i: (i, 0)),
        ],
        out_shape=[
            jax.ShapeDtypeStruct((count, wide), BF),
            jax.ShapeDtypeStruct((count, width), BF),
        ],
    )(x, gain, w)


def attend_body(q_ref, k_ref, v_ref, o_ref, total_ref, *, block):
    length = q_ref.shape[0]
    lane = iota((1, 128), 1)
    v_turned = jnp.transpose(v_ref[...])
    allowed = iota((block, block), 0) <= iota((block, block), 1)
    for row in range(length // block):
        end = (row + 1) * block
        outs = []
        for head in range(2):
            q = jnp.where(lane // 64 == head, q_ref[row * block : end, :] * BF(SCALE), BF(0))
            s = nt(k_ref[:end, :], q)
            last = jnp.where(allowed, s[end - block :], NEGATIVE)
            s = jnp.concatenate([s[: end - block], last], 0) if row else last
            highest = jnp.max(s, 0, keepdims=True)
            p = jnp.exp(s - highest)
            summed = jnp.sum(p, 0, keepdims=True)
            out = nn(v_turned[head * 64 : (head + 1) * 64, :end], p.astype(BF))
            outs.append(out * (1.0 / summed))
            total_ref[0, head : head + 1, row * block : end] = highest + jnp.log(summed)
        o_ref[row * block : end, :] = jnp.transpose(jnp.concatenate(outs, 0)).astype(BF)


def attend(packed):
    length = packed.shape[0]
    pairs = packed.shape[1] // 384
    part = lambda o: pl.BlockSpec((length, 128), lambda i: (0, o * pairs + i))
    return call(
        functools.partial(attend_body, block=min(512, length)),
        flops=1.2e10,
        moved=2 * length * pairs * 512,
        grid=(pairs,),
        in_specs=[part(0), part(1), part(2)],
        out_specs=[part(0), pl.BlockSpec((1, 2, length), lambda i: (i, 0, 0))],
        out_shape=[
            jax.ShapeDtypeStruct((length, pairs * 128), BF),
            jax.ShapeDtypeStruct((pairs, 2, length), F32),
        ],
    )(packed, packed, packed)


def attend_back_body(
    q_ref, k_ref, v_ref, o_ref, up_ref, total_ref, out_ref, acc_ref, *, block
):
    length = q_ref.shape[0]
    count = length // block
    lane = iota((1, 128), 1)
    inner = jnp.transpose(o_ref[...].astype(F32) * up_ref[...].astype(F32))
    inner = [jnp.sum(inner[:64], 0, keepdims=True), jnp.sum(inner[64:], 0, keepdims=True)]
    allowed = iota((block, block), 0) <= iota((block, block), 1)
    for part in range(count):
        begin, end = part * block, (part + 1) * block
        k = k_ref[begin:end, :]
        v = v_ref[begin:end, :]
        dk, dv = [], []
        for head in range(2):
            mine = lane // 64 == head
            q = jnp.where(mine, q_ref[begin:, :] * BF(SCALE), BF(0))
            up = jnp.where(mine, up_ref[begin:, :], BF(0))
            s = nt(k, q) - total_ref[0, head : head + 1, begin:]
            first = jnp.where(allowed, s[:, :block], NEGATIVE)
            s = jnp.concatenate([first, s[:, block:]], 1) if part < count - 1 else first
            p = jnp.exp(s)
            ds = (p * (nt(v, up) - inner[head][:, begin:])).astype(BF)
            dv.append(nn(p.astype(BF), up))
            dk.append(nn(ds, q))
            dq = tn(ds, jnp.where(mine, k * BF(SCALE), BF(0)))
            if part == 0 and head == 0:
                acc_ref[...] = dq
            else:
                acc_ref[begin:, :] += dq
        out_ref[1, begin:end, :] = (dk[0] + dk[1]).astype(BF)
        out_ref[2, begin:end, :] = (dv[0] + dv[1]).astype(BF)
    out_ref[0] = acc_ref[...].astype(BF)


def attend_back(packed, attended, totals, upstream):
    length = packed.shape[0]
    pairs = packed.shape[1] // 384
    part = lambda o: pl.BlockSpec((length, 128), lambda i: (0, o * pairs + i))
    return call(
        functools.partial(attend_back_body, block=min(256, length)),
        flops=3e10,
        moved=2 * length * pairs * 1024,
        grid=(pairs,),
        in_specs=[
            part(0), part(1), part(2), part(0), part(0),
            pl.BlockSpec((1, 2, length), lambda i: (i, 0, 0)),
        ],
        out_specs=pl.BlockSpec((3, length, 128), lambda i: (0, 0, i)),
        out_shape=jax.ShapeDtypeStruct((3, length, pairs * 128), BF),
        scratch_shapes=[pltpu.VMEM((length, 128), F32)],
    )(packed, packed, packed, attended, upstream, totals)


def dispatch_body(att_ref, w_ref, x_ref, gain_ref, row_ref, res_ref, *rest):
    send_refs, normed_ref = rest[:-1], rest[-1]
    for begin in range(0, att_ref.shape[0], 256):
        rows = slice(begin, begin + 256)
        residual = x_ref[rows, :].astype(F32) + nn(att_ref[rows, :], w_ref[...])
        res_ref[rows, :] = residual
        x_hat, _ = norm_parts(residual)
        normed_ref[rows, :] = (x_hat * gain_ref[...]).astype(BF)
    place(send_refs, row_ref[...], normed_ref, send_refs[0].shape[0])


def dispatch(attended, w, x, gain, row, experts, capacity):
    count, width = x.shape
    slots = experts * capacity
    return call(
        dispatch_body,
        flops=2 * count * width * (slots + width),
        moved=2 * width * (5 * count + slots),
        out_shape=[jax.ShapeDtypeStruct((count, width), F32)]
        + [jax.ShapeDtypeStruct((capacity, width), BF)] * experts,
        scratch_shapes=[pltpu.VMEM((count, width), BF)],
    )(attended, w, x, gain, row)


def expert_body(from_ref, *refs, parts, kept):
    x_refs, g_refs = refs[:parts], refs[parts : 2 * parts]
    w_ref, out_w_ref = refs[2 * parts : 2 * parts + 2]
    act_ref, gh_ref, x_ref, g_ref, *back_refs = refs[2 * parts + 2 + kept : -1]
    acc_ref = refs[-1]
    step = pl.program_id(0)
    size = x_refs[0].shape[0]
    c1 = 2.0 * math.sqrt(2.0 / math.pi)
    c2 = c1 * 0.044715

    @pl.when(step == 0)
    def _():
        for part in range(parts):
            rows = slice(part * size, (part + 1) * size)
            x_ref[rows, :] = x_refs[part][...]
            g_ref[rows, :] = g_refs[part][0]

    h = nn(x_ref[...], w_ref[...])
    ga = nn(g_ref[...], out_w_ref[...])
    square = h * h
    half = jnp.tanh(h * (0.5 * c1 + (0.5 * c2) * square)) * 0.5 + 0.5
    act = h * half
    slope = half + (act * (1.0 - half)) * (c1 + (3.0 * c2) * square)
    act_ref[...] = act.astype(BF)
    gh = (ga * slope).astype(BF)
    gh_ref[...] = gh
    back = nt(gh, w_ref[...])

    @pl.when(step == 0)
    def _():
        acc_ref[...] = back

    @pl.when(step > 0)
    def _():
        acc_ref[...] += back

    @pl.when(step == pl.num_programs(0) - 1)
    def _():
        for part in range(parts):
            back_refs[part][...] = acc_ref[part * size : (part + 1) * size, :].astype(BF)


def expert(chips, place_at, total, source, xs, g, w, out_w, earlier):
    parts = len(xs)
    size, width = xs[0].shape
    units = w.shape[1]
    block = min(1024, units)
    tall = parts * size
    tile = pl.BlockSpec((tall, block), lambda i, s: (place_at, i))
    rows = pl.BlockSpec((tall, width), lambda i, s: (place_at, 0))
    weight = pl.BlockSpec((width, block), lambda i, s: (0, i))
    pick = lambda k: pl.BlockSpec((1, size, width), lambda i, s: (s[k], 0, 0))
    every = total * size
    return pl.pallas_call(
        functools.partial(expert_body, parts=parts, kept=len(earlier)),
        grid_spec=pltpu.PrefetchScalarGridSpec(
            num_scalar_prefetch=1,
            grid=(units // block,),
            in_specs=[whole((size, width))] * parts
            + [pick(2 * chip + core) for chip in chips for core in range(2)]
            + [weight, weight]
            + [pl.BlockSpec(memory_space=pl.ANY)] * len(earlier),
            out_specs=[tile, tile, rows, rows] + [whole((size, width))] * parts,
            scratch_shapes=[pltpu.VMEM((tall, width), F32)],
        ),
        out_shape=[jax.ShapeDtypeStruct((every, units), BF)] * 2
        + [jax.ShapeDtypeStruct((every, width), BF)] * 2
        + [jax.ShapeDtypeStruct((size, width), BF)] * parts,
        input_output_aliases={1 + 2 * parts + 2 + i: i for i in range(len(earlier))},
        compiler_params=pltpu.CompilerParams(vmem_limit_bytes=60 << 20),
        cost_estimate=pl.CostEstimate(
            flops=6 * tall * width * units,
            bytes_accessed=2 * (5 * tall * width + 2 * width * units + 2 * tall * units),
            transcendentals=0,
        ),
    )(source, *xs, *[g] * parts, w, out_w, *earlier)


def weight_share_body(g_ref, act_ref, out_ref):
    out_ref[...] = tn(g_ref[...], act_ref[...]).astype(BF)


def weight_share(g, act, shares, begin, size):
    rows, width = g.shape
    share = act.shape[1] // shares
    block = math.gcd(768, size)
    per = size // block
    pick = pl.BlockSpec(
        (pl.Element(rows), pl.Element(block)),
        lambda i: (0, pl.multiple_of(i // per * share + begin + i % per * block, 128)),
    )
    return call(
        weight_share_body,
        flops=2 * rows * width * shares * size,
        moved=2 * (rows * width + rows * shares * size + width * shares * size),
        grid=(shares * per,),
        in_specs=[whole(g.shape), pick],
        out_specs=pl.BlockSpec((width, block), lambda i: (0, i)),
        out_shape=jax.ShapeDtypeStruct((width, shares * size), BF),
    )(g, act)


def result_body(chip_ref, act_ref, w_ref, out_ref):
    size = out_ref.shape[1]
    out = nt(act_ref[...], w_ref[...]).astype(BF)
    same = lax.axis_index("core") == 0

    @pl.when(same)
    def _():
        out_ref[0] = out[:size]
        out_ref[1] = out[size:]

    @pl.when(jnp.logical_not(same))
    def _():
        out_ref[0] = out[size:]
        out_ref[1] = out[:size]


def make_result(chips, active, w, experts):
    rows, units = active.shape
    width = w.shape[0]
    size = rows // experts
    return pl.pallas_call(
        result_body,
        grid_spec=pltpu.PrefetchScalarGridSpec(
            num_scalar_prefetch=1,
            grid=(experts // 2,),
            in_specs=[
                pl.BlockSpec((2 * size, units), lambda i, s: (i, 0)),
                pl.BlockSpec(w.shape, lambda i, s: (0, 0)),
            ],
            out_specs=pl.BlockSpec((2, size, width), lambda i, s: (s[i], 0, 0)),
        ),
        out_shape=jax.ShapeDtypeStruct((experts, size, width), BF),
        compiler_params=pltpu.CompilerParams(vmem_limit_bytes=60 << 20),
        cost_estimate=pl.CostEstimate(
            flops=2 * rows * units * width,
            bytes_accessed=2 * (rows * units + units * width + rows * width),
            transcendentals=0,
        ),
    )(chips, active, w)


def unplace(back_refs, col, rows_ref):
    size = back_refs[0].shape[0]

    @pl.when(pl.program_id(0) == 0)
    def _():
        for part, back_ref in enumerate(back_refs):
            rows_ref[part * size : (part + 1) * size, :] = back_ref[...]

    placer = (iota((col.shape[0], rows_ref.shape[0]), 1) == col).astype(BF)
    return nn(placer, rows_ref[...])


def collect_back_body(col_ref, res_ref, cot_ref, gain_ref, w_ref, *rest):
    back_refs, (gres_ref, gattn_ref, gatt_ref, ggain_ref, rows_ref) = rest[:-5], rest[-5:]
    step = pl.program_id(0)
    grad = unplace(back_refs, col_ref[...], rows_ref)
    x_hat, rate = norm_parts(res_ref[...])
    gres = cot_ref[...].astype(F32) + norm_grad(x_hat, rate, grad * gain_ref[...])
    gres_ref[...] = gres
    gain_part = jnp.sum(grad * x_hat, axis=0, keepdims=True)
    gattn = gres.astype(BF)
    gattn_ref[...] = gattn
    gatt_ref[...] = nt(gattn, w_ref[...]).astype(BF)

    @pl.when(step == 0)
    def _():
        ggain_ref[...] = gain_part

    @pl.when(step > 0)
    def _():
        ggain_ref[...] += gain_part


def collect_back(backs, col, residual, cot, gain, w):
    count, width = cot.shape
    size = backs[0].shape[0]
    block = 256
    row = pl.BlockSpec((block, width), lambda i: (i, 0))
    return call(
        collect_back_body,
        flops=2 * count * width * (len(backs) * size + 2 * width),
        moved=2 * width * (len(backs) * size + 8 * count),
        grid=(count // block,),
        in_specs=[
            pl.BlockSpec((block, 1), lambda i: (i, 0)), row, row,
            whole(gain.shape), whole(w.shape),
        ]
        + [whole((size, width))] * len(backs),
        out_specs=[row, row, row, whole((1, width))],
        out_shape=[
            jax.ShapeDtypeStruct((count, width), F32),
            jax.ShapeDtypeStruct((count, width), BF),
            jax.ShapeDtypeStruct((count, width), BF),
            jax.ShapeDtypeStruct((1, width), F32),
        ],
        scratch_shapes=[pltpu.VMEM((len(backs) * size, width), BF)],
    )(col, residual, cot, gain, w, *backs)


def collect_body(col_ref, res_ref, back_ref, out_ref):
    placer = (iota((col_ref.shape[0], back_ref.shape[0]), 1) == col_ref[...]).astype(BF)
    out_ref[...] = (res_ref[...] + nn(placer, back_ref[...])).astype(BF)


def collect(back, col, residual):
    count, width = residual.shape
    block = 256
    row = pl.BlockSpec((block, width), lambda i: (i, 0))
    return call(
        collect_body,
        flops=2 * count * width * back.shape[0],
        moved=2 * width * (back.shape[0] + 3 * count),
        grid=(count // block,),
        in_specs=[pl.BlockSpec((block, 1), lambda i: (i, 0)), row, whole(back.shape)],
        out_specs=row,
        out_shape=jax.ShapeDtypeStruct((count, width), BF),
    )(col, residual, back)


def weight_grad_body(normed_ref, g_ref, att_ref, gattn_ref, keep_ref, send_ref):
    step = pl.program_id(0)
    width = g_ref.shape[2]
    last = step == pl.num_programs(0) - 1
    rows = jnp.where(last, gattn_ref[...], g_ref[0])
    left = jnp.where(last, att_ref[...], normed_ref[...])
    out = tn(left, rows).astype(BF)
    mine = step // 2 == lax.axis_index("core")
    for half in range(2):
        columns = slice(half * width, (half + 1) * width)

        @pl.when((step % 2 == half) & mine)
        def _():
            keep_ref[:, columns] = out

        @pl.when((step % 2 == half) & jnp.logical_not(mine))
        def _():
            send_ref[:, columns] = out


def weight_grads(normed, g, attended, gattn):
    count, width = normed.shape
    out = jax.ShapeDtypeStruct((width, 2 * width), BF)
    return call(
        weight_grad_body,
        flops=8 * width * count * width,
        moved=2 * (6 * width * count + 4 * width * width),
        grid=(4,),
        in_specs=[
            whole(normed.shape),
            pl.BlockSpec((1, count, width), lambda i: (jnp.minimum(i, 2), 0, 0)),
            whole(attended.shape),
            whole(gattn.shape),
        ],
        out_specs=[whole(out.shape)] * 2,
        out_shape=[out] * 2,
    )(normed, g, attended, gattn)


def grad_in_body(x_ref, gain_ref, w_ref, g_ref, gres_ref, out_ref, ggain_ref):
    step = pl.program_id(0)
    width = x_ref.shape[1]
    x_hat, rate = norm_parts(x_ref[...].astype(F32))
    grad = nt(g_ref[0], w_ref[:, :width])
    grad += nt(g_ref[1], w_ref[:, width : 2 * width])
    grad += nt(g_ref[2], w_ref[:, 2 * width :])
    out_ref[...] = gres_ref[...] + norm_grad(x_hat, rate, grad * gain_ref[...])
    part = jnp.sum(grad * x_hat, axis=0, keepdims=True)

    @pl.when(step == 0)
    def _():
        ggain_ref[...] = part

    @pl.when(step > 0)
    def _():
        ggain_ref[...] += part


def grad_in(x, gain, w, g, gres):
    count, width = x.shape
    block = 256
    row = pl.BlockSpec((block, width), lambda i: (i, 0))
    return call(
        grad_in_body,
        flops=6 * count * width * width,
        moved=2 * width * 9 * count,
        grid=(count // block,),
        in_specs=[
            row, whole(gain.shape), whole(w.shape),
            pl.BlockSpec((3, block, width), lambda i: (0, i, 0)), row,
        ],
        out_specs=[row, whole((1, width))],
        out_shape=[
            jax.ShapeDtypeStruct((count, width), F32),
            jax.ShapeDtypeStruct((1, width), F32),
        ],
    )(x, gain, w, g, gres)


def shift(a, axis, k):
    n = lax.axis_size(axis)
    return lax.ppermute(a, axis, [(i, (i + k) % n) for i in range(n)])


def groups(chips):
    sizes = [1]
    while sum(sizes) < chips:
        sizes.append((chips - sum(sizes) + 1) // 2)
    out, begin, at = [], 0, chips
    tall = sorted(sizes, reverse=True)
    for i, size in enumerate(sizes):
        rank = tall.index(size) + sizes[:i].count(size)
        out.append((tuple(range(begin, begin + size)), sum(tall[:rank]) // size))
        begin += size
    return out


def source_parts(sides):
    high, low = sides
    y, x, core = (lax.axis_index(axis) for axis in PLANE)
    out = []
    for dy in range(high):
        for dx in range(low):
            for dc in range(2):
                chip = lax.rem(y + high - dy, high) * low + lax.rem(x + low - dx, low)
                out.append(chip * 2 + lax.rem(core + dc, 2))
    return jnp.stack(out).astype(jnp.int32)


def plane_shift(a, part, sign, sides):
    if part == 0:
        return a
    high, low = sides
    dy, dx, dc = sign * (part // (2 * low)), sign * (part // 2 % low), part % 2
    pairs = []
    for y in range(high):
        for x in range(low):
            for core in range(2):
                to = ((y + dy) % high * low + (x + dx) % low) * 2 + (core + dc) % 2
                pairs.append(((y * low + x) * 2 + core, to))
    return lax.ppermute(a, PLANE, pairs)


def cut(a, index, pieces, dim):
    size = a.shape[dim] // pieces
    return lax.dynamic_slice_in_dim(a, index * size, size, dim)


def scatter_sum(a, axis, dim):
    n = lax.axis_size(axis)
    me = lax.axis_index(axis)
    total = cut(a, me, n, dim).astype(F32)
    for k in range(1, n):
        total += shift(cut(a, lax.rem(me + k, n), n, dim), axis, k).astype(F32)
    return total.astype(a.dtype)


def gather_all(a, axis, dim):
    n = lax.axis_size(axis)
    me = lax.axis_index(axis)
    size = a.shape[dim]
    shape = a.shape[:dim] + (n * size,) + a.shape[dim + 1 :]
    out = lax.dynamic_update_slice_in_dim(jnp.zeros(shape, a.dtype), a, me * size, dim)
    for k in range(1, n):
        got = shift(a, axis, k)
        out = lax.dynamic_update_slice_in_dim(out, got, lax.rem(me - k + n, n) * size, dim)
    return out


def after(value, *first):
    return lax.optimization_barrier((value, first))[0]


def split_body(keep_ref, got_ref, one_ref, two_ref, *out_refs, ways):
    wide = keep_ref.shape[1]
    half = keep_ref.shape[0] // 2
    turned = jnp.transpose(
        jnp.concatenate([one_ref[...], two_ref[...]] + [jnp.zeros_like(one_ref[...])] * 6, 0)
    )
    turned = jnp.concatenate([turned, jnp.zeros((turned.shape[0], 120), F32)], 1)
    at = 0
    for begin, axis, count in ((0, "x", ways[1]), (half, "y", ways[0])):
        size = half // count
        me = lax.axis_index(axis)
        for k in range(count):
            piece = lax.rem(me + k, count)
            rows = pl.ds(pl.multiple_of(begin + piece * size, 8), size)
            out = out_refs[at]
            out[:, :wide] = (keep_ref[rows, :].astype(F32) + got_ref[rows, :].astype(F32)).astype(BF)
            for other in range(count):

                @pl.when(piece == other)
                def _():
                    begin_here = begin + other * size
                    out[:, wide:] = turned[begin_here : begin_here + size].astype(BF)

            at += 1


def split(keep, got, one, two, ways):
    rows, wide = keep.shape
    sizes = [rows // 2 // ways[1]] * ways[1] + [rows // 2 // ways[0]] * ways[0]
    outs = call(
        functools.partial(split_body, ways=ways),
        moved=6 * rows * wide,
        out_shape=[jax.ShapeDtypeStruct((size, wide + 128), BF) for size in sizes],
    )(keep, got, one, two)
    return outs[: ways[1]], outs[ways[1] :]


def add_up(parts, axis):
    return [parts[0]] + [shift(a, axis, k) for k, a in enumerate(parts) if k]


def total(parts):
    out = parts[0].astype(F32)
    for a in parts[1:]:
        out += a.astype(F32)
    return out.astype(parts[0].dtype)


def sum_planes(top, low, first):
    top = scatter_sum(total(top), "y", 0)
    low = scatter_sum(total(low), "x", 0)
    both = scatter_sum(jnp.stack([top, low]), "dp", 1)
    both = after(both, first)
    return gather_all(both, "dp", 1), both


def gather_planes(both, during_last):
    top = gather_all(both[0], "y", 0)
    low = gather_all(both[1], "x", 0)
    top, low = after((top, low), *during_last)
    top = gather_all(top, "x", 0)
    low = gather_all(low, "y", 0)
    mine = jnp.concatenate([top, low], 0)
    return mine, shift(mine, "core", 1)


def unpack_body(mine_ref, other_ref, qkv_ref, proj_ref, one_ref, two_ref):
    width = proj_ref.shape[1]
    first = lax.axis_index("core") == 0
    gains = mine_ref[:, 2 * width :].astype(F32) + other_ref[:, 2 * width :].astype(F32)
    gains = jnp.transpose(gains)
    one_ref[...] = gains[:1]
    two_ref[...] = gains[1:2]

    @pl.when(first)
    def _():
        qkv_ref[:, : 2 * width] = mine_ref[:, : 2 * width].astype(F32)
        qkv_ref[:, 2 * width :] = other_ref[:, :width].astype(F32)
        proj_ref[...] = other_ref[:, width : 2 * width].astype(F32)

    @pl.when(jnp.logical_not(first))
    def _():
        qkv_ref[:, : 2 * width] = other_ref[:, : 2 * width].astype(F32)
        qkv_ref[:, 2 * width :] = mine_ref[:, :width].astype(F32)
        proj_ref[...] = mine_ref[:, width : 2 * width].astype(F32)


def unpack(mine, other):
    width = mine.shape[0]
    block = min(256, width)
    row = lambda wide: pl.BlockSpec((block, wide), lambda i: (i, 0))
    return call(
        unpack_body,
        moved=24 * width * width,
        grid=(width // block,),
        in_specs=[row(mine.shape[1])] * 2,
        out_specs=[row(3 * width), row(width)] + [pl.BlockSpec((1, block), lambda i: (0, i))] * 2,
        out_shape=[
            jax.ShapeDtypeStruct((width, 3 * width), F32),
            jax.ShapeDtypeStruct((width, width), F32),
            jax.ShapeDtypeStruct((1, width), F32),
            jax.ShapeDtypeStruct((1, width), F32),
        ],
    )(mine, other)


def widen_body(*refs):
    at = 0
    for ref in refs[:-1]:
        refs[-1][:, :, at : at + ref.shape[2]] = ref[...].astype(F32)
        at += ref.shape[2]


def widen(*parts):
    rows = parts[0].shape[1]
    wide = sum(a.shape[2] for a in parts)
    block = lambda columns: pl.BlockSpec((1, rows // 2, columns), lambda i: (0, i, 0))
    return call(
        widen_body,
        moved=6 * rows * wide,
        grid=(2,),
        in_specs=[block(a.shape[2]) for a in parts],
        out_specs=block(wide),
        out_shape=jax.ShapeDtypeStruct((1, rows, wide), F32),
    )(*parts)


def local(tokens, token_ids, hash_table, gain_one, w_qkv, w_proj, gain_two, w_in, w_out, cotangent):
    width = tokens.shape[-1]
    x = tokens.reshape(-1, width)
    cot = cotangent.reshape(-1, width)
    count = x.shape[0]
    sides = (lax.axis_size("y"), lax.axis_size("x"))
    experts = lax.axis_size(PLANE)
    capacity = 2 * count // experts
    first_gain = gain_one.reshape(1, width)
    second_gain = gain_two.reshape(1, width)
    inner, outer = w_in[0], w_out[0]

    def exchange_all(a):
        return lax.all_to_all(a, PLANE, split_axis=0, concat_axis=0, tiled=True)

    def exchange(parts, sign):
        return {i: plane_shift(a, i, sign, sides) for i, a in parts.items()}

    row, col, first_col, grad_send = route(
        token_ids.reshape(1, count), hash_table.reshape(-1, 128), cot, sides, capacity
    )
    flat_grad = exchange_all(grad_send)
    packed, normed = make_packed(x, first_gain, w_qkv)
    attended, totals = attend(packed)
    residual, *outgoing = dispatch(attended, w_proj, x, second_gain, row, experts, capacity)
    outgoing = dict(enumerate(outgoing))
    far = {i: outgoing.pop(i) for i in range(experts - 2, experts)}
    arrived = exchange(outgoing, 1)
    source = source_parts(sides)
    kept, backs = (), {}
    plan = groups(experts // 2)
    for chips, place_at in plan:
        parts = [2 * chip + core for chip in chips for core in range(2)]
        flat = after(flat_grad, *[backs[i] for i in sorted(backs) if i < 2 and len(parts) < 4])
        out = expert(
            chips, place_at, experts, source, [arrived[i] for i in parts], flat,
            inner, outer, kept,
        )
        kept = out[:4]
        backs.update(exchange(dict(zip(parts, out[4:])), -1))
        if chips == (0,):
            near = [arrived[i] for i in range(2, experts - 2)]
            arrived.update(exchange(after(far, near, kept[0]), 1))
    active, grad_hidden, rows_in, rows_grad = kept
    shares = lax.axis_size("dp")
    share = inner.shape[1] // shares
    near_backs = [backs[i] for i in range(experts - 2)]
    grad_back = near_backs + [backs[i] for i in range(experts - 2, experts)]
    def scatter(a):
        return lax.psum_scatter(a[None], "dp", scatter_dimension=2, tiled=True)

    grad_outer = weight_share(after(rows_grad, *near_backs), active, shares, 0, share)
    grad_w_out = widen(scatter(grad_outer))
    part = share * 2 // 3 // 256 * 256
    grad_inner = weight_share(after(rows_in, grad_outer), grad_hidden, shares, 0, part)
    grad_w_in = [scatter(grad_inner)]
    tall_first = sorted((chips for chips, _ in plan), key=lambda chips: (-len(chips), chips))
    order = [chip for chips in tall_first for chip in chips]
    chips = jnp.stack([source[2 * chip] // 2 for chip in order])
    results = make_result(chips, after(active, grad_inner), outer, experts)
    returned = exchange_all(results)

    grad_residual, grad_attn, grad_attended, grad_gain_two = collect_back(
        after(grad_back, results), col, residual, cot, second_gain, w_proj
    )
    grad_packed = attend_back(packed, attended, totals, grad_attended)
    returned, grad_packed = after((returned, grad_packed), grad_packed)
    keep, send = weight_grads(normed, grad_packed, attended, grad_attn)
    got = shift(send, "core", 1)
    grad_tokens, grad_gain_one = grad_in(
        x, first_gain, w_qkv, after(grad_packed, keep, grad_w_out), grad_residual
    )
    top, low = split(keep, after(got, grad_tokens), grad_gain_one, grad_gain_two, sides)
    grad_later = weight_share(
        after(rows_in, top, low), grad_hidden, shares, part, share - part
    )
    outputs = collect(after(returned.reshape(-1, width), grad_later), first_col, residual)
    top, low = after((add_up(top, "x"), add_up(low, "y")), outputs)
    both, summed = sum_planes(top, low, grad_w_in[0])
    grad_w_in.append(scatter(after(grad_later, summed)))
    grad_qkv, grad_proj, one, two = unpack(*gather_planes(both, ()))
    grad_w_in = widen(grad_w_in[0], after(grad_w_in[1], grad_qkv))
    return (
        outputs.reshape(tokens.shape),
        grad_tokens.reshape(tokens.shape),
        one.reshape(width),
        grad_qkv,
        grad_proj,
        two.reshape(width),
        grad_w_in,
        grad_w_out,
    )


def solution(mesh):
    dp, experts = mesh.devices.shape
    side = math.isqrt(experts // 2)
    parts = Mesh(mesh.devices.reshape(dp, side, experts // 2 // side, 2), ("dp", "y", "x", "core"))
    rows = ("dp",) + PLANE
    in_specs = (
        P(rows, None, None),
        P(rows, None),
        P(),
        P(),
        P(),
        P(),
        P(),
        P(PLANE, None, None),
        P(PLANE, None, None),
        P(rows, None, None),
    )
    out_specs = (
        P(rows, None, None),
        P(rows, None, None),
        P(),
        P(),
        P(),
        P(),
        P(PLANE, None, "dp"),
        P(PLANE, None, "dp"),
    )
    return jax.shard_map(local, mesh=parts, in_specs=in_specs, out_specs=out_specs, check_vma=False)
```

time: 471 us -> 380 us (0.81)
  Pallas kernels: 126 us -> 235 us
  waiting for transfers between devices: 157 us -> 73.4 us
  matrix products: 58 us -> 0 us
  local copies, waits for them, and re-layouts: 32.8 us -> 6.67 us
  starting transfers between devices: 57.9 us -> 41.8 us
  other arithmetic: 16.8 us -> 4.02 us
    pallas_call x6 -> x14, Pallas kernels: 58.4 us -> 154 us  [the longest x3 53.7 us: expert(): pl.pallas_call(functools.partial(expert_body, parts=parts, kept=len(earli...]
    dot_general x4 -> x0, matrix products: 58 us -> none  [the longest x2 26.8 us: nt(): lax.dot_general(a, b, (((1,), (1,)), ((), ())), preferred_element_type=F32)]
    ppermute x38 -> x16, waiting for transfers between devices: 108 us -> 59.2 us  [shift(): return lax.ppermute(a, axis, [(i, (i + k) % n) for i in range(n)])]
    all_to_all x4 -> x2, waiting for transfers between devices: 48 us -> 0.01 us  [exchange_all(): return lax.all_to_all(a, PLANE, split_axis=0, concat_axis=0, tiled=True)]
    ppermute x38 -> x16, starting transfers between devices: 40.9 us -> 18.9 us  [shift(): return lax.ppermute(a, axis, [(i, (i + k) % n) for i in range(n)])]
    unnamed x76 -> x34, local copies, waits for them, and re-layouts: 25.8 us -> 3.86 us
    ppermute x0 -> x14, starting transfers between devices: none -> 13.4 us  [plane_shift(): return lax.ppermute(a, PLANE, pairs)]
    convert_element_type x4 -> x2, other arithmetic: 10.7 us -> 0.3 us  [total(): return out.astype(parts[0].dtype)]
  transfers between devices with their start and end apart: 44 -> 35, of which waited for: 23 -> 15; matrix products, arithmetic and copies ran while one was open for 14% -> 2% of each run, Pallas kernels for 19% -> 56%
where the time goes in v2:
time: 380 us; the launch traced here: 375 us
  Pallas kernels  235 us (62%)
  waiting for transfers between devices  73.4 us (19%)
  starting transfers between devices  41.8 us (11%)
  between operations  14.4 us (4%)
  local copies, waits for them, and re-layouts  6.67 us (2%)
  other arithmetic  4.02 us (1%)
    ppermute x16, waiting for transfers between devices, shift(): return lax.ppermute(a, axis, [(i, (i + k) % n) for i in range(n)])  59.2 us
    pallas_call x3, Pallas kernels, expert(): pl.pallas_call(functools.partial(expert_body, parts=parts, kept=len(earli...  53.7 us
    pallas_call x3, Pallas kernels, weight_share(): call(weight_share_body, flops=2 * rows * width * shares * size, moved=2 *...  35.5 us
    pallas_call x1, Pallas kernels, attend_back(): call(functools.partial(attend_back_body, block=min(256, length)), flops=3...  29.1 us
    ppermute x16, starting transfers between devices, shift(): return lax.ppermute(a, axis, [(i, (i + k) % n) for i in range(n)])  18.9 us
    pallas_call x1, Pallas kernels, attend(): call(functools.partial(attend_body, block=min(512, length)), flops=120000...  17.2 us
    pallas_call x1, Pallas kernels, make_result(): pl.pallas_call(result_body, grid_spec=pltpu.PrefetchScalarGridSpec(num_sc...  15.9 us
    ppermute x14, starting transfers between devices, plane_shift(): return lax.ppermute(a, PLANE, pairs)  13.4 us
  transfers between devices with their start and end apart: 35, of which 15 were waited for; matrix products, arithmetic and copies ran while one was open for 2% of the time, Pallas kernels for 56%

profile of v2, /device:TPU:0, one launch (start us, length us, event | category | flops | bytes accessed | tf_op | source)
XLA Modules:
  0.0 375.4 jit_solution(17130317026585646221)
XLA Ops:
  7.2 7.2 %shard_map.161 = (s32[1,1024]{1,0:T(1,128)}, s32[1024,1]{1,0:T(8,128)}, s32[1024,1]{1,0:T(8,128)}, bf16[8,256,768]{2,1,0:T(8,128)(2,1)}) custom-call(s32[1,1024]{1,0:T(1,128)} %ids_ref.1, s32[64,128]{1,0:T(8,128)} %bitcast.51, bf16[1024,768]{1,0:T(8,128)(2,1)} %bitcast.46), custom_call_target="tpu_custom_call" | custom-call | flops 3221225472 | bytes 4718592 | tf_op jit(solution)/shard_map/pallas_call | solution.py:109
  14.3 5.3 %all-to-all-start = ((bf16[8,256,768]{2,1,0:T(8,128)(2,1)}), bf16[8,256,768]{2,1,0:T(8,128)(2,1)S(1)}, u32[]{:S(2)}, u32[]{:S(2)}) async-start(bf16[8,256,768]{2,1,0:T(8,128)(2,1)} %get-tuple-element.103), calls=%async_computation | async-start | bytes 6291456 | tf_op jit(solution)/shard_map/all_to_all | solution.py:787
  21.1 8.4 %shard_map.162 = (bf16[1024,2304]{1,0:T(8,128)(2,1)}, bf16[1024,768]{1,0:T(8,128)(2,1)}) custom-call(bf16[1024,768]{1,0:T(8,128)(2,1)} %bitcast.48, f32[1,768]{1,0:T(1,128)} %reshape.49.gain_ref, bf16[768,2304]{1,0:T(8,128)(2,1)} %w_ref.7), custom_call_target="tpu_custom_call" | custom-call | flops 3623878656 | bytes 11403264 | tf_op jit(solution)/shard_map/pallas_call | solution.py:133
  29.5 17.2 %shard_map.163 = (bf16[1024,768]{1,0:T(8,128)(2,1)}, f32[6,2,1024]{2,1,0:T(2,128)}) custom-call(bf16[1024,2304]{1,0:T(8,128)(2,1)} %get-tuple-element.91.q_ref.k_ref.v_ref, bf16[1024,2304]{1,0:T(8,128)(2,1)} %get-tuple-element.91.q_ref.k_ref.v_ref, bf16[1024,2304]{1,0:T(8,128)(2,1)} %get-tuple-element.91.q_ref.k_ref.v_ref), custom_call_target="tpu_custom_call" | custom-call | flops 12000000000 | bytes 6291456 | tf_op jit(solution)/shard_map/pallas_call | solution.py:180
  46.6 8.4 %shard_map.164 = (f32[1024,768]{1,0:T(8,128)}, bf16[256,768]{1,0:T(8,128)(2,1)}, bf16[256,768]{1,0:T(8,128)(2,1)}, bf16[256,768]{1,0:T(8,128)(2,1)}, bf16[256,76...) custom-call(bf16[1024,768]{1,0:T(8,128)(2,1)} %get-tuple-element.92., ...), custom_call_target="tpu_custom_call" | custom-call | flops 4429185024 | bytes 11010048 | tf_op jit(solution)/shard_map/pallas_call | solution.py:262
  61.3 14.4 %shard_map.165 = (bf16[2048,3072]{1,0:T(8,128)(2,1)}, bf16[2048,3072]{1,0:T(8,128)(2,1)}, bf16[2048,768]{1,0:T(8,128)(2,1)}, bf16[2048,768]{1,0:T(8,128)(2,1)}, ...) custom-call(s32[8]{0:T(128)} %stack.64.from_ref, bf16[256,768]{1,0:T(8,128)(2,1)} %get-tuple-element.101.refs_0_, ...), custom_call_target="tpu_custom_call" | custom-call | flops 7247757312 | bytes 19660800 | tf_op jit(solution)/shard_map/pallas_call | solution.py:325
  80.0 24.9 %shard_map.166 = (bf16[2048,3072]{1,0:T(8,128)(2,1)}, bf16[2048,3072]{1,0:T(8,128)(2,1)}, bf16[2048,768]{1,0:T(8,128)(2,1)}, bf16[2048,768]{1,0:T(8,128)(2,1)}, ...) custom-call(s32[8]{0:T(128)} %stack.64.from_ref, ...), custom_call_target="tpu_custom_call", output_to_operand_aliasing={{0}: (11, {}), {1}: (12, {}), {2}: (13, {}), {3}: (14, {})} | custom-call | flops 14495514624 | bytes 29884416 | tf_op jit(solution)/shard_map/pallas_call | solution.py:325
  109.3 14.4 %shard_map.167 = (bf16[2048,3072]{1,0:T(8,128)(2,1)}, bf16[2048,3072]{1,0:T(8,128)(2,1)}, bf16[2048,768]{1,0:T(8,128)(2,1)}, bf16[2048,768]{1,0:T(8,128)(2,1)}, ...) custom-call(s32[8]{0:T(128)} %stack.64.from_ref, ...), custom_call_target="tpu_custom_call", output_to_operand_aliasing={{0}: (7, {}), {1}: (8, {}), {2}: (9, {}), {3}: (10, {})} | custom-call | flops 7247757312 | bytes 19660800 | tf_op jit(solution)/shard_map/pallas_call | solution.py:325
  126.4 14.8 %shard_map.168 = bf16[768,3072]{1,0:T(8,128)(2,1)} custom-call(bf16[2048,768]{1,0:T(8,128)(2,1)} %get-tuple-element.124.g_ref, bf16[2048,3072]{1,0:T(8,128)(2,1)} %get-tuple-element.127.act_ref), custom_call_target="tpu_custom_call" | custom-call | flops 9663676416 | bytes 20447232 | tf_op jit(solution)/shard_map/pallas_call | solution.py:363
  141.9 13.0 %shard_map.169 = bf16[768,2048]{1,0:T(8,128)(2,1)} custom-call(bf16[2048,768]{1,0:T(8,128)(2,1)} %get-tuple-element.157.g_ref, bf16[2048,3072]{1,0:T(8,128)(2,1)} %get-tuple-element.126.act_ref), custom_call_target="tpu_custom_call" | custom-call | flops 6442450944 | bytes 14680064 | tf_op jit(solution)/shard_map/pallas_call | solution.py:363
  154.9 2.8 collective-permute-start.12
  157.8 15.9 %shard_map.170 = bf16[8,256,768]{2,1,0:T(8,128)(2,1)} custom-call(s32[4]{0:T(128)} %pad_add_fusion.chip_ref, bf16[2048,3072]{1,0:T(8,128)(2,1)} %get-tuple-element.127.act_ref, bf16[768,3072]{1,0:T(8,128)(2,1)} %bitcast.41), custom_call_target="tpu_custom_call" | custom-call | flops 9663676416 | bytes 20447232 | tf_op jit(solution)/shard_map/pallas_call | solution.py:394
  173.6 3.9 %all-to-all-start.1 = ((bf16[8,256,768]{2,1,0:T(8,128)(2,1)}), bf16[8,256,768]{2,1,0:T(8,128)(2,1)S(1)}, u32[]{:S(2)}, u32[]{:S(2)}) async-start(bf16[8,256,768]{2,1,0:T(8,128)(2,1)} %shard_map.170), calls=%async_computation.1 | async-start | bytes 6291456 | tf_op jit(solution)/shard_map/all_to_all | solution.py:787
  178.3 13.1 %shard_map.171 = (f32[1024,768]{1,0:T(8,128)}, bf16[1024,768]{1,0:T(8,128)(2,1)}, bf16[1024,768]{1,0:T(8,128)(2,1)}, f32[1,768]{1,0:T(1,128)}) custom-call(s32[1024,1]{1,0:T(8,128)} %get-tuple-element.128.col_ref, f32[1024,768]{1,0:T(8,128)} %get-tuple-element.94.res_ref, bf16[1024,768]{1,0:T(8,128)(2,1)} %bitcast.47, f32[1,768]{1,0:T(1,128)} %reshape.50.gain_ref, ...), custom_call_target="tpu_custom_call" | custom-call | flops 5637144576 | bytes 15728640 | tf_op jit(solution)/shard_map/pallas_call | solution.py:453
  191.4 29.1 %shard_map.172.g_ref = bf16[3,1024,768]{2,1,0:T(8,128)(2,1)} custom-call(bf16[1024,2304]{1,0:T(8,128)(2,1)} %get-tuple-element.91.q_ref.k_ref.v_ref, bf16[1024,2304]{1,0:T(8,128)(2,1)} %get-tuple-element.91.q_ref.k_ref.v_ref, bf16[1024,2304]{1,0:T(8,128)(2,1)} %get-tuple-element.91.q_ref.k_ref.v_ref, bf16[1024,768]{1,0:T(8,128)(2,1)} %get-tuple-element.92.att_ref.o_ref, ...), custom_call_target="tpu_custom_call" | custom-call | flops 30000001024 | bytes 12582912 | tf_op jit(solution)/shard_map/pallas_call | solution.py:233
  220.5 12.6 %shard_map.173 = (bf16[768,1536]{1,0:T(8,128)(2,1)}, bf16[768,1536]{1,0:T(8,128)(2,1)}) custom-call(bf16[1024,768]{1,0:T(8,128)(2,1)} %get-tuple-element.142.normed_ref, bf16[3,1024,768]{2,1,0:T(8,128)(2,1)} %shard_map.172.g_ref, bf16[1024,768]{1,0:T(8,128)(2,1)} %get-tuple-element.92.att_ref.o_ref, bf16[1024,768]{1,0:T(8,128)(2,1)} %get-tuple-element.144.gattn_ref), custom_call_target="tpu_custom_call" | custom-call | flops 4831838208 | bytes 14155776 | tf_op jit(solution)/shard_map/pallas_call | solution.py:517
  236.1 10.3 %shard_map.175 = (f32[1024,768]{1,0:T(8,128)}, f32[1,768]{1,0:T(1,128)}) custom-call(bf16[1024,768]{1,0:T(8,128)(2,1)} %bitcast.50, f32[1,768]{1,0:T(1,128)} %reshape.49.gain_ref, bf16[768,2304]{1,0:T(8,128)(2,1)} %w_ref.7, bf16[3,1024,768]{2,1,0:T(8,128)(2,1)} %shard_map.172.g_ref, f32[1024,768]{1,0:T(8,128)} %get-tuple-element.148.gres_ref), custom_call_target="tpu_custom_call" | custom-call | flops 3623878656 | bytes 14155776 | tf_op jit(solution)/shard_map/pallas_call | solution.py:556
  247.9 4.7 %shard_map.176 = (bf16[192,1664]{1,0:T(8,128)(2,1)}, bf16[192,1664]{1,0:T(8,128)(2,1)}, bf16[192,1664]{1,0:T(8,128)(2,1)}, bf16[192,1664]{1,0:T(8,128)(2,1)}) custom-call(bf16[768,1536]{1,0:T(8,128)(2,1)} %get-tuple-element.145.keep_ref, bf16[768,1536]{1,0:T(8,128)(2,1)} %copy-done.3, f32[1,768]{1,0:T(1,128)} %get-tuple-element.151.one_ref, ...), custom_call_target="tpu_custom_call" | custom-call | bytes 7077888 | tf_op jit(solution)/shard_map/pallas_call | solution.py:676
  255.8 7.8 %shard_map.177 = bf16[768,1024]{1,0:T(8,128)(2,1)} custom-call(bf16[2048,768]{1,0:T(8,128)(2,1)} %get-tuple-element.157.g_ref, bf16[2048,3072]{1,0:T(8,128)(2,1)} %get-tuple-element.126.act_ref), custom_call_target="tpu_custom_call" | custom-call | flops 3221225472 | bytes 8912896 | tf_op jit(solution)/shard_map/pallas_call | solution.py:363
  263.6 7.5 %shard_map.178 = bf16[1024,768]{1,0:T(8,128)(2,1)} custom-call(s32[1024,1]{1,0:T(8,128)} %get-tuple-element.90.col_ref, f32[1024,768]{1,0:T(8,128)} %get-tuple-element.94.res_ref, bf16[2048,768]{1,0:T(8,128)(2,1)} %bitcast.45), custom_call_target="tpu_custom_call" | custom-call | flops 3221225472 | bytes 7864320 | tf_op jit(solution)/shard_map/pallas_call | solution.py:483
  273.4 7.1 %collective-permute-done.17 = bf16[96,1664]{1,0:T(8,128)(2,1)S(1)} collective-permute-done((bf16[96,1664]{1,0:T(8,128)(2,1)S(1)}, bf16[96,1664]{1,0:T(8,128)(2,1)S(1)}, u32[]{:S(2)}, u32[]{:S(2)}) %collective-permute-start.17) | collective-permute-done | bytes 319520 | tf_op jit(solution)/shard_map/ppermute | solution.py:575
  281.7 3.5 collective-permute-start.21
  286.3 5.9 %collective-permute-done.21 = bf16[2,24,1664]{2,1,0:T(8,128)(2,1)S(1)} collective-permute-done((bf16[2,24,1664]{2,1,0:T(8,128)(2,1)S(1)}, bf16[2,24,1664]{2,1,0:T(8,128)(2,1)S(1)}, u32[]{:S(2)}, u32[]{:S(2)}) %collective-permute-start.21) | collective-permute-done | bytes 159776 | tf_op jit(solution)/shard_map/ppermute | solution.py:575
  292.2 12.0 %collective-permute-done.20 = bf16[2,24,1664]{2,1,0:T(8,128)(2,1)S(1)} collective-permute-done((bf16[2,24,1664]{2,1,0:T(8,128)(2,1)S(1)}, bf16[2,24,1664]{2,1,0:T(8,128)(2,1)S(1)}, u32[]{:S(2)}, u32[]{:S(2)}) %collective-permute-start.20) | collective-permute-done | bytes 159776 | tf_op jit(solution)/shard_map/ppermute | solution.py:575
  305.0 3.2 collective-permute-start.24
  308.3 5.0 %collective-permute-done.22 = bf16[2,24,1664]{2,1,0:T(8,128)(2,1)S(1)} collective-permute-done((bf16[2,24,1664]{2,1,0:T(8,128)(2,1)S(1)}, bf16[2,24,1664]{2,1,0:T(8,128)(2,1)S(1)}, u32[]{:S(2)}, u32[]{:S(2)}) %collective-permute-start.22) | collective-permute-done | bytes 159776 | tf_op jit(solution)/shard_map/ppermute | solution.py:575
  313.3 5.8 %collective-permute-done.23 = bf16[2,24,1664]{2,1,0:T(8,128)(2,1)S(1)} collective-permute-done((bf16[2,24,1664]{2,1,0:T(8,128)(2,1)S(1)}, bf16[2,24,1664]{2,1,0:T(8,128)(2,1)S(1)}, u32[]{:S(2)}, u32[]{:S(2)}) %collective-permute-start.23) | collective-permute-done | bytes 159776 | tf_op jit(solution)/shard_map/ppermute | solution.py:575
  322.2 4.9 %collective-permute-done.25 = bf16[96,1664]{1,0:T(8,128)(2,1)S(1)} collective-permute-done((bf16[96,1664]{1,0:T(8,128)(2,1)S(1)}, bf16[96,1664]{1,0:T(8,128)(2,1)S(1)}, u32[]{:S(2)}, u32[]{:S(2)}) %collective-permute-start.25) | collective-permute-done | bytes 319520 | tf_op jit(solution)/shard_map/ppermute | solution.py:575
  330.8 11.0 %collective-permute-done.28 = bf16[192,1664]{1,0:T(8,128)(2,1)S(1)} collective-permute-done((bf16[192,1664]{1,0:T(8,128)(2,1)S(1)}, bf16[192,1664]{1,0:T(8,128)(2,1)S(1)}, u32[]{:S(2)}, u32[]{:S(2)}) %collective-permute-start.28) | collective-permute-done | bytes 639008 | tf_op jit(solution)/shard_map/ppermute | solution.py:575
  342.6 4.9 %collective-permute-done.29.other_ref = bf16[768,1664]{1,0:T(8,128)(2,1)} collective-permute-done((bf16[768,1664]{1,0:T(8,128)(2,1)S(1)}, bf16[768,1664]{1,0:T(8,128)(2,1)}, u32[]{:S(2)}, u32[]{:S(2)}) %collective-permute-start.29) | collective-permute-done | bytes 2555936 | tf_op jit(solution)/shard_map/ppermute | solution.py:575
  347.6 6.4 %shard_map.179 = (f32[768,2304]{1,0:T(8,128)}, f32[768,768]{1,0:T(8,128)}, f32[1,768]{1,0:T(1,128)}, f32[1,768]{1,0:T(1,128)}) custom-call(bf16[768,1664]{1,0:T(8,128)(2,1)} %copy-done.1, bf16[768,1664]{1,0:T(8,128)(2,1)} %collective-permute-done.29.other_ref), custom_call_target="tpu_custom_call" | custom-call | bytes 14155776 | tf_op jit(solution)/shard_map/pallas_call | solution.py:738
  356.5 9.6 %reduce-scatter.8.cloned.1.call-done.refs_1_ = bf16[1,768,256]{2,1,0:T(8,128)(2,1)} async-done(((bf16[1,768,1024]{2,1,0:T(8,128)(2,1)}), bf16[1,768,256]{2,1,0:T(8,128)(2,1)}) %reduce-scatter.8.cloned.1.call-update) | async-done | bytes 393232 | tf_op jit(solution)/shard_map/reduce_scatter | solution.py:823
  (128 shorter events, 46.0 us)
Async XLA Ops:
  14.3 45.3 %all-to-all-start = ((bf16[8,256,768]{2,1,0:T(8,128)(2,1)}), bf16[8,256,768]{2,1,0:T(8,128)(2,1)S(1)}, u32[]{:S(2)}, u32[]{:S(2)}) async-start(bf16[8,256,768]{2,1,0:T(8,128)(2,1)} %get-tuple-element.103), calls=%async_computation | async-start | bytes 6291456 | tf_op jit(solution)/shard_map/all_to_all | solution.py:787
  19.6 213.9 %reduce-scatter.4.cloned.1.call-start = ((), (), s32[]{:S(2)}) async-start(), calls=%async_computation.5 | async-start | bytes 5898240 | tf_op jit(solution)/shard_map/reduce_scatter | solution.py:823
  55.5 20.2 %collective-permute-start = (bf16[256,768]{1,0:T(8,128)(2,1)}, bf16[256,768]{1,0:T(8,128)(2,1)S(1)}, u32[]{:S(2)}, u32[]{:S(2)}) collective-permute-start(bf16[256,768]{1,0:T(8,128)(2,1)} %get-tuple-element.97), channel_id=1, source_target_pairs={{0,2},{1,3},{2,0},{3,1},{4,6},{5,7},{6,4},{7,5},{8,10},{9,11},{10,... | collective-permute-start | bytes 1179656 | tf_op jit(solution)/shard_map/ppermute | solution.py:614
  57.2 18.6 %collective-permute-start.1 = (bf16[256,768]{1,0:T(8,128)(2,1)}, bf16[256,768]{1,0:T(8,128)(2,1)}, u32[]{:S(2)}, u32[]{:S(2)}) collective-permute-start(bf16[256,768]{1,0:T(8,128)(2,1)} %get-tuple-element.98), channel_id=1, source_target_pairs={{0,3},{1,2},{2,1},{3,0},{4,7},{5,6},{6,5},{7,4},{8,11},{9,10},{10,... | collective-permute-start | bytes 1179656 | tf_op jit(solution)/shard_map/ppermute | solution.py:614
  57.2 18.6 %collective-permute-start.2 = (bf16[256,768]{1,0:T(8,128)(2,1)}, bf16[256,768]{1,0:T(8,128)(2,1)}, u32[]{:S(2)}, u32[]{:S(2)}) collective-permute-start(bf16[256,768]{1,0:T(8,128)(2,1)} %get-tuple-element.99), channel_id=1, source_target_pairs={{0,4},{1,5},{2,6},{3,7},{4,0},{5,1},{6,2},{7,3},{8,12},{9,13},{10,... | collective-permute-start | bytes 1179656 | tf_op jit(solution)/shard_map/ppermute | solution.py:614
  58.9 18.1 %collective-permute-start.3 = (bf16[256,768]{1,0:T(8,128)(2,1)}, bf16[256,768]{1,0:T(8,128)(2,1)}, u32[]{:S(2)}, u32[]{:S(2)}) collective-permute-start(bf16[256,768]{1,0:T(8,128)(2,1)} %get-tuple-element.100), channel_id=1, source_target_pairs={{0,5},{1,4},{2,7},{3,6},{4,1},{5,0},{6,3},{7,2},{8,13},{9,12},{10,... | collective-permute-start | bytes 1179656 | tf_op jit(solution)/shard_map/ppermute | solution.py:614
  77.0 31.2 %collective-permute-start.5 = (bf16[256,768]{1,0:T(8,128)(2,1)}, bf16[256,768]{1,0:T(8,128)(2,1)S(1)}, u32[]{:S(2)}, u32[]{:S(2)}) collective-permute-start(bf16[256,768]{1,0:T(8,128)(2,1)} %get-tuple-element.105), channel_id=1, source_target_pairs={{0,6},{1,7},{2,4},{3,5},{4,2},{5,3},{6,0},{7,1},{8,14},{9,15},{10,... | collective-permute-start | bytes 1179656 | tf_op jit(solution)/shard_map/ppermute | solution.py:614
  79.5 29.0 %collective-permute-start.6 = (bf16[256,768]{1,0:T(8,128)(2,1)}, bf16[256,768]{1,0:T(8,128)(2,1)S(1)}, u32[]{:S(2)}, u32[]{:S(2)}) collective-permute-start(bf16[256,768]{1,0:T(8,128)(2,1)} %get-tuple-element.106), channel_id=1, source_target_pairs={{0,7},{1,6},{2,5},{3,4},{4,3},{5,2},{6,1},{7,0},{8,15},{9,14},{10,... | collective-permute-start | bytes 1179656 | tf_op jit(solution)/shard_map/ppermute | solution.py:614
  79.5 27.2 %collective-permute-start.7 = (bf16[256,768]{1,0:T(8,128)(2,1)}, bf16[256,768]{1,0:T(8,128)(2,1)S(1)}, u32[]{:S(2)}, u32[]{:S(2)}) collective-permute-start(bf16[256,768]{1,0:T(8,128)(2,1)} %get-tuple-element.108), channel_id=1, source_target_pairs={{0,1},{1,0},{2,3},{3,2},{4,5},{5,4},{6,7},{7,6},{8,9},{9,8},{10,11... | collective-permute-start | bytes 1179656 | tf_op jit(solution)/shard_map/ppermute | solution.py:614
  105.0 18.7 %collective-permute-start.8 = (bf16[256,768]{1,0:T(8,128)(2,1)}, bf16[256,768]{1,0:T(8,128)(2,1)S(1)}, u32[]{:S(2)}, u32[]{:S(2)}) collective-permute-start(bf16[256,768]{1,0:T(8,128)(2,1)} %get-tuple-element.120), channel_id=1, source_target_pairs={{0,2},{1,3},{2,0},{3,1},{4,6},{5,7},{6,4},{7,5},{8,10},{9,11},{10,... | collective-permute-start | bytes 1179656 | tf_op jit(solution)/shard_map/ppermute | solution.py:614
  106.7 17.3 %collective-permute-start.9 = (bf16[256,768]{1,0:T(8,128)(2,1)}, bf16[256,768]{1,0:T(8,128)(2,1)S(1)}, u32[]{:S(2)}, u32[]{:S(2)}) collective-permute-start(bf16[256,768]{1,0:T(8,128)(2,1)} %get-tuple-element.121), channel_id=1, source_target_pairs={{0,3},{1,2},{2,1},{3,0},{4,7},{5,6},{6,5},{7,4},{8,11},{9,10},{10,... | collective-permute-start | bytes 1179656 | tf_op jit(solution)/shard_map/ppermute | solution.py:614
  106.7 17.3 %collective-permute-start.10 = (bf16[256,768]{1,0:T(8,128)(2,1)}, bf16[256,768]{1,0:T(8,128)(2,1)S(1)}, u32[]{:S(2)}, u32[]{:S(2)}) collective-permute-start(bf16[256,768]{1,0:T(8,128)(2,1)} %get-tuple-element.122), channel_id=1, source_target_pairs={{0,4},{1,5},{2,6},{3,7},{4,0},{5,1},{6,2},{7,3},{8,12},{9,13},{10,... | collective-permute-start | bytes 1179656 | tf_op jit(solution)/shard_map/ppermute | solution.py:614
  108.2 18.2 %collective-permute-start.11 = (bf16[256,768]{1,0:T(8,128)(2,1)}, bf16[256,768]{1,0:T(8,128)(2,1)S(1)}, u32[]{:S(2)}, u32[]{:S(2)}) collective-permute-start(bf16[256,768]{1,0:T(8,128)(2,1)} %get-tuple-element.123), channel_id=1, source_target_pairs={{0,5},{1,4},{2,7},{3,6},{4,1},{5,0},{6,3},{7,2},{8,13},{9,12},{10,... | collective-permute-start | bytes 1179656 | tf_op jit(solution)/shard_map/ppermute | solution.py:614
  154.9 23.3 %collective-permute-start.12 = (bf16[256,768]{1,0:T(8,128)(2,1)}, bf16[256,768]{1,0:T(8,128)(2,1)}, u32[]{:S(2)}, u32[]{:S(2)}) collective-permute-start(bf16[256,768]{1,0:T(8,128)(2,1)} %get-tuple-element.129), channel_id=1, source_target_pairs={{0,6},{1,7},{2,4},{3,5},{4,2},{5,3},{6,0},{7,1},{8,14},{9,15},{10,... | collective-permute-start | bytes 1179656 | tf_op jit(solution)/shard_map/ppermute | solution.py:614
  157.8 20.5 %collective-permute-start.13 = (bf16[256,768]{1,0:T(8,128)(2,1)S(1)}, bf16[256,768]{1,0:T(8,128)(2,1)}, u32[]{:S(2)}, u32[]{:S(2)}) collective-permute-start(bf16[256,768]{1,0:T(8,128)(2,1)S(1)} %copy-done.16), channel_id=1, source_target_pairs={{0,7},{1,6},{2,5},{3,4},{4,3},{5,2},{6,1},{7,0},{8,15},{9,14},{10,... | collective-permute-start | bytes 1179656 | tf_op jit(solution)/shard_map/ppermute | solution.py:614
  173.6 46.9 %all-to-all-start.1 = ((bf16[8,256,768]{2,1,0:T(8,128)(2,1)}), bf16[8,256,768]{2,1,0:T(8,128)(2,1)S(1)}, u32[]{:S(2)}, u32[]{:S(2)}) async-start(bf16[8,256,768]{2,1,0:T(8,128)(2,1)} %shard_map.170), calls=%async_computation.1 | async-start | bytes 6291456 | tf_op jit(solution)/shard_map/all_to_all | solution.py:787
  177.5 126.9 %reduce-scatter.6.cloned.1.call-start = ((), (), s32[]{:S(2)}) async-start(), calls=%async_computation.6 | async-start | bytes 3932160 | tf_op jit(solution)/shard_map/reduce_scatter | solution.py:823
  178.2 187.9 %reduce-scatter.8.cloned.1.call-start = ((), (), s32[]{:S(2)}) async-start(), calls=%async_computation.7 | async-start | bytes 1966080 | tf_op jit(solution)/shard_map/reduce_scatter | solution.py:823
  233.1 13.4 %collective-permute-start.14 = (bf16[768,1536]{1,0:T(8,128)(2,1)}, bf16[768,1536]{1,0:T(8,128)(2,1)S(1)}, u32[]{:S(2)}, u32[]{:S(2)}) collective-permute-start(bf16[768,1536]{1,0:T(8,128)(2,1)} %get-tuple-element.146), channel_id=1, source_target_pairs={{0,1},{1,0},{2,3},{3,2},{4,5},{5,4},{6,7},{7,6},{8,9},{9,8},{10,11... | collective-permute-start | bytes 7077896 | tf_op jit(solution)/shard_map/ppermute | solution.py:575
  252.6 18.5 %collective-permute-start.15 = (bf16[192,1664]{1,0:T(8,128)(2,1)}, bf16[192,1664]{1,0:T(8,128)(2,1)S(1)}, u32[]{:S(2)}, u32[]{:S(2)}) collective-permute-start(bf16[192,1664]{1,0:T(8,128)(2,1)} %get-tuple-element.154), channel_id=1, source_target_pairs={{0,2},{2,0},{1,3},{3,1},{4,6},{6,4},{5,7},{7,5},{8,10},{10,8},{9,1... | collective-permute-start | bytes 1916936 | tf_op jit(solution)/shard_map/ppermute | solution.py:575
  254.3 16.7 %collective-permute-start.16 = (bf16[192,1664]{1,0:T(8,128)(2,1)}, bf16[192,1664]{1,0:T(8,128)(2,1)S(1)}, u32[]{:S(2)}, u32[]{:S(2)}) collective-permute-start(bf16[192,1664]{1,0:T(8,128)(2,1)} %get-tuple-element.156), channel_id=1, source_target_pairs={{0,4},{4,0},{1,5},{5,1},{2,6},{6,2},{3,7},{7,3},{8,12},{12,8},{9,1... | collective-permute-start | bytes 1916936 | tf_op jit(solution)/shard_map/ppermute | solution.py:575
  271.3 9.2 %collective-permute-start.17 = (bf16[96,1664]{1,0:T(8,128)(2,1)S(1)}, bf16[96,1664]{1,0:T(8,128)(2,1)S(1)}, u32[]{:S(2)}, u32[]{:S(2)}) collective-permute-start(bf16[96,1664]{1,0:T(8,128)(2,1)S(1)} %constant_dynamic-slice_fusion.1), channel_id=1, source_target_pairs={{0,4},{4,0},{1,5},{5,1},{2,6},{6,2},{3,7},{7,3},{8,12},{12,8},{9,1... | collective-permute-start | bytes 958472 | tf_op jit(solution)/shard_map/ppermute | solution.py:575
  272.7 8.8 %collective-permute-start.18 = (bf16[96,1664]{1,0:T(8,128)(2,1)S(1)}, bf16[96,1664]{1,0:T(8,128)(2,1)S(1)}, u32[]{:S(2)}, u32[]{:S(2)}) collective-permute-start(bf16[96,1664]{1,0:T(8,128)(2,1)S(1)} %constant_dynamic-slice_fusion), channel_id=1, source_target_pairs={{0,2},{2,0},{1,3},{3,1},{4,6},{6,4},{5,7},{7,5},{8,10},{10,8},{9,1... | collective-permute-start | bytes 958472 | tf_op jit(solution)/shard_map/ppermute | solution.py:575
  281.7 10.5 %collective-permute-start.21 = (bf16[2,24,1664]{2,1,0:T(8,128)(2,1)S(1)}, bf16[2,24,1664]{2,1,0:T(8,128)(2,1)S(1)}, u32[]{:S(2)}, u32[]{:S(2)}) collective-permute-start(bf16[2,24,1664]{2,1,0:T(8,128)(2,1)S(1)} %get-tuple-element.176), channel_id=1, source_target_pairs={{0,24},{8,0},{16,8},{24,16},{1,25},{9,1},{17,9},{25,17},{2,26},{10... | collective-permute-start | bytes 479240 | tf_op jit(solution)/shard_map/ppermute | solution.py:575
  285.2 19.0 %collective-permute-start.20 = (bf16[2,24,1664]{2,1,0:T(8,128)(2,1)S(1)}, bf16[2,24,1664]{2,1,0:T(8,128)(2,1)S(1)}, u32[]{:S(2)}, u32[]{:S(2)}) collective-permute-start(bf16[2,24,1664]{2,1,0:T(8,128)(2,1)S(1)} %get-tuple-element.175), channel_id=1, source_target_pairs={{0,16},{8,24},{16,0},{24,8},{1,17},{9,25},{17,1},{25,9},{2,18},{10... | collective-permute-start | bytes 479240 | tf_op jit(solution)/shard_map/ppermute | solution.py:575
  285.2 19.0 %collective-permute-start.19 = (bf16[2,24,1664]{2,1,0:T(8,128)(2,1)S(1)}, bf16[2,24,1664]{2,1,0:T(8,128)(2,1)S(1)}, u32[]{:S(2)}, u32[]{:S(2)}) collective-permute-start(bf16[2,24,1664]{2,1,0:T(8,128)(2,1)S(1)} %get-tuple-element.174), channel_id=1, source_target_pairs={{0,8},{8,16},{16,24},{24,0},{1,9},{9,17},{17,25},{25,1},{2,10},{10... | collective-permute-start | bytes 479240 | tf_op jit(solution)/shard_map/ppermute | solution.py:575
  304.4 8.9 %collective-permute-start.22 = (bf16[2,24,1664]{2,1,0:T(8,128)(2,1)S(1)}, bf16[2,24,1664]{2,1,0:T(8,128)(2,1)S(1)}, u32[]{:S(2)}, u32[]{:S(2)}) collective-permute-start(bf16[2,24,1664]{2,1,0:T(8,128)(2,1)S(1)} %add_convert_fusion.4), channel_id=1, source_target_pairs={{0,8},{8,16},{16,24},{24,0},{1,9},{9,17},{17,25},{25,1},{2,10},{10... | collective-permute-start | bytes 479240 | tf_op jit(solution)/shard_map/ppermute | solution.py:575
  304.4 14.7 %collective-permute-start.23 = (bf16[2,24,1664]{2,1,0:T(8,128)(2,1)S(1)}, bf16[2,24,1664]{2,1,0:T(8,128)(2,1)S(1)}, u32[]{:S(2)}, u32[]{:S(2)}) collective-permute-start(bf16[2,24,1664]{2,1,0:T(8,128)(2,1)S(1)} %add_convert_fusion.4), channel_id=1, source_target_pairs={{0,16},{8,24},{16,0},{24,8},{1,17},{9,25},{17,1},{25,9},{2,18},{10... | collective-permute-start | bytes 479240 | tf_op jit(solution)/shard_map/ppermute | solution.py:575
  305.0 14.1 %collective-permute-start.24 = (bf16[2,24,1664]{2,1,0:T(8,128)(2,1)S(1)}, bf16[2,24,1664]{2,1,0:T(8,128)(2,1)S(1)}, u32[]{:S(2)}, u32[]{:S(2)}) collective-permute-start(bf16[2,24,1664]{2,1,0:T(8,128)(2,1)S(1)} %add_convert_fusion.4), channel_id=1, source_target_pairs={{0,24},{8,0},{16,8},{24,16},{1,25},{9,1},{17,9},{25,17},{2,26},{10... | collective-permute-start | bytes 479240 | tf_op jit(solution)/shard_map/ppermute | solution.py:575
  319.4 7.8 %collective-permute-start.25 = (bf16[96,1664]{1,0:T(8,128)(2,1)S(1)}, bf16[96,1664]{1,0:T(8,128)(2,1)S(1)}, u32[]{:S(2)}, u32[]{:S(2)}) collective-permute-start(bf16[96,1664]{1,0:T(8,128)(2,1)S(1)} %get-tuple-element.173), channel_id=1, source_target_pairs={{0,4},{4,0},{1,5},{5,1},{2,6},{6,2},{3,7},{7,3},{8,12},{12,8},{9,1... | collective-permute-start | bytes 958472 | tf_op jit(solution)/shard_map/ppermute | solution.py:575
  328.4 13.4 %collective-permute-start.28 = (bf16[192,1664]{1,0:T(8,128)(2,1)S(1)}, bf16[192,1664]{1,0:T(8,128)(2,1)S(1)}, u32[]{:S(2)}, u32[]{:S(2)}) collective-permute-start(bf16[192,1664]{1,0:T(8,128)(2,1)S(1)} %constant_dynamic-update-slice_fusion.4), channel_id=1, source_target_pairs={{0,4},{4,0},{1,5},{5,1},{2,6},{6,2},{3,7},{7,3},{8,12},{12,8},{9,1... | collective-permute-start | bytes 1916936 | tf_op jit(solution)/shard_map/ppermute | solution.py:575
  329.0 13.3 %collective-permute-start.27 = (bf16[192,1664]{1,0:T(8,128)(2,1)S(1)}, bf16[192,1664]{1,0:T(8,128)(2,1)S(1)}, u32[]{:S(2)}, u32[]{:S(2)}) collective-permute-start(bf16[192,1664]{1,0:T(8,128)(2,1)S(1)} %constant_dynamic-update-slice_fusion.6), channel_id=1, source_target_pairs={{0,2},{2,0},{1,3},{3,1},{4,6},{6,4},{5,7},{7,5},{8,10},{10,8},{9,1... | collective-permute-start | bytes 1916936 | tf_op jit(solution)/shard_map/ppermute | solution.py:575
  (20 other events, 163.6 us)
Sparse Core Ops, SparseCore 0:
  141.3 86.8 reduce-scatter.3
  230.5 64.9 reduce-scatter.5
  329.1 36.9 reduce-scatter.7

commit v3 on v2

--- a/solution.py
+++ b/solution.py
@@ -64,7 +64,7 @@
 
 
 def route_body(
-    ids_ref, table_ref, cot_ref, row_ref, col_ref, first_ref, send_ref, *, sides, capacity
+    ids_ref, table_ref, cot_ref, row_ref, col_ref, send_ref, *, sides, capacity
 ):
     high_side, low_side = sides
     count = ids_ref.shape[1]
@@ -89,9 +89,8 @@
     row = target.astype(jnp.int32)
     row_ref[...] = row
     first = chosen.astype(F32) * capacity + rank
-    turned = jnp.transpose(jnp.concatenate([target, first] * 4, 0))
+    turned = jnp.transpose(jnp.broadcast_to(first, (8, count)))
     col_ref[...] = turned[:, :1].astype(jnp.int32)
-    first_ref[...] = turned[:, 1:2].astype(jnp.int32)
     first = first.astype(jnp.int32)
     place([send_ref.at[part] for part in range(send_ref.shape[0])], first, cot_ref, capacity)
 
@@ -112,7 +111,6 @@
         moved=2 * (count + slots) * width,
         out_shape=[
             jax.ShapeDtypeStruct((1, count), jnp.int32),
-            jax.ShapeDtypeStruct((count, 1), jnp.int32),
             jax.ShapeDtypeStruct((count, 1), jnp.int32),
             jax.ShapeDtypeStruct((experts, capacity, width), BF),
         ],
@@ -272,8 +270,7 @@
 def expert_body(from_ref, *refs, parts, kept):
     x_refs, g_refs = refs[:parts], refs[parts : 2 * parts]
     w_ref, out_w_ref = refs[2 * parts : 2 * parts + 2]
-    act_ref, gh_ref, x_ref, g_ref, *back_refs = refs[2 * parts + 2 + kept : -1]
-    acc_ref = refs[-1]
+    act_ref, gh_ref, x_ref, g_ref = refs[2 * parts + 2 + kept :]
     step = pl.program_id(0)
     size = x_refs[0].shape[0]
     c1 = 2.0 * math.sqrt(2.0 / math.pi)
@@ -293,22 +290,7 @@
     act = h * half
     slope = half + (act * (1.0 - half)) * (c1 + (3.0 * c2) * square)
     act_ref[...] = act.astype(BF)
-    gh = (ga * slope).astype(BF)
-    gh_ref[...] = gh
-    back = nt(gh, w_ref[...])
-
-    @pl.when(step == 0)
-    def _():
-        acc_ref[...] = back
-
-    @pl.when(step > 0)
-    def _():
-        acc_ref[...] += back
-
-    @pl.when(step == pl.num_programs(0) - 1)
-    def _():
-        for part in range(parts):
-            back_refs[part][...] = acc_ref[part * size : (part + 1) * size, :].astype(BF)
+    gh_ref[...] = (ga * slope).astype(BF)
 
 
 def expert(chips, place_at, total, source, xs, g, w, out_w, earlier):
@@ -331,17 +313,15 @@
             + [pick(2 * chip + core) for chip in chips for core in range(2)]
             + [weight, weight]
             + [pl.BlockSpec(memory_space=pl.ANY)] * len(earlier),
-            out_specs=[tile, tile, rows, rows] + [whole((size, width))] * parts,
-            scratch_shapes=[pltpu.VMEM((tall, width), F32)],
+            out_specs=[tile, tile, rows, rows],
         ),
         out_shape=[jax.ShapeDtypeStruct((every, units), BF)] * 2
-        + [jax.ShapeDtypeStruct((every, width), BF)] * 2
-        + [jax.ShapeDtypeStruct((size, width), BF)] * parts,
+        + [jax.ShapeDtypeStruct((every, width), BF)] * 2,
         input_output_aliases={1 + 2 * parts + 2 + i: i for i in range(len(earlier))},
         compiler_params=pltpu.CompilerParams(vmem_limit_bytes=60 << 20),
         cost_estimate=pl.CostEstimate(
-            flops=6 * tall * width * units,
-            bytes_accessed=2 * (5 * tall * width + 2 * width * units + 2 * tall * units),
+            flops=4 * tall * width * units,
+            bytes_accessed=2 * (4 * tall * width + 2 * width * units + 2 * tall * units),
             transcendentals=0,
         ),
     )(source, *xs, *[g] * parts, w, out_w, *earlier)
@@ -412,22 +392,12 @@
     )(chips, active, w)
 
 
-def unplace(back_refs, col, rows_ref):
-    size = back_refs[0].shape[0]
-
-    @pl.when(pl.program_id(0) == 0)
-    def _():
-        for part, back_ref in enumerate(back_refs):
-            rows_ref[part * size : (part + 1) * size, :] = back_ref[...]
-
-    placer = (iota((col.shape[0], rows_ref.shape[0]), 1) == col).astype(BF)
-    return nn(placer, rows_ref[...])
-
-
-def collect_back_body(col_ref, res_ref, cot_ref, gain_ref, w_ref, *rest):
-    back_refs, (gres_ref, gattn_ref, gatt_ref, ggain_ref, rows_ref) = rest[:-5], rest[-5:]
+def collect_back_body(
+    col_ref, res_ref, cot_ref, gain_ref, w_ref, back_ref, gres_ref, gattn_ref, gatt_ref, ggain_ref
+):
     step = pl.program_id(0)
-    grad = unplace(back_refs, col_ref[...], rows_ref)
+    placer = (iota((col_ref.shape[0], back_ref.shape[0]), 1) == col_ref[...]).astype(BF)
+    grad = nn(placer, back_ref[...])
     x_hat, rate = norm_parts(res_ref[...])
     gres = cot_ref[...].astype(F32) + norm_grad(x_hat, rate, grad * gain_ref[...])
     gres_ref[...] = gres
@@ -445,21 +415,19 @@
         ggain_ref[...] += gain_part
 
 
-def collect_back(backs, col, residual, cot, gain, w):
+def collect_back(back, col, residual, cot, gain, w):
     count, width = cot.shape
-    size = backs[0].shape[0]
     block = 256
     row = pl.BlockSpec((block, width), lambda i: (i, 0))
     return call(
         collect_back_body,
-        flops=2 * count * width * (len(backs) * size + 2 * width),
-        moved=2 * width * (len(backs) * size + 8 * count),
+        flops=2 * count * width * (back.shape[0] + 2 * width),
+        moved=2 * width * (back.shape[0] + 8 * count),
         grid=(count // block,),
         in_specs=[
             pl.BlockSpec((block, 1), lambda i: (i, 0)), row, row,
-            whole(gain.shape), whole(w.shape),
-        ]
-        + [whole((size, width))] * len(backs),
+            whole(gain.shape), whole(w.shape), whole(back.shape),
+        ],
         out_specs=[row, row, row, whole((1, width))],
         out_shape=[
             jax.ShapeDtypeStruct((count, width), F32),
@@ -467,8 +435,7 @@
             jax.ShapeDtypeStruct((count, width), BF),
             jax.ShapeDtypeStruct((1, width), F32),
         ],
-        scratch_shapes=[pltpu.VMEM((len(backs) * size, width), BF)],
-    )(col, residual, cot, gain, w, *backs)
+    )(col, residual, cot, gain, w, back)
 
 
 def collect_body(col_ref, res_ref, back_ref, out_ref):
@@ -600,11 +567,11 @@
     return jnp.stack(out).astype(jnp.int32)
 
 
-def plane_shift(a, part, sign, sides):
+def plane_shift(a, part, sides):
     if part == 0:
         return a
     high, low = sides
-    dy, dx, dc = sign * (part // (2 * low)), sign * (part // 2 % low), part % 2
+    dy, dx, dc = part // (2 * low), part // 2 % low, part % 2
     pairs = []
     for y in range(high):
         for x in range(low):
@@ -617,15 +584,6 @@
 def cut(a, index, pieces, dim):
     size = a.shape[dim] // pieces
     return lax.dynamic_slice_in_dim(a, index * size, size, dim)
-
-
-def scatter_sum(a, axis, dim):
-    n = lax.axis_size(axis)
-    me = lax.axis_index(axis)
-    total = cut(a, me, n, dim).astype(F32)
-    for k in range(1, n):
-        total += shift(cut(a, lax.rem(me + k, n), n, dim), axis, k).astype(F32)
-    return total.astype(a.dtype)
 
 
 def gather_all(a, axis, dim):
@@ -692,18 +650,20 @@
     return out.astype(parts[0].dtype)
 
 
-def sum_planes(top, low, first):
-    top = scatter_sum(total(top), "y", 0)
-    low = scatter_sum(total(low), "x", 0)
-    both = scatter_sum(jnp.stack([top, low]), "dp", 1)
-    both = after(both, first)
-    return gather_all(both, "dp", 1), both
-
-
-def gather_planes(both, during_last):
+def pieces_of(a, axis, dim):
+    n = lax.axis_size(axis)
+    me = lax.axis_index(axis)
+    return [cut(a, lax.rem(me + k, n), n, dim) for k in range(n)]
+
+
+def gather_planes(parts):
+    return gather_all(total(parts), "dp", 1)
+
+
+def gather_plane(both, during):
     top = gather_all(both[0], "y", 0)
     low = gather_all(both[1], "x", 0)
-    top, low = after((top, low), *during_last)
+    top, low = after((top, low), *during)
     top = gather_all(top, "x", 0)
     low = gather_all(low, "y", 0)
     mine = jnp.concatenate([top, low], 0)
@@ -715,8 +675,12 @@
     first = lax.axis_index("core") == 0
     gains = mine_ref[:, 2 * width :].astype(F32) + other_ref[:, 2 * width :].astype(F32)
     gains = jnp.transpose(gains)
-    one_ref[...] = gains[:1]
-    two_ref[...] = gains[1:2]
+    lines = gains.shape[1] // 128
+    for part in range(lines):
+        line = pl.ds(pl.program_id(0) * lines + part, 1)
+        columns = slice(part * 128, (part + 1) * 128)
+        one_ref[line, :] = gains[:1, columns]
+        two_ref[line, :] = gains[1:2, columns]
 
     @pl.when(first)
     def _():
@@ -737,15 +701,14 @@
     row = lambda wide: pl.BlockSpec((block, wide), lambda i: (i, 0))
     return call(
         unpack_body,
-        moved=24 * width * width,
         grid=(width // block,),
         in_specs=[row(mine.shape[1])] * 2,
-        out_specs=[row(3 * width), row(width)] + [pl.BlockSpec((1, block), lambda i: (0, i))] * 2,
+        out_specs=[row(3 * width), row(width)] + [whole((width // 128, 128))] * 2,
         out_shape=[
             jax.ShapeDtypeStruct((width, 3 * width), F32),
             jax.ShapeDtypeStruct((width, width), F32),
-            jax.ShapeDtypeStruct((1, width), F32),
-            jax.ShapeDtypeStruct((1, width), F32),
+            jax.ShapeDtypeStruct((width // 128, 128), F32),
+            jax.ShapeDtypeStruct((width // 128, 128), F32),
         ],
     )(mine, other)
 
@@ -786,10 +749,10 @@
     def exchange_all(a):
         return lax.all_to_all(a, PLANE, split_axis=0, concat_axis=0, tiled=True)
 
-    def exchange(parts, sign):
-        return {i: plane_shift(a, i, sign, sides) for i, a in parts.items()}
-
-    row, col, first_col, grad_send = route(
+    def exchange(parts):
+        return {i: plane_shift(a, i, sides) for i, a in parts.items()}
+
+    row, col, grad_send = route(
         token_ids.reshape(1, count), hash_table.reshape(-1, 128), cot, sides, capacity
     )
     flat_grad = exchange_all(grad_send)
@@ -798,61 +761,56 @@
     residual, *outgoing = dispatch(attended, w_proj, x, second_gain, row, experts, capacity)
     outgoing = dict(enumerate(outgoing))
     far = {i: outgoing.pop(i) for i in range(experts - 2, experts)}
-    arrived = exchange(outgoing, 1)
+    arrived = exchange(outgoing)
     source = source_parts(sides)
-    kept, backs = (), {}
+    kept = ()
     plan = groups(experts // 2)
     for chips, place_at in plan:
         parts = [2 * chip + core for chip in chips for core in range(2)]
-        flat = after(flat_grad, *[backs[i] for i in sorted(backs) if i < 2 and len(parts) < 4])
-        out = expert(
-            chips, place_at, experts, source, [arrived[i] for i in parts], flat,
+        kept = expert(
+            chips, place_at, experts, source, [arrived[i] for i in parts], flat_grad,
             inner, outer, kept,
         )
-        kept = out[:4]
-        backs.update(exchange(dict(zip(parts, out[4:])), -1))
         if chips == (0,):
             near = [arrived[i] for i in range(2, experts - 2)]
-            arrived.update(exchange(after(far, near, kept[0]), 1))
+            arrived.update(exchange(after(far, near, kept[0])))
     active, grad_hidden, rows_in, rows_grad = kept
+    tall_first = sorted((chips for chips, _ in plan), key=lambda chips: (-len(chips), chips))
+    chips = jnp.stack([source[2 * chip] // 2 for chips in tall_first for chip in chips])
     shares = lax.axis_size("dp")
     share = inner.shape[1] // shares
-    near_backs = [backs[i] for i in range(experts - 2)]
-    grad_back = near_backs + [backs[i] for i in range(experts - 2, experts)]
     def scatter(a):
         return lax.psum_scatter(a[None], "dp", scatter_dimension=2, tiled=True)
 
-    grad_outer = weight_share(after(rows_grad, *near_backs), active, shares, 0, share)
-    grad_w_out = widen(scatter(grad_outer))
-    part = share * 2 // 3 // 256 * 256
-    grad_inner = weight_share(after(rows_in, grad_outer), grad_hidden, shares, 0, part)
-    grad_w_in = [scatter(grad_inner)]
-    tall_first = sorted((chips for chips, _ in plan), key=lambda chips: (-len(chips), chips))
-    order = [chip for chips in tall_first for chip in chips]
-    chips = jnp.stack([source[2 * chip] // 2 for chip in order])
+    grad_outer = weight_share(rows_grad, active, shares, 0, share)
+    grad_w_out = scatter(grad_outer)
+    grad_flat = make_result(chips, after(grad_hidden, grad_outer), inner, experts)
+    grad_back = exchange_all(grad_flat).reshape(-1, width)
+    grad_inner = weight_share(after(rows_in, grad_flat), grad_hidden, shares, 0, share)
+    grad_w_in = scatter(grad_inner)
     results = make_result(chips, after(active, grad_inner), outer, experts)
-    returned = exchange_all(results)
+    returned = exchange_all(after(results, grad_back))
 
     grad_residual, grad_attn, grad_attended, grad_gain_two = collect_back(
         after(grad_back, results), col, residual, cot, second_gain, w_proj
     )
     grad_packed = attend_back(packed, attended, totals, grad_attended)
-    returned, grad_packed = after((returned, grad_packed), grad_packed)
     keep, send = weight_grads(normed, grad_packed, attended, grad_attn)
     got = shift(send, "core", 1)
     grad_tokens, grad_gain_one = grad_in(
         x, first_gain, w_qkv, after(grad_packed, keep, grad_w_out), grad_residual
     )
     top, low = split(keep, after(got, grad_tokens), grad_gain_one, grad_gain_two, sides)
-    grad_later = weight_share(
-        after(rows_in, top, low), grad_hidden, shares, part, share - part
-    )
-    outputs = collect(after(returned.reshape(-1, width), grad_later), first_col, residual)
-    top, low = after((add_up(top, "x"), add_up(low, "y")), outputs)
-    both, summed = sum_planes(top, low, grad_w_in[0])
-    grad_w_in.append(scatter(after(grad_later, summed)))
-    grad_qkv, grad_proj, one, two = unpack(*gather_planes(both, ()))
-    grad_w_in = widen(grad_w_in[0], after(grad_w_in[1], grad_qkv))
+    grad_w_out = widen(after(grad_w_out, top, low))
+    outputs = collect(after(returned.reshape(-1, width), top, low), col, residual)
+    top, low = after((add_up(top, "x"), add_up(low, "y")), outputs, grad_w_out)
+    top = add_up(pieces_of(total(top), "y", 0), "y")
+    low = add_up(pieces_of(total(low), "x", 0), "x")
+    both = jnp.stack([total(top), total(low)])
+    both = gather_planes(add_up(pieces_of(both, "dp", 1), "dp"))
+    grad_w_in = widen(after(grad_w_in, both))
+    mine, other = gather_plane(both, (grad_w_in,))
+    grad_qkv, grad_proj, one, two = unpack(mine, other)
     return (
         outputs.reshape(tokens.shape),
         grad_tokens.reshape(tokens.shape),

time: 380 us -> 375 us (0.987)
  Pallas kernels: 235 us -> 228 us
    pallas_call x1 -> x2, Pallas kernels: 15.9 us -> 31.6 us  [make_result(): pl.pallas_call(result_body, grid_spec=pltpu.PrefetchScalarGridSpec(num_sc...]
    pallas_call x3, Pallas kernels: 53.7 us -> 38.4 us  [expert(): pl.pallas_call(functools.partial(expert_body, parts=parts, kept=len(earli...]
    reduce_scatter x3 -> x2, waiting for transfers between devices: 9.59 us -> 0.02 us  [scatter(): return lax.psum_scatter(a[None], 'dp', scatter_dimension=2, tiled=True)]
    all_to_all x2 -> x3, waiting for transfers between devices: 0.01 us -> 7.36 us  [exchange_all(): return lax.all_to_all(a, PLANE, split_axis=0, concat_axis=0, tiled=True)]
    ppermute x14 -> x7, starting transfers between devices: 13.4 us -> 6.52 us  [plane_shift(): return lax.ppermute(a, PLANE, pairs)]
    pallas_call x3 -> x2, Pallas kernels: 35.5 us -> 29.3 us  [weight_share(): call(weight_share_body, flops=2 * rows * width * shares * size, moved=2 *...]
    all_to_all x2 -> x3, starting transfers between devices: 9.16 us -> 13.3 us  [exchange_all(): return lax.all_to_all(a, PLANE, split_axis=0, concat_axis=0, tiled=True)]
  transfers between devices with their start and end apart: 35 -> 28, of which waited for: 15 -> 17; matrix products, arithmetic and copies ran while one was open for 2% -> 2% of each run, Pallas kernels for 56% -> 51%
where the time goes in v3:
time: 375 us; the launch traced here: 368 us
  Pallas kernels  228 us (61%)
  waiting for transfers between devices  74.5 us (20%)
  starting transfers between devices  40.2 us (11%)
  between operations  14.6 us (4%)
  local copies, waits for them, and re-layouts  6.89 us (2%)
  other arithmetic  3.77 us (1%)
    ppermute x16, waiting for transfers between devices, shift(): return lax.ppermute(a, axis, [(i, (i + k) % n) for i in range(n)])  61.5 us
    pallas_call x3, Pallas kernels, expert(): pl.pallas_call(functools.partial(expert_body, parts=parts, kept=len(earli...  38.4 us
    pallas_call x2, Pallas kernels, make_result(): pl.pallas_call(result_body, grid_spec=pltpu.PrefetchScalarGridSpec(num_sc...  31.6 us
    pallas_call x2, Pallas kernels, weight_share(): call(weight_share_body, flops=2 * rows * width * shares * size, moved=2 *...  29.3 us
    pallas_call x1, Pallas kernels, attend_back(): call(functools.partial(attend_back_body, block=min(256, length)), flops=3...  29.1 us
    ppermute x16, starting transfers between devices, shift(): return lax.ppermute(a, axis, [(i, (i + k) % n) for i in range(n)])  20.1 us
    pallas_call x1, Pallas kernels, attend(): call(functools.partial(attend_body, block=min(512, length)), flops=120000...  17.2 us
    all_to_all x3, starting transfers between devices, exchange_all(): return lax.all_to_all(a, PLANE, split_axis=0, concat_axis=0, tiled=True)  13.3 us
  transfers between devices with their start and end apart: 28, of which 17 were waited for; matrix products, arithmetic and copies ran while one was open for 2% of the time, Pallas kernels for 51%

profile of v3, /device:TPU:0, one launch (start us, length us, event | category | flops | bytes accessed | tf_op | source)
XLA Modules:
  0.0 367.8 jit_solution(14578452567403991452)
XLA Ops:
  7.2 7.1 %shard_map.161 = (s32[1,1024]{1,0:T(1,128)}, s32[1024,1]{1,0:T(8,128)}, bf16[8,256,768]{2,1,0:T(8,128)(2,1)}) custom-call(s32[1,1024]{1,0:T(1,128)} %ids_ref.1, s32[64,128]{1,0:T(8,128)} %bitcast.54, bf16[1024,768]{1,0:T(8,128)(2,1)} %bitcast.49), custom_call_target="tpu_custom_call" | custom-call | flops 3221225472 | bytes 4718592 | tf_op jit(solution)/shard_map/pallas_call | solution.py:108
  14.2 5.3 %all-to-all-start = ((bf16[8,256,768]{2,1,0:T(8,128)(2,1)}), bf16[8,256,768]{2,1,0:T(8,128)(2,1)S(1)}, u32[]{:S(2)}, u32[]{:S(2)}) async-start(bf16[8,256,768]{2,1,0:T(8,128)(2,1)} %get-tuple-element.83), calls=%async_computation | async-start | bytes 6291456 | tf_op jit(solution)/shard_map/all_to_all | solution.py:750
  20.9 8.4 %shard_map.162 = (bf16[1024,2304]{1,0:T(8,128)(2,1)}, bf16[1024,768]{1,0:T(8,128)(2,1)}) custom-call(bf16[1024,768]{1,0:T(8,128)(2,1)} %bitcast.51, f32[1,768]{1,0:T(1,128)} %reshape.52.gain_ref, bf16[768,2304]{1,0:T(8,128)(2,1)} %w_ref.7), custom_call_target="tpu_custom_call" | custom-call | flops 3623878656 | bytes 11403264 | tf_op jit(solution)/shard_map/pallas_call | solution.py:131
  29.4 17.2 %shard_map.163 = (bf16[1024,768]{1,0:T(8,128)(2,1)}, f32[6,2,1024]{2,1,0:T(2,128)}) custom-call(bf16[1024,2304]{1,0:T(8,128)(2,1)} %get-tuple-element.71.q_ref.k_ref.v_ref, bf16[1024,2304]{1,0:T(8,128)(2,1)} %get-tuple-element.71.q_ref.k_ref.v_ref, bf16[1024,2304]{1,0:T(8,128)(2,1)} %get-tuple-element.71.q_ref.k_ref.v_ref), custom_call_target="tpu_custom_call" | custom-call | flops 12000000000 | bytes 6291456 | tf_op jit(solution)/shard_map/pallas_call | solution.py:178
  46.5 8.4 %shard_map.164 = (f32[1024,768]{1,0:T(8,128)}, bf16[256,768]{1,0:T(8,128)(2,1)}, bf16[256,768]{1,0:T(8,128)(2,1)}, bf16[256,768]{1,0:T(8,128)(2,1)}, bf16[256,76...) custom-call(bf16[1024,768]{1,0:T(8,128)(2,1)} %get-tuple-element.72., ...), custom_call_target="tpu_custom_call" | custom-call | flops 4429185024 | bytes 11010048 | tf_op jit(solution)/shard_map/pallas_call | solution.py:260
  61.2 10.7 %shard_map.165 = (bf16[2048,3072]{1,0:T(8,128)(2,1)}, bf16[2048,3072]{1,0:T(8,128)(2,1)}, bf16[2048,768]{1,0:T(8,128)(2,1)}, bf16[2048,768]{1,0:T(8,128)(2,1)}) custom-call(s32[8]{0:T(128)} %stack.64.from_ref, bf16[256,768]{1,0:T(8,128)(2,1)} %get-tuple-element.81.refs_0_, bf16[256,768]{1,0:T(8,128)(2,1)} %collective-permute-done.4.refs_1_, ...), custom_call_target="tpu_custom_call" | custom-call | flops 4831838208 | bytes 18874368 | tf_op jit(solution)/shard_map/pallas_call | solution.py:307
  79.4 16.8 %shard_map.166 = (bf16[2048,3072]{1,0:T(8,128)(2,1)}, bf16[2048,3072]{1,0:T(8,128)(2,1)}, bf16[2048,768]{1,0:T(8,128)(2,1)}, bf16[2048,768]{1,0:T(8,128)(2,1)}) custom-call(s32[8]{0:T(128)} %stack.64.from_ref, bf16[256,768]{1,0:T(8,128)(2,1)} %copy-done.5, ...), custom_call_target="tpu_custom_call", output_to_operand_aliasing={{0}: (11, {}), {1}: (12, {}), {2}: (13, {}), {3}: (14, {})} | custom-call | flops 9663676416 | bytes 28311552 | tf_op jit(solution)/shard_map/pallas_call | solution.py:307
  97.8 10.8 %shard_map.167 = (bf16[2048,3072]{1,0:T(8,128)(2,1)}, bf16[2048,3072]{1,0:T(8,128)(2,1)}, bf16[2048,768]{1,0:T(8,128)(2,1)}, bf16[2048,768]{1,0:T(8,128)(2,1)}) custom-call(s32[8]{0:T(128)} %stack.64.from_ref, bf16[256,768]{1,0:T(8,128)(2,1)} %copy-done.6, ...), custom_call_target="tpu_custom_call", output_to_operand_aliasing={{0}: (7, {}), {1}: (8, {}), {2}: (9, {}), {3}: (10, {})} | custom-call | flops 4831838208 | bytes 18874368 | tf_op jit(solution)/shard_map/pallas_call | solution.py:307
  108.6 14.7 %shard_map.168 = bf16[768,3072]{1,0:T(8,128)(2,1)} custom-call(bf16[2048,768]{1,0:T(8,128)(2,1)} %get-tuple-element.97.g_ref, bf16[2048,3072]{1,0:T(8,128)(2,1)} %get-tuple-element.100.act_ref), custom_call_target="tpu_custom_call" | custom-call | flops 9663676416 | bytes 20447232 | tf_op jit(solution)/shard_map/pallas_call | solution.py:343
  124.0 15.8 %shard_map.169 = bf16[8,256,768]{2,1,0:T(8,128)(2,1)} custom-call(s32[4]{0:T(128)} %pad_add_fusion.chip_ref, bf16[2048,3072]{1,0:T(8,128)(2,1)} %get-tuple-element.98.act_ref, bf16[768,3072]{1,0:T(8,128)(2,1)} %bitcast.40), custom_call_target="tpu_custom_call" | custom-call | flops 9663676416 | bytes 20447232 | tf_op jit(solution)/shard_map/pallas_call | solution.py:374
  139.8 3.9 %all-to-all-start.1 = ((bf16[8,256,768]{2,1,0:T(8,128)(2,1)}), bf16[8,256,768]{2,1,0:T(8,128)(2,1)S(1)}, u32[]{:S(2)}, u32[]{:S(2)}) async-start(bf16[8,256,768]{2,1,0:T(8,128)(2,1)} %shard_map.169), calls=%async_computation.1 | async-start | bytes 6291456 | tf_op jit(solution)/shard_map/all_to_all | solution.py:750
  143.8 14.6 %shard_map.170 = bf16[768,3072]{1,0:T(8,128)(2,1)} custom-call(bf16[2048,768]{1,0:T(8,128)(2,1)} %get-tuple-element.99.g_ref, bf16[2048,3072]{1,0:T(8,128)(2,1)} %get-tuple-element.98.act_ref), custom_call_target="tpu_custom_call" | custom-call | flops 9663676416 | bytes 20447232 | tf_op jit(solution)/shard_map/pallas_call | solution.py:343
  158.4 15.8 %shard_map.171 = bf16[8,256,768]{2,1,0:T(8,128)(2,1)} custom-call(s32[4]{0:T(128)} %pad_add_fusion.chip_ref, bf16[2048,3072]{1,0:T(8,128)(2,1)} %get-tuple-element.100.act_ref, bf16[768,3072]{1,0:T(8,128)(2,1)} %bitcast.44), custom_call_target="tpu_custom_call" | custom-call | flops 9663676416 | bytes 20447232 | tf_op jit(solution)/shard_map/pallas_call | solution.py:374
  174.2 7.4 %all-to-all-done.1 = bf16[8,256,768]{2,1,0:T(8,128)(2,1)S(1)} async-done(((bf16[8,256,768]{2,1,0:T(8,128)(2,1)}), bf16[8,256,768]{2,1,0:T(8,128)(2,1)S(1)}, u32[]{:S(2)}, u32[]{:S(2)}) %all-to-all-start.1) | async-done | bytes 3145760 | tf_op jit(solution)/shard_map/all_to_all | solution.py:750
  183.3 4.1 %all-to-all-start.2 = ((bf16[8,256,768]{2,1,0:T(8,128)(2,1)}), bf16[8,256,768]{2,1,0:T(8,128)(2,1)S(1)}, u32[]{:S(2)}, u32[]{:S(2)}) async-start(bf16[8,256,768]{2,1,0:T(8,128)(2,1)} %shard_map.171), calls=%async_computation.2 | async-start | bytes 6291456 | tf_op jit(solution)/shard_map/all_to_all | solution.py:750
  187.3 12.9 %shard_map.172 = (f32[1024,768]{1,0:T(8,128)}, bf16[1024,768]{1,0:T(8,128)(2,1)}, bf16[1024,768]{1,0:T(8,128)(2,1)}, f32[1,768]{1,0:T(1,128)}) custom-call(s32[1024,1]{1,0:T(8,128)} %get-tuple-element.70.col_ref, f32[1024,768]{1,0:T(8,128)} %get-tuple-element.74.res_ref, bf16[1024,768]{1,0:T(8,128)(2,1)} %bitcast.50, f32[1,768]{1,0:T(1,128)} %reshape.53.gain_ref, ...), custom_call_target="tpu_custom_call" | custom-call | flops 5637144576 | bytes 15728640 | tf_op jit(solution)/shard_map/pallas_call | solution.py:422
  200.2 29.1 %shard_map.173.g_ref = bf16[3,1024,768]{2,1,0:T(8,128)(2,1)} custom-call(bf16[1024,2304]{1,0:T(8,128)(2,1)} %get-tuple-element.71.q_ref.k_ref.v_ref, bf16[1024,2304]{1,0:T(8,128)(2,1)} %get-tuple-element.71.q_ref.k_ref.v_ref, bf16[1024,2304]{1,0:T(8,128)(2,1)} %get-tuple-element.71.q_ref.k_ref.v_ref, bf16[1024,768]{1,0:T(8,128)(2,1)} %get-tuple-element.72.att_ref.o_ref, ...), custom_call_target="tpu_custom_call" | custom-call | flops 30000001024 | bytes 12582912 | tf_op jit(solution)/shard_map/pallas_call | solution.py:231
  229.3 11.4 %shard_map.174 = (bf16[768,1536]{1,0:T(8,128)(2,1)}, bf16[768,1536]{1,0:T(8,128)(2,1)}) custom-call(bf16[1024,768]{1,0:T(8,128)(2,1)} %get-tuple-element.102.normed_ref, bf16[3,1024,768]{2,1,0:T(8,128)(2,1)} %shard_map.173.g_ref, bf16[1024,768]{1,0:T(8,128)(2,1)} %get-tuple-element.72.att_ref.o_ref, bf16[1024,768]{1,0:T(8,128)(2,1)} %get-tuple-element.106.gattn_ref), custom_call_target="tpu_custom_call" | custom-call | flops 4831838208 | bytes 14155776 | tf_op jit(solution)/shard_map/pallas_call | solution.py:484
  241.2 9.9 %shard_map.175 = (f32[1024,768]{1,0:T(8,128)}, f32[1,768]{1,0:T(1,128)}) custom-call(bf16[1024,768]{1,0:T(8,128)(2,1)} %bitcast.53, f32[1,768]{1,0:T(1,128)} %reshape.52.gain_ref, bf16[768,2304]{1,0:T(8,128)(2,1)} %w_ref.7, bf16[3,1024,768]{2,1,0:T(8,128)(2,1)} %shard_map.173.g_ref, f32[1024,768]{1,0:T(8,128)} %get-tuple-element.110.gres_ref), custom_call_target="tpu_custom_call" | custom-call | flops 3623878656 | bytes 14155776 | tf_op jit(solution)/shard_map/pallas_call | solution.py:523
  251.1 4.7 %shard_map.176 = (bf16[192,1664]{1,0:T(8,128)(2,1)}, bf16[192,1664]{1,0:T(8,128)(2,1)}, bf16[192,1664]{1,0:T(8,128)(2,1)}, bf16[192,1664]{1,0:T(8,128)(2,1)}) custom-call(bf16[768,1536]{1,0:T(8,128)(2,1)} %get-tuple-element.107.keep_ref, bf16[768,1536]{1,0:T(8,128)(2,1)} %collective-permute-done.7.got_ref, f32[1,768]{1,0:T(1,128)} %get-tuple-element.113.one_ref, ...), custom_call_target="tpu_custom_call" | custom-call | bytes 7077888 | tf_op jit(solution)/shard_map/pallas_call | solution.py:634
  259.0 3.2 shard_map.178
  262.1 7.5 %shard_map.177 = bf16[1024,768]{1,0:T(8,128)(2,1)} custom-call(s32[1024,1]{1,0:T(8,128)} %get-tuple-element.70.col_ref, f32[1024,768]{1,0:T(8,128)} %get-tuple-element.74.res_ref, bf16[2048,768]{1,0:T(8,128)(2,1)} %bitcast.47), custom_call_target="tpu_custom_call" | custom-call | flops 3221225472 | bytes 7864320 | tf_op jit(solution)/shard_map/pallas_call | solution.py:450
  279.0 5.2 %collective-permute-done.10 = bf16[96,1664]{1,0:T(8,128)(2,1)S(1)} collective-permute-done((bf16[96,1664]{1,0:T(8,128)(2,1)S(1)}, bf16[96,1664]{1,0:T(8,128)(2,1)S(1)}, u32[]{:S(2)}, u32[]{:S(2)}) %collective-permute-start.10) | collective-permute-done | bytes 319520 | tf_op jit(solution)/shard_map/ppermute | solution.py:542
  286.8 3.8 %collective-permute-start.14 = (bf16[2,24,1664]{2,1,0:T(8,128)(2,1)S(1)}, bf16[2,24,1664]{2,1,0:T(8,128)(2,1)S(1)}, u32[]{:S(2)}, u32[]{:S(2)}) collective-permute-start(bf16[2,24,1664]{2,1,0:T(8,128)(2,1)S(1)} %get-tuple-element.138), channel_id=1, source_target_pairs={{0,24},{8,0},{16,8},{24,16},{1,25},{9,1},{17,9},{25,17},{2,26},{10... | collective-permute-start | bytes 479240 | tf_op jit(solution)/shard_map/ppermute | solution.py:542
  291.7 7.6 %collective-permute-done.14 = bf16[2,24,1664]{2,1,0:T(8,128)(2,1)S(1)} collective-permute-done((bf16[2,24,1664]{2,1,0:T(8,128)(2,1)S(1)}, bf16[2,24,1664]{2,1,0:T(8,128)(2,1)S(1)}, u32[]{:S(2)}, u32[]{:S(2)}) %collective-permute-start.14) | collective-permute-done | bytes 159776 | tf_op jit(solution)/shard_map/ppermute | solution.py:542
  299.3 12.1 %collective-permute-done.13 = bf16[2,24,1664]{2,1,0:T(8,128)(2,1)S(1)} collective-permute-done((bf16[2,24,1664]{2,1,0:T(8,128)(2,1)S(1)}, bf16[2,24,1664]{2,1,0:T(8,128)(2,1)S(1)}, u32[]{:S(2)}, u32[]{:S(2)}) %collective-permute-start.13) | collective-permute-done | bytes 159776 | tf_op jit(solution)/shard_map/ppermute | solution.py:542
  312.3 3.2 collective-permute-start.17
  315.5 5.1 %collective-permute-done.15 = bf16[2,24,1664]{2,1,0:T(8,128)(2,1)S(1)} collective-permute-done((bf16[2,24,1664]{2,1,0:T(8,128)(2,1)S(1)}, bf16[2,24,1664]{2,1,0:T(8,128)(2,1)S(1)}, u32[]{:S(2)}, u32[]{:S(2)}) %collective-permute-start.15) | collective-permute-done | bytes 159776 | tf_op jit(solution)/shard_map/ppermute | solution.py:542
  320.7 5.4 %collective-permute-done.16 = bf16[2,24,1664]{2,1,0:T(8,128)(2,1)S(1)} collective-permute-done((bf16[2,24,1664]{2,1,0:T(8,128)(2,1)S(1)}, bf16[2,24,1664]{2,1,0:T(8,128)(2,1)S(1)}, u32[]{:S(2)}, u32[]{:S(2)}) %collective-permute-start.16) | collective-permute-done | bytes 159776 | tf_op jit(solution)/shard_map/ppermute | solution.py:542
  337.9 11.0 %collective-permute-done.21 = bf16[192,1664]{1,0:T(8,128)(2,1)S(1)} collective-permute-done((bf16[192,1664]{1,0:T(8,128)(2,1)S(1)}, bf16[192,1664]{1,0:T(8,128)(2,1)S(1)}, u32[]{:S(2)}, u32[]{:S(2)}) %collective-permute-start.21) | collective-permute-done | bytes 639008 | tf_op jit(solution)/shard_map/ppermute | solution.py:542
  349.6 4.9 %collective-permute-done.22.other_ref = bf16[768,1664]{1,0:T(8,128)(2,1)} collective-permute-done((bf16[768,1664]{1,0:T(8,128)(2,1)S(1)}, bf16[768,1664]{1,0:T(8,128)(2,1)}, u32[]{:S(2)}, u32[]{:S(2)}) %collective-permute-start.22) | collective-permute-done | bytes 2555936 | tf_op jit(solution)/shard_map/ppermute | solution.py:542
  354.5 6.3 %shard_map.180 = (f32[768,2304]{1,0:T(8,128)}, f32[768,768]{1,0:T(8,128)}, f32[6,128]{1,0:T(8,128)}, f32[6,128]{1,0:T(8,128)}) custom-call(bf16[768,1664]{1,0:T(8,128)(2,1)} %copy-done.1, bf16[768,1664]{1,0:T(8,128)(2,1)} %collective-permute-done.22.other_ref), custom_call_target="tpu_custom_call" | custom-call | tf_op jit(solution)/shard_map/pallas_call | solution.py:702
  (96 shorter events, 48.9 us)
Async XLA Ops:
  14.2 5.5 %copy-start.8 = (f32[768]{0:T(1024)S(1)}, f32[768]{0:T(1024)}, u32[]{:S(2)}) copy-start(f32[768]{0:T(1024)} %param.13) | copy-start | bytes 9220
  14.2 6.1 %copy-start.9 = (f32[768]{0:T(1024)S(1)}, f32[768]{0:T(1024)}, u32[]{:S(2)}) copy-start(f32[768]{0:T(1024)} %param.16) | copy-start | bytes 9220
  14.2 45.3 %all-to-all-start = ((bf16[8,256,768]{2,1,0:T(8,128)(2,1)}), bf16[8,256,768]{2,1,0:T(8,128)(2,1)S(1)}, u32[]{:S(2)}, u32[]{:S(2)}) async-start(bf16[8,256,768]{2,1,0:T(8,128)(2,1)} %get-tuple-element.83), calls=%async_computation | async-start | bytes 6291456 | tf_op jit(solution)/shard_map/all_to_all | solution.py:750
  19.5 221.7 %reduce-scatter.3.cloned.1.call-start = ((), (), s32[]{:S(2)}) async-start(), calls=%async_computation.5 | async-start | bytes 5898240 | tf_op jit(solution)/shard_map/reduce_scatter | solution.py:783
  54.9 4.6 %collective-permute-start.4 = (bf16[256,768]{1,0:T(8,128)(2,1)}, bf16[256,768]{1,0:T(8,128)(2,1)}, u32[]{:S(2)}, u32[]{:S(2)}) collective-permute-start(bf16[256,768]{1,0:T(8,128)(2,1)} %get-tuple-element.82), channel_id=1, source_target_pairs={{0,1},{1,0},{2,3},{3,2},{4,5},{5,4},{6,7},{7,6},{8,9},{9,8},{10,11... | collective-permute-start | bytes 1179656 | tf_op jit(solution)/shard_map/ppermute | solution.py:581
  55.4 16.6 %collective-permute-start = (bf16[256,768]{1,0:T(8,128)(2,1)}, bf16[256,768]{1,0:T(8,128)(2,1)S(1)}, u32[]{:S(2)}, u32[]{:S(2)}) collective-permute-start(bf16[256,768]{1,0:T(8,128)(2,1)} %get-tuple-element.77), channel_id=1, source_target_pairs={{0,2},{1,3},{2,0},{3,1},{4,6},{5,7},{6,4},{7,5},{8,10},{9,11},{10,... | collective-permute-start | bytes 1179656 | tf_op jit(solution)/shard_map/ppermute | solution.py:581
  57.1 17.7 %collective-permute-start.1 = (bf16[256,768]{1,0:T(8,128)(2,1)}, bf16[256,768]{1,0:T(8,128)(2,1)}, u32[]{:S(2)}, u32[]{:S(2)}) collective-permute-start(bf16[256,768]{1,0:T(8,128)(2,1)} %get-tuple-element.78), channel_id=1, source_target_pairs={{0,3},{1,2},{2,1},{3,0},{4,7},{5,6},{6,5},{7,4},{8,11},{9,10},{10,... | collective-permute-start | bytes 1179656 | tf_op jit(solution)/shard_map/ppermute | solution.py:581
  57.1 17.7 %collective-permute-start.2 = (bf16[256,768]{1,0:T(8,128)(2,1)}, bf16[256,768]{1,0:T(8,128)(2,1)}, u32[]{:S(2)}, u32[]{:S(2)}) collective-permute-start(bf16[256,768]{1,0:T(8,128)(2,1)} %get-tuple-element.79), channel_id=1, source_target_pairs={{0,4},{1,5},{2,6},{3,7},{4,0},{5,1},{6,2},{7,3},{8,12},{9,13},{10,... | collective-permute-start | bytes 1179656 | tf_op jit(solution)/shard_map/ppermute | solution.py:581
  58.8 18.1 %collective-permute-start.3 = (bf16[256,768]{1,0:T(8,128)(2,1)}, bf16[256,768]{1,0:T(8,128)(2,1)}, u32[]{:S(2)}, u32[]{:S(2)}) collective-permute-start(bf16[256,768]{1,0:T(8,128)(2,1)} %get-tuple-element.80), channel_id=1, source_target_pairs={{0,5},{1,4},{2,7},{3,6},{4,1},{5,0},{6,3},{7,2},{8,13},{9,12},{10,... | collective-permute-start | bytes 1179656 | tf_op jit(solution)/shard_map/ppermute | solution.py:581
  72.0 7.4 %copy-start.5 = (bf16[256,768]{1,0:T(8,128)(2,1)}, bf16[256,768]{1,0:T(8,128)(2,1)S(1)}, u32[]{:S(2)}) copy-start(bf16[256,768]{1,0:T(8,128)(2,1)S(1)} %collective-permute-done.refs_0_) | copy-start | bytes 1179652
  76.8 19.4 %collective-permute-start.5 = (bf16[256,768]{1,0:T(8,128)(2,1)}, bf16[256,768]{1,0:T(8,128)(2,1)S(1)}, u32[]{:S(2)}, u32[]{:S(2)}) collective-permute-start(bf16[256,768]{1,0:T(8,128)(2,1)} %get-tuple-element.85), channel_id=1, source_target_pairs={{0,6},{1,7},{2,4},{3,5},{4,2},{5,3},{6,0},{7,1},{8,14},{9,15},{10,... | collective-permute-start | bytes 1179656 | tf_op jit(solution)/shard_map/ppermute | solution.py:581
  79.4 17.6 %collective-permute-start.6 = (bf16[256,768]{1,0:T(8,128)(2,1)}, bf16[256,768]{1,0:T(8,128)(2,1)S(1)}, u32[]{:S(2)}, u32[]{:S(2)}) collective-permute-start(bf16[256,768]{1,0:T(8,128)(2,1)} %get-tuple-element.86), channel_id=1, source_target_pairs={{0,7},{1,6},{2,5},{3,4},{4,3},{5,2},{6,1},{7,0},{8,15},{9,14},{10,... | collective-permute-start | bytes 1179656 | tf_op jit(solution)/shard_map/ppermute | solution.py:581
  139.8 41.8 %all-to-all-start.1 = ((bf16[8,256,768]{2,1,0:T(8,128)(2,1)}), bf16[8,256,768]{2,1,0:T(8,128)(2,1)S(1)}, u32[]{:S(2)}, u32[]{:S(2)}) async-start(bf16[8,256,768]{2,1,0:T(8,128)(2,1)} %shard_map.169), calls=%async_computation.1 | async-start | bytes 6291456 | tf_op jit(solution)/shard_map/all_to_all | solution.py:750
  143.7 186.1 %reduce-scatter.5.cloned.1.call-start = ((), (), s32[]{:S(2)}) async-start(), calls=%async_computation.6 | async-start | bytes 5898240 | tf_op jit(solution)/shard_map/reduce_scatter | solution.py:783
  183.3 75.7 %all-to-all-start.2 = ((bf16[8,256,768]{2,1,0:T(8,128)(2,1)}), bf16[8,256,768]{2,1,0:T(8,128)(2,1)S(1)}, u32[]{:S(2)}, u32[]{:S(2)}) async-start(bf16[8,256,768]{2,1,0:T(8,128)(2,1)} %shard_map.171), calls=%async_computation.2 | async-start | bytes 6291456 | tf_op jit(solution)/shard_map/all_to_all | solution.py:750
  240.8 10.3 %collective-permute-start.7 = (bf16[768,1536]{1,0:T(8,128)(2,1)}, bf16[768,1536]{1,0:T(8,128)(2,1)}, u32[]{:S(2)}, u32[]{:S(2)}) collective-permute-start(bf16[768,1536]{1,0:T(8,128)(2,1)} %get-tuple-element.108), channel_id=1, source_target_pairs={{0,1},{1,0},{2,3},{3,2},{4,5},{5,4},{6,7},{7,6},{8,9},{9,8},{10,11... | collective-permute-start | bytes 7077896 | tf_op jit(solution)/shard_map/ppermute | solution.py:542
  255.8 16.8 %collective-permute-start.8 = (bf16[192,1664]{1,0:T(8,128)(2,1)}, bf16[192,1664]{1,0:T(8,128)(2,1)}, u32[]{:S(2)}, u32[]{:S(2)}) collective-permute-start(bf16[192,1664]{1,0:T(8,128)(2,1)} %get-tuple-element.116), channel_id=1, source_target_pairs={{0,2},{2,0},{1,3},{3,1},{4,6},{6,4},{5,7},{7,5},{8,10},{10,8},{9,1... | collective-permute-start | bytes 1916936 | tf_op jit(solution)/shard_map/ppermute | solution.py:542
  257.5 16.6 %collective-permute-start.9 = (bf16[192,1664]{1,0:T(8,128)(2,1)}, bf16[192,1664]{1,0:T(8,128)(2,1)}, u32[]{:S(2)}, u32[]{:S(2)}) collective-permute-start(bf16[192,1664]{1,0:T(8,128)(2,1)} %get-tuple-element.118), channel_id=1, source_target_pairs={{0,4},{4,0},{1,5},{5,1},{2,6},{6,2},{3,7},{7,3},{8,12},{12,8},{9,1... | collective-permute-start | bytes 1916936 | tf_op jit(solution)/shard_map/ppermute | solution.py:542
  269.6 7.5 %copy-start.4 = (bf16[192,1664]{1,0:T(8,128)(2,1)S(1)}, bf16[192,1664]{1,0:T(8,128)(2,1)}, u32[]{:S(2)}) copy-start(bf16[192,1664]{1,0:T(8,128)(2,1)} %get-tuple-element.123) | copy-start | bytes 1916932
  275.5 8.6 %collective-permute-start.10 = (bf16[96,1664]{1,0:T(8,128)(2,1)S(1)}, bf16[96,1664]{1,0:T(8,128)(2,1)S(1)}, u32[]{:S(2)}, u32[]{:S(2)}) collective-permute-start(bf16[96,1664]{1,0:T(8,128)(2,1)S(1)} %constant_dynamic-slice_fusion.1), channel_id=1, source_target_pairs={{0,4},{4,0},{1,5},{5,1},{2,6},{6,2},{3,7},{7,3},{8,12},{12,8},{9,1... | collective-permute-start | bytes 958472 | tf_op jit(solution)/shard_map/ppermute | solution.py:542
  278.3 8.4 %collective-permute-start.11 = (bf16[96,1664]{1,0:T(8,128)(2,1)S(1)}, bf16[96,1664]{1,0:T(8,128)(2,1)S(1)}, u32[]{:S(2)}, u32[]{:S(2)}) collective-permute-start(bf16[96,1664]{1,0:T(8,128)(2,1)S(1)} %constant_dynamic-slice_fusion), channel_id=1, source_target_pairs={{0,2},{2,0},{1,3},{3,1},{4,6},{6,4},{5,7},{7,5},{8,10},{10,8},{9,1... | collective-permute-start | bytes 958472 | tf_op jit(solution)/shard_map/ppermute | solution.py:542
  286.8 12.5 %collective-permute-start.14 = (bf16[2,24,1664]{2,1,0:T(8,128)(2,1)S(1)}, bf16[2,24,1664]{2,1,0:T(8,128)(2,1)S(1)}, u32[]{:S(2)}, u32[]{:S(2)}) collective-permute-start(bf16[2,24,1664]{2,1,0:T(8,128)(2,1)S(1)} %get-tuple-element.138), channel_id=1, source_target_pairs={{0,24},{8,0},{16,8},{24,16},{1,25},{9,1},{17,9},{25,17},{2,26},{10... | collective-permute-start | bytes 479240 | tf_op jit(solution)/shard_map/ppermute | solution.py:542
  290.7 20.8 %collective-permute-start.13 = (bf16[2,24,1664]{2,1,0:T(8,128)(2,1)S(1)}, bf16[2,24,1664]{2,1,0:T(8,128)(2,1)S(1)}, u32[]{:S(2)}, u32[]{:S(2)}) collective-permute-start(bf16[2,24,1664]{2,1,0:T(8,128)(2,1)S(1)} %get-tuple-element.137), channel_id=1, source_target_pairs={{0,16},{8,24},{16,0},{24,8},{1,17},{9,25},{17,1},{25,9},{2,18},{10... | collective-permute-start | bytes 479240 | tf_op jit(solution)/shard_map/ppermute | solution.py:542
  290.7 20.8 %collective-permute-start.12 = (bf16[2,24,1664]{2,1,0:T(8,128)(2,1)S(1)}, bf16[2,24,1664]{2,1,0:T(8,128)(2,1)S(1)}, u32[]{:S(2)}, u32[]{:S(2)}) collective-permute-start(bf16[2,24,1664]{2,1,0:T(8,128)(2,1)S(1)} %get-tuple-element.136), channel_id=1, source_target_pairs={{0,8},{8,16},{16,24},{24,0},{1,9},{9,17},{17,25},{25,1},{2,10},{10... | collective-permute-start | bytes 479240 | tf_op jit(solution)/shard_map/ppermute | solution.py:542
  311.7 9.0 %collective-permute-start.15 = (bf16[2,24,1664]{2,1,0:T(8,128)(2,1)S(1)}, bf16[2,24,1664]{2,1,0:T(8,128)(2,1)S(1)}, u32[]{:S(2)}, u32[]{:S(2)}) collective-permute-start(bf16[2,24,1664]{2,1,0:T(8,128)(2,1)S(1)} %get-tuple-element.133), channel_id=1, source_target_pairs={{0,8},{8,16},{16,24},{24,0},{1,9},{9,17},{17,25},{25,1},{2,10},{10... | collective-permute-start | bytes 479240 | tf_op jit(solution)/shard_map/ppermute | solution.py:542
  311.7 14.3 %collective-permute-start.16 = (bf16[2,24,1664]{2,1,0:T(8,128)(2,1)S(1)}, bf16[2,24,1664]{2,1,0:T(8,128)(2,1)S(1)}, u32[]{:S(2)}, u32[]{:S(2)}) collective-permute-start(bf16[2,24,1664]{2,1,0:T(8,128)(2,1)S(1)} %get-tuple-element.133), channel_id=1, source_target_pairs={{0,16},{8,24},{16,0},{24,8},{1,17},{9,25},{17,1},{25,9},{2,18},{10... | collective-permute-start | bytes 479240 | tf_op jit(solution)/shard_map/ppermute | solution.py:542
  312.3 13.7 %collective-permute-start.17 = (bf16[2,24,1664]{2,1,0:T(8,128)(2,1)S(1)}, bf16[2,24,1664]{2,1,0:T(8,128)(2,1)S(1)}, u32[]{:S(2)}, u32[]{:S(2)}) collective-permute-start(bf16[2,24,1664]{2,1,0:T(8,128)(2,1)S(1)} %get-tuple-element.133), channel_id=1, source_target_pairs={{0,24},{8,0},{16,8},{24,16},{1,25},{9,1},{17,9},{25,17},{2,26},{10... | collective-permute-start | bytes 479240 | tf_op jit(solution)/shard_map/ppermute | solution.py:542
  326.2 7.8 %collective-permute-start.18 = (bf16[96,1664]{1,0:T(8,128)(2,1)S(1)}, bf16[96,1664]{1,0:T(8,128)(2,1)S(1)}, u32[]{:S(2)}, u32[]{:S(2)}) collective-permute-start(bf16[96,1664]{1,0:T(8,128)(2,1)S(1)} %get-tuple-element.135), channel_id=1, source_target_pairs={{0,4},{4,0},{1,5},{5,1},{2,6},{6,2},{3,7},{7,3},{8,12},{12,8},{9,1... | collective-permute-start | bytes 958472 | tf_op jit(solution)/shard_map/ppermute | solution.py:542
  328.0 7.4 %collective-permute-start.19 = (bf16[96,1664]{1,0:T(8,128)(2,1)S(1)}, bf16[96,1664]{1,0:T(8,128)(2,1)S(1)}, u32[]{:S(2)}, u32[]{:S(2)}) collective-permute-start(bf16[96,1664]{1,0:T(8,128)(2,1)S(1)} %get-tuple-element.134), channel_id=1, source_target_pairs={{0,2},{2,0},{1,3},{3,1},{4,6},{6,4},{5,7},{7,5},{8,10},{10,8},{9,1... | collective-permute-start | bytes 958472 | tf_op jit(solution)/shard_map/ppermute | solution.py:542
  335.5 13.4 %collective-permute-start.21 = (bf16[192,1664]{1,0:T(8,128)(2,1)S(1)}, bf16[192,1664]{1,0:T(8,128)(2,1)S(1)}, u32[]{:S(2)}, u32[]{:S(2)}) collective-permute-start(bf16[192,1664]{1,0:T(8,128)(2,1)S(1)} %constant_dynamic-update-slice_fusion.4), channel_id=1, source_target_pairs={{0,4},{4,0},{1,5},{5,1},{2,6},{6,2},{3,7},{7,3},{8,12},{12,8},{9,1... | collective-permute-start | bytes 1916936 | tf_op jit(solution)/shard_map/ppermute | solution.py:542
  335.9 13.3 %collective-permute-start.20 = (bf16[192,1664]{1,0:T(8,128)(2,1)S(1)}, bf16[192,1664]{1,0:T(8,128)(2,1)S(1)}, u32[]{:S(2)}, u32[]{:S(2)}) collective-permute-start(bf16[192,1664]{1,0:T(8,128)(2,1)S(1)} %constant_dynamic-update-slice_fusion.6), channel_id=1, source_target_pairs={{0,2},{2,0},{1,3},{3,1},{4,6},{6,4},{5,7},{7,5},{8,10},{10,8},{9,1... | collective-permute-start | bytes 1916936 | tf_op jit(solution)/shard_map/ppermute | solution.py:542
  349.5 5.0 %collective-permute-start.22 = (bf16[768,1664]{1,0:T(8,128)(2,1)S(1)}, bf16[768,1664]{1,0:T(8,128)(2,1)}, u32[]{:S(2)}, u32[]{:S(2)}) collective-permute-start(bf16[768,1664]{1,0:T(8,128)(2,1)S(1)} %pad_maximum_fusion.mine_ref), channel_id=1, source_target_pairs={{0,1},{1,0},{2,3},{3,2},{4,5},{5,4},{6,7},{7,6},{8,9},{9,8},{10,11... | collective-permute-start | bytes 7667720 | tf_op jit(solution)/shard_map/ppermute | solution.py:542
  (6 other events, 13.1 us)
Sparse Core Ops, SparseCore 0:
  123.4 86.7 reduce-scatter.2
  212.5 90.4 reduce-scatter.4

commit v4 on v3

--- a/solution.py
+++ b/solution.py
@@ -34,7 +34,7 @@
     return lax.broadcasted_iota(jnp.int32, shape, dim)
 
 
-def call(body, flops=0, moved=0, limit=60, **kw):
+def call(body, flops=0, moved=0, limit=62, **kw):
     return pl.pallas_call(
         body,
         compiler_params=pltpu.CompilerParams(vmem_limit_bytes=limit << 20),
@@ -117,49 +117,32 @@
     )(ids, table, cot)
 
 
-def packed_body(x_ref, gain_ref, w_ref, packed_ref, normed_ref):
-    x_hat, _ = norm_parts(x_ref[...].astype(F32))
-    normed = (x_hat * gain_ref[...]).astype(BF)
-    packed_ref[...] = nn(normed, w_ref[...]).astype(BF)
-    normed_ref[...] = normed
-
-
-def make_packed(x, gain, w):
-    count, width = x.shape
-    wide = w.shape[1]
-    block = 256
-    return call(
-        packed_body,
-        flops=2 * count * width * wide,
-        moved=2 * (count * (2 * width + wide) + width * wide),
-        grid=(count // block,),
-        in_specs=[
-            pl.BlockSpec((block, width), lambda i: (i, 0)),
-            whole(gain.shape),
-            whole(w.shape),
-        ],
-        out_specs=[
-            pl.BlockSpec((block, wide), lambda i: (i, 0)),
-            pl.BlockSpec((block, width), lambda i: (i, 0)),
-        ],
-        out_shape=[
-            jax.ShapeDtypeStruct((count, wide), BF),
-            jax.ShapeDtypeStruct((count, width), BF),
-        ],
-    )(x, gain, w)
-
-
-def attend_body(q_ref, k_ref, v_ref, o_ref, total_ref, *, block):
-    length = q_ref.shape[0]
+def attend_body(
+    x_ref, gain_ref, wq_ref, wk_ref, wv_ref, packed_ref, normed_ref, o_ref, total_ref, *, block
+):
+    length = x_ref.shape[0]
+
+    @pl.when(pl.program_id(0) == 0)
+    def _():
+        for begin in range(0, length, 256):
+            rows = slice(begin, begin + 256)
+            x_hat, _ = norm_parts(x_ref[rows, :].astype(F32))
+            normed_ref[rows, :] = (x_hat * gain_ref[...]).astype(BF)
+
+    w = jnp.concatenate([wq_ref[...], wk_ref[...], wv_ref[...]], 1)
+    packed = nn(normed_ref[...], w).astype(BF)
+    for part in range(3):
+        packed_ref[part] = packed[:, part * 128 : (part + 1) * 128]
     lane = iota((1, 128), 1)
-    v_turned = jnp.transpose(v_ref[...])
+    v_turned = jnp.transpose(packed_ref[2])
     allowed = iota((block, block), 0) <= iota((block, block), 1)
     for row in range(length // block):
         end = (row + 1) * block
         outs = []
         for head in range(2):
-            q = jnp.where(lane // 64 == head, q_ref[row * block : end, :] * BF(SCALE), BF(0))
-            s = nt(k_ref[:end, :], q)
+            q = packed_ref[0, row * block : end, :] * BF(SCALE)
+            q = jnp.where(lane // 64 == head, q, BF(0))
+            s = nt(packed_ref[1, :end, :], q)
             last = jnp.where(allowed, s[end - block :], NEGATIVE)
             s = jnp.concatenate([s[: end - block], last], 0) if row else last
             highest = jnp.max(s, 0, keepdims=True)
@@ -171,33 +154,44 @@
         o_ref[row * block : end, :] = jnp.transpose(jnp.concatenate(outs, 0)).astype(BF)
 
 
-def attend(packed):
-    length = packed.shape[0]
-    pairs = packed.shape[1] // 384
-    part = lambda o: pl.BlockSpec((length, 128), lambda i: (0, o * pairs + i))
+def attend(x, gain, w):
+    length, width = x.shape
+    pairs = width // 128
+    part = lambda o: pl.BlockSpec((width, 128), lambda i: (0, o * pairs + i))
     return call(
         functools.partial(attend_body, block=min(512, length)),
-        flops=1.2e10,
-        moved=2 * length * pairs * 512,
+        flops=1.2e10 + 6 * length * width * width,
+        moved=2 * (length * width * 6 + 3 * width * width),
         grid=(pairs,),
-        in_specs=[part(0), part(1), part(2)],
-        out_specs=[part(0), pl.BlockSpec((1, 2, length), lambda i: (i, 0, 0))],
+        in_specs=[whole(x.shape), whole(gain.shape), part(0), part(1), part(2)],
+        out_specs=[
+            pl.BlockSpec((3, length, 128), lambda i: (0, 0, i)),
+            whole(x.shape),
+            pl.BlockSpec((length, 128), lambda i: (0, i)),
+            pl.BlockSpec((1, 2, length), lambda i: (i, 0, 0)),
+        ],
         out_shape=[
-            jax.ShapeDtypeStruct((length, pairs * 128), BF),
+            jax.ShapeDtypeStruct((3, length, width), BF),
+            jax.ShapeDtypeStruct(x.shape, BF),
+            jax.ShapeDtypeStruct(x.shape, BF),
             jax.ShapeDtypeStruct((pairs, 2, length), F32),
         ],
-    )(packed, packed, packed)
+    )(x, gain, w, w, w)
 
 
 def attend_back_body(
-    q_ref, k_ref, v_ref, o_ref, up_ref, total_ref, out_ref, acc_ref, *, block
+    packed_ref, o_ref, up_ref, total_ref, out_ref, acc_ref, *, block
 ):
+    q_ref, k_ref, v_ref = (packed_ref.at[part] for part in range(3))
     length = q_ref.shape[0]
     count = length // block
     lane = iota((1, 128), 1)
     inner = jnp.transpose(o_ref[...].astype(F32) * up_ref[...].astype(F32))
     inner = [jnp.sum(inner[:64], 0, keepdims=True), jnp.sum(inner[64:], 0, keepdims=True)]
     allowed = iota((block, block), 0) <= iota((block, block), 1)
+    k_turned = jnp.transpose(k_ref[...] * BF(SCALE))
+    q_turned = jnp.transpose(q_ref[...] * BF(SCALE))
+    up_turned = jnp.transpose(up_ref[...])
     for part in range(count):
         begin, end = part * block, (part + 1) * block
         k = k_ref[begin:end, :]
@@ -212,35 +206,36 @@
             s = jnp.concatenate([first, s[:, block:]], 1) if part < count - 1 else first
             p = jnp.exp(s)
             ds = (p * (nt(v, up) - inner[head][:, begin:])).astype(BF)
-            dv.append(nn(p.astype(BF), up))
-            dk.append(nn(ds, q))
-            dq = tn(ds, jnp.where(mine, k * BF(SCALE), BF(0)))
-            if part == 0 and head == 0:
-                acc_ref[...] = dq
+            dv.append(nt(up_turned[head * 64 : head * 64 + 64, begin:], p.astype(BF)))
+            dk.append(nt(q_turned[head * 64 : head * 64 + 64, begin:], ds))
+            dq = nn(k_turned[head * 64 : head * 64 + 64, begin:end], ds)
+            if part == 0:
+                acc_ref[head * 64 : head * 64 + 64, :] = dq
             else:
-                acc_ref[begin:, :] += dq
-        out_ref[1, begin:end, :] = (dk[0] + dk[1]).astype(BF)
-        out_ref[2, begin:end, :] = (dv[0] + dv[1]).astype(BF)
-    out_ref[0] = acc_ref[...].astype(BF)
+                acc_ref[head * 64 : head * 64 + 64, begin:] += dq
+        out_ref[1, begin:end, :] = jnp.transpose(jnp.concatenate(dk, 0)).astype(BF)
+        out_ref[2, begin:end, :] = jnp.transpose(jnp.concatenate(dv, 0)).astype(BF)
+    out_ref[0] = jnp.transpose(acc_ref[...]).astype(BF)
 
 
 def attend_back(packed, attended, totals, upstream):
-    length = packed.shape[0]
-    pairs = packed.shape[1] // 384
-    part = lambda o: pl.BlockSpec((length, 128), lambda i: (0, o * pairs + i))
+    _, length, width = packed.shape
+    pairs = width // 128
+    part = pl.BlockSpec((length, 128), lambda i: (0, i))
+    three = pl.BlockSpec((3, length, 128), lambda i: (0, 0, i))
     return call(
         functools.partial(attend_back_body, block=min(256, length)),
         flops=3e10,
         moved=2 * length * pairs * 1024,
         grid=(pairs,),
         in_specs=[
-            part(0), part(1), part(2), part(0), part(0),
+            three, part, part,
             pl.BlockSpec((1, 2, length), lambda i: (i, 0, 0)),
         ],
-        out_specs=pl.BlockSpec((3, length, 128), lambda i: (0, 0, i)),
-        out_shape=jax.ShapeDtypeStruct((3, length, pairs * 128), BF),
-        scratch_shapes=[pltpu.VMEM((length, 128), F32)],
-    )(packed, packed, packed, attended, upstream, totals)
+        out_specs=three,
+        out_shape=jax.ShapeDtypeStruct(packed.shape, BF),
+        scratch_shapes=[pltpu.VMEM((128, length), F32)],
+    )(packed, attended, upstream, totals)
 
 
 def dispatch_body(att_ref, w_ref, x_ref, gain_ref, row_ref, res_ref, *rest):
@@ -318,7 +313,7 @@
         out_shape=[jax.ShapeDtypeStruct((every, units), BF)] * 2
         + [jax.ShapeDtypeStruct((every, width), BF)] * 2,
         input_output_aliases={1 + 2 * parts + 2 + i: i for i in range(len(earlier))},
-        compiler_params=pltpu.CompilerParams(vmem_limit_bytes=60 << 20),
+        compiler_params=pltpu.CompilerParams(vmem_limit_bytes=62 << 20),
         cost_estimate=pl.CostEstimate(
             flops=4 * tall * width * units,
             bytes_accessed=2 * (4 * tall * width + 2 * width * units + 2 * tall * units),
@@ -383,7 +378,7 @@
             out_specs=pl.BlockSpec((2, size, width), lambda i, s: (s[i], 0, 0)),
         ),
         out_shape=jax.ShapeDtypeStruct((experts, size, width), BF),
-        compiler_params=pltpu.CompilerParams(vmem_limit_bytes=60 << 20),
+        compiler_params=pltpu.CompilerParams(vmem_limit_bytes=62 << 20),
         cost_estimate=pl.CostEstimate(
             flops=2 * rows * units * width,
             bytes_accessed=2 * (rows * units + units * width + rows * width),
@@ -449,6 +444,7 @@
     row = pl.BlockSpec((block, width), lambda i: (i, 0))
     return call(
         collect_body,
+        limit=60,
         flops=2 * count * width * back.shape[0],
         moved=2 * width * (back.shape[0] + 3 * count),
         grid=(count // block,),
@@ -483,6 +479,7 @@
     out = jax.ShapeDtypeStruct((width, 2 * width), BF)
     return call(
         weight_grad_body,
+        limit=60,
         flops=8 * width * count * width,
         moved=2 * (6 * width * count + 4 * width * width),
         grid=(4,),
@@ -522,6 +519,7 @@
     row = pl.BlockSpec((block, width), lambda i: (i, 0))
     return call(
         grad_in_body,
+        limit=60,
         flops=6 * count * width * width,
         moved=2 * width * 9 * count,
         grid=(count // block,),
@@ -602,45 +600,41 @@
     return lax.optimization_barrier((value, first))[0]
 
 
-def split_body(keep_ref, got_ref, one_ref, two_ref, *out_refs, ways):
-    wide = keep_ref.shape[1]
+def split_body(keep_ref, got_ref, *out_refs, ways):
     half = keep_ref.shape[0] // 2
-    turned = jnp.transpose(
-        jnp.concatenate([one_ref[...], two_ref[...]] + [jnp.zeros_like(one_ref[...])] * 6, 0)
-    )
-    turned = jnp.concatenate([turned, jnp.zeros((turned.shape[0], 120), F32)], 1)
     at = 0
     for begin, axis, count in ((0, "x", ways[1]), (half, "y", ways[0])):
         size = half // count
         me = lax.axis_index(axis)
         for k in range(count):
-            piece = lax.rem(me + k, count)
-            rows = pl.ds(pl.multiple_of(begin + piece * size, 8), size)
-            out = out_refs[at]
-            out[:, :wide] = (keep_ref[rows, :].astype(F32) + got_ref[rows, :].astype(F32)).astype(BF)
-            for other in range(count):
-
-                @pl.when(piece == other)
-                def _():
-                    begin_here = begin + other * size
-                    out[:, wide:] = turned[begin_here : begin_here + size].astype(BF)
-
+            rows = pl.ds(pl.multiple_of(begin + lax.rem(me + k, count) * size, 8), size)
+            out_refs[at][...] = (
+                keep_ref[rows, :].astype(F32) + got_ref[rows, :].astype(F32)
+            ).astype(BF)
             at += 1
 
 
-def split(keep, got, one, two, ways):
+def split(keep, got, ways):
     rows, wide = keep.shape
     sizes = [rows // 2 // ways[1]] * ways[1] + [rows // 2 // ways[0]] * ways[0]
     outs = call(
         functools.partial(split_body, ways=ways),
+        limit=20,
         moved=6 * rows * wide,
-        out_shape=[jax.ShapeDtypeStruct((size, wide + 128), BF) for size in sizes],
-    )(keep, got, one, two)
+        out_shape=[jax.ShapeDtypeStruct((size, wide), BF) for size in sizes],
+    )(keep, got)
     return outs[: ways[1]], outs[ways[1] :]
 
 
 def add_up(parts, axis):
     return [parts[0]] + [shift(a, axis, k) for k, a in enumerate(parts) if k]
+
+
+def sum_over(a, axis):
+    out = a
+    for k in range(1, lax.axis_size(axis)):
+        out = out + shift(a, axis, k)
+    return out
 
 
 def total(parts):
@@ -670,45 +664,36 @@
     return mine, shift(mine, "core", 1)
 
 
-def unpack_body(mine_ref, other_ref, qkv_ref, proj_ref, one_ref, two_ref):
+def unpack_body(mine_ref, other_ref, qkv_ref, proj_ref):
     width = proj_ref.shape[1]
     first = lax.axis_index("core") == 0
-    gains = mine_ref[:, 2 * width :].astype(F32) + other_ref[:, 2 * width :].astype(F32)
-    gains = jnp.transpose(gains)
-    lines = gains.shape[1] // 128
-    for part in range(lines):
-        line = pl.ds(pl.program_id(0) * lines + part, 1)
-        columns = slice(part * 128, (part + 1) * 128)
-        one_ref[line, :] = gains[:1, columns]
-        two_ref[line, :] = gains[1:2, columns]
 
     @pl.when(first)
     def _():
-        qkv_ref[:, : 2 * width] = mine_ref[:, : 2 * width].astype(F32)
+        qkv_ref[:, : 2 * width] = mine_ref[...].astype(F32)
         qkv_ref[:, 2 * width :] = other_ref[:, :width].astype(F32)
-        proj_ref[...] = other_ref[:, width : 2 * width].astype(F32)
+        proj_ref[...] = other_ref[:, width:].astype(F32)
 
     @pl.when(jnp.logical_not(first))
     def _():
-        qkv_ref[:, : 2 * width] = other_ref[:, : 2 * width].astype(F32)
+        qkv_ref[:, : 2 * width] = other_ref[...].astype(F32)
         qkv_ref[:, 2 * width :] = mine_ref[:, :width].astype(F32)
-        proj_ref[...] = mine_ref[:, width : 2 * width].astype(F32)
+        proj_ref[...] = mine_ref[:, width:].astype(F32)
 
 
 def unpack(mine, other):
     width = mine.shape[0]
-    block = min(256, width)
+    block = min(192, width)
     row = lambda wide: pl.BlockSpec((block, wide), lambda i: (i, 0))
     return call(
         unpack_body,
+        limit=60,
         grid=(width // block,),
-        in_specs=[row(mine.shape[1])] * 2,
-        out_specs=[row(3 * width), row(width)] + [whole((width // 128, 128))] * 2,
+        in_specs=[row(2 * width)] * 2,
+        out_specs=[row(3 * width), row(width)],
         out_shape=[
             jax.ShapeDtypeStruct((width, 3 * width), F32),
             jax.ShapeDtypeStruct((width, width), F32),
-            jax.ShapeDtypeStruct((width // 128, 128), F32),
-            jax.ShapeDtypeStruct((width // 128, 128), F32),
         ],
     )(mine, other)
 
@@ -726,6 +711,7 @@
     block = lambda columns: pl.BlockSpec((1, rows // 2, columns), lambda i: (0, i, 0))
     return call(
         widen_body,
+        limit=60,
         moved=6 * rows * wide,
         grid=(2,),
         in_specs=[block(a.shape[2]) for a in parts],
@@ -756,8 +742,7 @@
         token_ids.reshape(1, count), hash_table.reshape(-1, 128), cot, sides, capacity
     )
     flat_grad = exchange_all(grad_send)
-    packed, normed = make_packed(x, first_gain, w_qkv)
-    attended, totals = attend(packed)
+    packed, normed, attended, totals = attend(x, first_gain, w_qkv)
     residual, *outgoing = dispatch(attended, w_proj, x, second_gain, row, experts, capacity)
     outgoing = dict(enumerate(outgoing))
     far = {i: outgoing.pop(i) for i in range(experts - 2, experts)}
@@ -797,27 +782,36 @@
     grad_packed = attend_back(packed, attended, totals, grad_attended)
     keep, send = weight_grads(normed, grad_packed, attended, grad_attn)
     got = shift(send, "core", 1)
+    grad_w_out = widen(after(grad_w_out, keep))
+    top, low = split(keep, after(got, grad_w_out, returned), sides)
     grad_tokens, grad_gain_one = grad_in(
-        x, first_gain, w_qkv, after(grad_packed, keep, grad_w_out), grad_residual
+        x, first_gain, w_qkv, after(grad_packed, top, low), grad_residual
     )
-    top, low = split(keep, after(got, grad_tokens), grad_gain_one, grad_gain_two, sides)
-    grad_w_out = widen(after(grad_w_out, top, low))
-    outputs = collect(after(returned.reshape(-1, width), top, low), col, residual)
-    top, low = after((add_up(top, "x"), add_up(low, "y")), outputs, grad_w_out)
-    top = add_up(pieces_of(total(top), "y", 0), "y")
-    low = add_up(pieces_of(total(low), "x", 0), "x")
+    small = jnp.concatenate([grad_gain_one, grad_gain_two], 0).reshape(-1, 128)
+    small = sum_over(small, "core")
+    top, low = after((add_up(top, "x"), add_up(low, "y")), grad_tokens)
+    top, low = pieces_of(total(top), "y", 0), pieces_of(total(low), "x", 0)
+    small = sum_over(sum_over(small, "x"), "y")
+    top, low = add_up(top, "y"), add_up(low, "x")
     both = jnp.stack([total(top), total(low)])
-    both = gather_planes(add_up(pieces_of(both, "dp", 1), "dp"))
+    pad = both.shape[0] * both.shape[1] - small.shape[0]
+    small = jnp.concatenate([small, jnp.zeros((pad, 128), F32)], 0).astype(BF)
+    both = jnp.concatenate([both, small.reshape(both.shape[:2] + (128,))], 2)
+    pieces = pieces_of(both, "dp", 1)
+    outputs = collect(after(returned.reshape(-1, width), pieces), col, residual)
+    both = gather_planes(after(add_up(pieces, "dp"), outputs))
+    small = both[:, :, 2 * width :].reshape(-1, 128)[: 2 * width // 128]
+    gains = small.astype(F32).reshape(2, width)
     grad_w_in = widen(after(grad_w_in, both))
-    mine, other = gather_plane(both, (grad_w_in,))
-    grad_qkv, grad_proj, one, two = unpack(mine, other)
+    mine, other = gather_plane(both[:, :, : 2 * width], (grad_w_in,))
+    grad_qkv, grad_proj = unpack(mine, other)
     return (
         outputs.reshape(tokens.shape),
         grad_tokens.reshape(tokens.shape),
-        one.reshape(width),
+        gains[0],
         grad_qkv,
         grad_proj,
-        two.reshape(width),
+        gains[1],
         grad_w_in,
         grad_w_out,
     )

time: 375 us -> 369 us (0.984)
  starting transfers between devices: 40.2 us -> 51.4 us
  Pallas kernels: 228 us -> 222 us
  waiting for transfers between devices: 74.5 us -> 69.8 us
    pallas_call x8 -> x7, Pallas kernels: 53.9 us -> 43.7 us  [the longest x1 11.4 us: weight_grads(): call(weight_grad_body, limit=60, flops=8 * width * count * width, moved=2...]
    ppermute x16 -> x19, starting transfers between devices: 20.1 us -> 30 us  [shift(): return lax.ppermute(a, axis, [(i, (i + k) % n) for i in range(n)])]
    pallas_call x1, Pallas kernels: 17.2 us -> 24.3 us  [attend(): call(functools.partial(attend_body, block=min(512, length)), flops=120000...]
    ppermute x16 -> x19, waiting for transfers between devices: 61.5 us -> 56.4 us  [shift(): return lax.ppermute(a, axis, [(i, (i + k) % n) for i in range(n)])]
  transfers between devices with their start and end apart: 28 -> 31, of which waited for: 17 -> 18; matrix products, arithmetic and copies ran while one was open for 2% -> 1% of each run, Pallas kernels for 51% -> 50%
where the time goes in v4:
time: 369 us; the launch traced here: 364 us
  Pallas kernels  222 us (60%)
  waiting for transfers between devices  69.8 us (19%)
  starting transfers between devices  51.4 us (14%)
  between operations  14.6 us (4%)
  local copies, waits for them, and re-layouts  4.17 us (1%)
    ppermute x19, waiting for transfers between devices, shift(): return lax.ppermute(a, axis, [(i, (i + k) % n) for i in range(n)])  56.4 us
    pallas_call x3, Pallas kernels, expert(): pl.pallas_call(functools.partial(expert_body, parts=parts, kept=len(earli...  38.6 us
    pallas_call x2, Pallas kernels, make_result(): pl.pallas_call(result_body, grid_spec=pltpu.PrefetchScalarGridSpec(num_sc...  31.6 us
    ppermute x19, starting transfers between devices, shift(): return lax.ppermute(a, axis, [(i, (i + k) % n) for i in range(n)])  30 us
    pallas_call x2, Pallas kernels, weight_share(): call(weight_share_body, flops=2 * rows * width * shares * size, moved=2 *...  29.4 us
    pallas_call x1, Pallas kernels, attend_back(): call(functools.partial(attend_back_body, block=min(256, length)), flops=3...  25.6 us
    pallas_call x1, Pallas kernels, attend(): call(functools.partial(attend_body, block=min(512, length)), flops=120000...  24.3 us
    all_to_all x3, starting transfers between devices, exchange_all(): return lax.all_to_all(a, PLANE, split_axis=0, concat_axis=0, tiled=True)  14.4 us
  transfers between devices with their start and end apart: 31, of which 18 were waited for; matrix products, arithmetic and copies ran while one was open for 1% of the time, Pallas kernels for 50%

profile of v4, /device:TPU:0, one launch (start us, length us, event | category | flops | bytes accessed | tf_op | source)
XLA Modules:
  0.0 363.8 jit_solution(1610794125601585369)
XLA Ops:
  7.2 7.1 %shard_map.161 = (s32[1,1024]{1,0:T(1,128)}, s32[1024,1]{1,0:T(8,128)}, bf16[8,256,768]{2,1,0:T(8,128)(2,1)}) custom-call(s32[1,1024]{1,0:T(1,128)} %ids_ref.1, s32[64,128]{1,0:T(8,128)} %bitcast.58, bf16[1024,768]{1,0:T(8,128)(2,1)} %bitcast.53), custom_call_target="tpu_custom_call" | custom-call | flops 3221225472 | bytes 4718592 | tf_op jit(solution)/shard_map/pallas_call | solution.py:108
  14.2 5.3 %all-to-all-start = ((bf16[8,256,768]{2,1,0:T(8,128)(2,1)}), bf16[8,256,768]{2,1,0:T(8,128)(2,1)}, u32[]{:S(2)}, u32[]{:S(2)}) async-start(bf16[8,256,768]{2,1,0:T(8,128)(2,1)} %get-tuple-element.84), calls=%async_computation | async-start | bytes 6291456 | tf_op jit(solution)/shard_map/all_to_all | solution.py:736
  20.9 24.3 %shard_map.162 = (bf16[3,1024,768]{2,1,0:T(8,128)(2,1)}, bf16[1024,768]{1,0:T(8,128)(2,1)}, bf16[1024,768]{1,0:T(8,128)(2,1)}, f32[6,2,1024]{2,1,0:T(2,128)}) custom-call(bf16[1024,768]{1,0:T(8,128)(2,1)} %bitcast.55, f32[1,768]{1,0:T(1,128)} %reshape.60.gain_ref, bf16[768,2304]{1,0:T(8,128)(2,1)} %w_ref.5, bf16[768,2304]{1,0:T(8,128)(2,1)} %w_ref.5, ...), custom_call_target="tpu_custom_call" | custom-call | flops 15623878656 | bytes 12976128 | tf_op jit(solution)/shard_map/pallas_call | solution.py:161
  45.3 8.4 %shard_map.163 = (f32[1024,768]{1,0:T(8,128)}, bf16[256,768]{1,0:T(8,128)(2,1)}, bf16[256,768]{1,0:T(8,128)(2,1)}, bf16[256,768]{1,0:T(8,128)(2,1)}, bf16[256,76...) custom-call(bf16[1024,768]{1,0:T(8,128)(2,1)} %get-tuple-element.73., ...), custom_call_target="tpu_custom_call" | custom-call | flops 4429185024 | bytes 11010048 | tf_op jit(solution)/shard_map/pallas_call | solution.py:255
  59.1 10.8 %shard_map.164 = (bf16[2048,3072]{1,0:T(8,128)(2,1)}, bf16[2048,3072]{1,0:T(8,128)(2,1)}, bf16[2048,768]{1,0:T(8,128)(2,1)}, bf16[2048,768]{1,0:T(8,128)(2,1)}) custom-call(s32[8]{0:T(128)} %stack.64.from_ref, bf16[256,768]{1,0:T(8,128)(2,1)} %get-tuple-element.82.refs_0_, bf16[256,768]{1,0:T(8,128)(2,1)} %copy-done.10, ...), custom_call_target="tpu_custom_call" | custom-call | flops 4831838208 | bytes 18874368 | tf_op jit(solution)/shard_map/pallas_call | solution.py:302
  69.9 3.9 %collective-permute-done.1.refs_1_ = bf16[256,768]{1,0:T(8,128)(2,1)S(1)} collective-permute-done((bf16[256,768]{1,0:T(8,128)(2,1)}, bf16[256,768]{1,0:T(8,128)(2,1)S(1)}, u32[]{:S(2)}, u32[]{:S(2)}) %collective-permute-start.1) | collective-permute-done | bytes 393248 | tf_op jit(solution)/shard_map/ppermute | solution.py:579
  78.1 17.1 %shard_map.165 = (bf16[2048,3072]{1,0:T(8,128)(2,1)}, bf16[2048,3072]{1,0:T(8,128)(2,1)}, bf16[2048,768]{1,0:T(8,128)(2,1)}, bf16[2048,768]{1,0:T(8,128)(2,1)}) custom-call(s32[8]{0:T(128)} %stack.64.from_ref, bf16[256,768]{1,0:T(8,128)(2,1)} %copy-done.2, ...), custom_call_target="tpu_custom_call", output_to_operand_aliasing={{0}: (11, {}), {1}: (12, {}), {2}: (13, {}), {3}: (14, {})} | custom-call | flops 9663676416 | bytes 28311552 | tf_op jit(solution)/shard_map/pallas_call | solution.py:302
  96.0 10.8 %shard_map.166 = (bf16[2048,3072]{1,0:T(8,128)(2,1)}, bf16[2048,3072]{1,0:T(8,128)(2,1)}, bf16[2048,768]{1,0:T(8,128)(2,1)}, bf16[2048,768]{1,0:T(8,128)(2,1)}) custom-call(s32[8]{0:T(128)} %stack.64.from_ref, bf16[256,768]{1,0:T(8,128)(2,1)} %copy-done.6, ...), custom_call_target="tpu_custom_call", output_to_operand_aliasing={{0}: (7, {}), {1}: (8, {}), {2}: (9, {}), {3}: (10, {})} | custom-call | flops 4831838208 | bytes 18874368 | tf_op jit(solution)/shard_map/pallas_call | solution.py:302
  106.8 14.6 %shard_map.167 = bf16[768,3072]{1,0:T(8,128)(2,1)} custom-call(bf16[2048,768]{1,0:T(8,128)(2,1)} %get-tuple-element.98.g_ref, bf16[2048,3072]{1,0:T(8,128)(2,1)} %get-tuple-element.101.act_ref), custom_call_target="tpu_custom_call" | custom-call | flops 9663676416 | bytes 20447232 | tf_op jit(solution)/shard_map/pallas_call | solution.py:338
  122.1 15.8 %shard_map.168 = bf16[8,256,768]{2,1,0:T(8,128)(2,1)} custom-call(s32[4]{0:T(128)} %pad_add_fusion.chip_ref, bf16[2048,3072]{1,0:T(8,128)(2,1)} %get-tuple-element.99.act_ref, bf16[768,3072]{1,0:T(8,128)(2,1)} %bitcast.44), custom_call_target="tpu_custom_call" | custom-call | flops 9663676416 | bytes 20447232 | tf_op jit(solution)/shard_map/pallas_call | solution.py:369
  137.9 4.5 %all-to-all-start.1 = ((bf16[8,256,768]{2,1,0:T(8,128)(2,1)}), bf16[8,256,768]{2,1,0:T(8,128)(2,1)}, u32[]{:S(2)}, u32[]{:S(2)}) async-start(bf16[8,256,768]{2,1,0:T(8,128)(2,1)} %shard_map.168), calls=%async_computation.1 | async-start | bytes 6291456 | tf_op jit(solution)/shard_map/all_to_all | solution.py:736
  142.4 14.8 %shard_map.169 = bf16[768,3072]{1,0:T(8,128)(2,1)} custom-call(bf16[2048,768]{1,0:T(8,128)(2,1)} %get-tuple-element.100.g_ref, bf16[2048,3072]{1,0:T(8,128)(2,1)} %get-tuple-element.99.act_ref), custom_call_target="tpu_custom_call" | custom-call | flops 9663676416 | bytes 20447232 | tf_op jit(solution)/shard_map/pallas_call | solution.py:338
  157.3 15.8 %shard_map.170 = bf16[8,256,768]{2,1,0:T(8,128)(2,1)} custom-call(s32[4]{0:T(128)} %pad_add_fusion.chip_ref, bf16[2048,3072]{1,0:T(8,128)(2,1)} %get-tuple-element.101.act_ref, bf16[768,3072]{1,0:T(8,128)(2,1)} %bitcast.48), custom_call_target="tpu_custom_call" | custom-call | flops 9663676416 | bytes 20447232 | tf_op jit(solution)/shard_map/pallas_call | solution.py:369
  173.1 7.2 %all-to-all-done.1 = bf16[8,256,768]{2,1,0:T(8,128)(2,1)} async-done(((bf16[8,256,768]{2,1,0:T(8,128)(2,1)}), bf16[8,256,768]{2,1,0:T(8,128)(2,1)}, u32[]{:S(2)}, u32[]{:S(2)}) %all-to-all-start.1) | async-done | bytes 3145760 | tf_op jit(solution)/shard_map/all_to_all | solution.py:736
  180.3 4.6 %all-to-all-start.2 = ((bf16[8,256,768]{2,1,0:T(8,128)(2,1)}), bf16[8,256,768]{2,1,0:T(8,128)(2,1)}, u32[]{:S(2)}, u32[]{:S(2)}) async-start(bf16[8,256,768]{2,1,0:T(8,128)(2,1)} %shard_map.170), calls=%async_computation.2 | async-start | bytes 6291456 | tf_op jit(solution)/shard_map/all_to_all | solution.py:736
  184.9 12.9 %shard_map.171 = (f32[1024,768]{1,0:T(8,128)}, bf16[1024,768]{1,0:T(8,128)(2,1)}, bf16[1024,768]{1,0:T(8,128)(2,1)}, f32[1,768]{1,0:T(1,128)}) custom-call(s32[1024,1]{1,0:T(8,128)} %get-tuple-element.72.col_ref, f32[1024,768]{1,0:T(8,128)} %get-tuple-element.75.res_ref, bf16[1024,768]{1,0:T(8,128)(2,1)} %bitcast.54, f32[1,768]{1,0:T(1,128)} %reshape.61.gain_ref, ...), custom_call_target="tpu_custom_call" | custom-call | flops 5637144576 | bytes 15728640 | tf_op jit(solution)/shard_map/pallas_call | solution.py:417
  197.8 25.6 %shard_map.172.g_ref = bf16[3,1024,768]{2,1,0:T(8,128)(2,1)} custom-call(bf16[3,1024,768]{2,1,0:T(8,128)(2,1)} %get-tuple-element.104.packed_ref, bf16[1024,768]{1,0:T(8,128)(2,1)} %get-tuple-element.73.att_ref.o_ref, bf16[1024,768]{1,0:T(8,128)(2,1)} %get-tuple-element.106.up_ref, f32[6,2,1024]{2,1,0:T(2,128)} %get-tuple-element.107.total_ref), custom_call_target="tpu_custom_call" | custom-call | flops 30000001024 | bytes 12582912 | tf_op jit(solution)/shard_map/pallas_call | solution.py:226
  223.5 11.4 %shard_map.173 = (bf16[768,1536]{1,0:T(8,128)(2,1)}, bf16[768,1536]{1,0:T(8,128)(2,1)}) custom-call(bf16[1024,768]{1,0:T(8,128)(2,1)} %get-tuple-element.103.normed_ref, bf16[3,1024,768]{2,1,0:T(8,128)(2,1)} %shard_map.172.g_ref, bf16[1024,768]{1,0:T(8,128)(2,1)} %get-tuple-element.73.att_ref.o_ref, bf16[1024,768]{1,0:T(8,128)(2,1)} %get-tuple-element.108.gattn_ref), custom_call_target="tpu_custom_call" | custom-call | flops 4831838208 | bytes 14155776 | tf_op jit(solution)/shard_map/pallas_call | solution.py:480
  239.8 3.2 shard_map.175
  246.4 9.8 %shard_map.176 = (f32[1024,768]{1,0:T(8,128)}, f32[1,768]{1,0:T(1,128)}) custom-call(bf16[1024,768]{1,0:T(8,128)(2,1)} %bitcast.57, f32[1,768]{1,0:T(1,128)} %reshape.60.gain_ref, bf16[768,2304]{1,0:T(8,128)(2,1)} %w_ref.5, bf16[3,1024,768]{2,1,0:T(8,128)(2,1)} %shard_map.172.g_ref, f32[1024,768]{1,0:T(8,128)} %get-tuple-element.118.gres_ref), custom_call_target="tpu_custom_call" | custom-call | flops 3623878656 | bytes 14155776 | tf_op jit(solution)/shard_map/pallas_call | solution.py:520
  258.7 3.1 collective-permute-done.13
  262.4 3.1 collective-permute-done.14
  266.8 6.6 %collective-permute-done.11 = bf16[96,1536]{1,0:T(8,128)(2,1)S(1)} collective-permute-done((bf16[96,1536]{1,0:T(8,128)(2,1)S(1)}, bf16[96,1536]{1,0:T(8,128)(2,1)S(1)}, u32[]{:S(2)}, u32[]{:S(2)}) %collective-permute-start.11) | collective-permute-done | bytes 294944 | tf_op jit(solution)/shard_map/ppermute | solution.py:540
  280.2 7.4 %shard_map.177 = bf16[1024,768]{1,0:T(8,128)(2,1)} custom-call(s32[1024,1]{1,0:T(8,128)} %get-tuple-element.72.col_ref, f32[1024,768]{1,0:T(8,128)} %get-tuple-element.75.res_ref, bf16[2048,768]{1,0:T(8,128)(2,1)} %bitcast.18.back_ref), custom_call_target="tpu_custom_call" | custom-call | flops 3221225472 | bytes 7864320 | tf_op jit(solution)/shard_map/pallas_call | solution.py:445
  287.6 11.4 %collective-permute-done.16 = bf16[2,24,1664]{2,1,0:T(8,128)(2,1)S(1)} collective-permute-done((bf16[2,24,1664]{2,1,0:T(8,128)(2,1)S(1)}, bf16[2,24,1664]{2,1,0:T(8,128)(2,1)S(1)}, u32[]{:S(2)}, u32[]{:S(2)}) %collective-permute-start.16) | collective-permute-done | bytes 159776 | tf_op jit(solution)/shard_map/ppermute | solution.py:540
  299.1 10.0 %collective-permute-start.18 = (bf16[2,24,1664]{2,1,0:T(8,128)(2,1)S(1)}, bf16[2,24,1664]{2,1,0:T(8,128)(2,1)S(1)}, u32[]{:S(2)}, u32[]{:S(2)}) collective-permute-start(bf16[2,24,1664]{2,1,0:T(8,128)(2,1)S(1)} %get-tuple-element.137), channel_id=1, source_target_pairs={{0,8},{8,16},{16,24},{24,0},{1,9},{9,17},{17,25},{25,1},{2,10},{10... | collective-permute-start | bytes 479240 | tf_op jit(solution)/shard_map/ppermute | solution.py:540
  311.8 4.6 %collective-permute-done.18 = bf16[2,24,1664]{2,1,0:T(8,128)(2,1)S(1)} collective-permute-done((bf16[2,24,1664]{2,1,0:T(8,128)(2,1)S(1)}, bf16[2,24,1664]{2,1,0:T(8,128)(2,1)S(1)}, u32[]{:S(2)}, u32[]{:S(2)}) %collective-permute-start.18) | collective-permute-done | bytes 159776 | tf_op jit(solution)/shard_map/ppermute | solution.py:540
  316.4 4.0 %collective-permute-done.19 = bf16[2,24,1664]{2,1,0:T(8,128)(2,1)S(1)} collective-permute-done((bf16[2,24,1664]{2,1,0:T(8,128)(2,1)S(1)}, bf16[2,24,1664]{2,1,0:T(8,128)(2,1)S(1)}, u32[]{:S(2)}, u32[]{:S(2)}) %collective-permute-start.19) | collective-permute-done | bytes 159776 | tf_op jit(solution)/shard_map/ppermute | solution.py:540
  326.4 3.1 collective-permute-done.21
  333.2 11.7 %collective-permute-done.24 = bf16[192,1536]{1,0:T(8,128)(2,1)S(1)} collective-permute-done((bf16[192,1536]{1,0:T(8,128)(2,1)S(1)}, bf16[192,1536]{1,0:T(8,128)(2,1)S(1)}, u32[]{:S(2)}, u32[]{:S(2)}) %collective-permute-start.24) | collective-permute-done | bytes 589856 | tf_op jit(solution)/shard_map/ppermute | solution.py:540
  346.4 3.9 %collective-permute-done.25.other_ref = bf16[768,1536]{1,0:T(8,128)(2,1)} collective-permute-done((bf16[768,1536]{1,0:T(8,128)(2,1)S(1)}, bf16[768,1536]{1,0:T(8,128)(2,1)}, u32[]{:S(2)}, u32[]{:S(2)}) %collective-permute-start.25) | collective-permute-done | bytes 2359328 | tf_op jit(solution)/shard_map/ppermute | solution.py:540
  350.3 6.5 %shard_map.179 = (f32[768,2304]{1,0:T(8,128)}, f32[768,768]{1,0:T(8,128)}) custom-call(bf16[768,1536]{1,0:T(8,128)(2,1)} %copy-done.1, bf16[768,1536]{1,0:T(8,128)(2,1)} %collective-permute-done.25.other_ref), custom_call_target="tpu_custom_call" | custom-call | tf_op jit(solution)/shard_map/pallas_call | solution.py:688
  (113 shorter events, 45.9 us)
Async XLA Ops:
  14.2 44.2 %all-to-all-start = ((bf16[8,256,768]{2,1,0:T(8,128)(2,1)}), bf16[8,256,768]{2,1,0:T(8,128)(2,1)}, u32[]{:S(2)}, u32[]{:S(2)}) async-start(bf16[8,256,768]{2,1,0:T(8,128)(2,1)} %get-tuple-element.84), calls=%async_computation | async-start | bytes 6291456 | tf_op jit(solution)/shard_map/all_to_all | solution.py:736
  19.5 215.8 %reduce-scatter.3.cloned.1.call-start = ((), (), s32[]{:S(2)}) async-start(), calls=%async_computation.5 | async-start | bytes 5898240 | tf_op jit(solution)/shard_map/reduce_scatter | solution.py:768
  53.6 4.7 %collective-permute-start.4 = (bf16[256,768]{1,0:T(8,128)(2,1)}, bf16[256,768]{1,0:T(8,128)(2,1)S(1)}, u32[]{:S(2)}, u32[]{:S(2)}) collective-permute-start(bf16[256,768]{1,0:T(8,128)(2,1)} %get-tuple-element.83), channel_id=1, source_target_pairs={{0,1},{1,0},{2,3},{3,2},{4,5},{5,4},{6,7},{7,6},{8,9},{9,8},{10,11... | collective-permute-start | bytes 1179656 | tf_op jit(solution)/shard_map/ppermute | solution.py:579
  54.1 15.8 %collective-permute-start = (bf16[256,768]{1,0:T(8,128)(2,1)}, bf16[256,768]{1,0:T(8,128)(2,1)S(1)}, u32[]{:S(2)}, u32[]{:S(2)}) collective-permute-start(bf16[256,768]{1,0:T(8,128)(2,1)} %get-tuple-element.78), channel_id=1, source_target_pairs={{0,2},{1,3},{2,0},{3,1},{4,6},{5,7},{6,4},{7,5},{8,10},{9,11},{10,... | collective-permute-start | bytes 1179656 | tf_op jit(solution)/shard_map/ppermute | solution.py:579
  55.8 18.0 %collective-permute-start.1 = (bf16[256,768]{1,0:T(8,128)(2,1)}, bf16[256,768]{1,0:T(8,128)(2,1)S(1)}, u32[]{:S(2)}, u32[]{:S(2)}) collective-permute-start(bf16[256,768]{1,0:T(8,128)(2,1)} %get-tuple-element.79), channel_id=1, source_target_pairs={{0,3},{1,2},{2,1},{3,0},{4,7},{5,6},{6,5},{7,4},{8,11},{9,10},{10,... | collective-permute-start | bytes 1179656 | tf_op jit(solution)/shard_map/ppermute | solution.py:579
  56.0 17.8 %collective-permute-start.2 = (bf16[256,768]{1,0:T(8,128)(2,1)}, bf16[256,768]{1,0:T(8,128)(2,1)S(1)}, u32[]{:S(2)}, u32[]{:S(2)}) collective-permute-start(bf16[256,768]{1,0:T(8,128)(2,1)} %get-tuple-element.80), channel_id=1, source_target_pairs={{0,4},{1,5},{2,6},{3,7},{4,0},{5,1},{6,2},{7,3},{8,12},{9,13},{10,... | collective-permute-start | bytes 1179656 | tf_op jit(solution)/shard_map/ppermute | solution.py:579
  57.7 17.6 %collective-permute-start.3 = (bf16[256,768]{1,0:T(8,128)(2,1)}, bf16[256,768]{1,0:T(8,128)(2,1)S(1)}, u32[]{:S(2)}, u32[]{:S(2)}) collective-permute-start(bf16[256,768]{1,0:T(8,128)(2,1)} %get-tuple-element.81), channel_id=1, source_target_pairs={{0,5},{1,4},{2,7},{3,6},{4,1},{5,0},{6,3},{7,2},{8,13},{9,12},{10,... | collective-permute-start | bytes 1179656 | tf_op jit(solution)/shard_map/ppermute | solution.py:579
  75.3 19.8 %collective-permute-start.5 = (bf16[256,768]{1,0:T(8,128)(2,1)}, bf16[256,768]{1,0:T(8,128)(2,1)S(1)}, u32[]{:S(2)}, u32[]{:S(2)}) collective-permute-start(bf16[256,768]{1,0:T(8,128)(2,1)} %get-tuple-element.86), channel_id=1, source_target_pairs={{0,6},{1,7},{2,4},{3,5},{4,2},{5,3},{6,0},{7,1},{8,14},{9,15},{10,... | collective-permute-start | bytes 1179656 | tf_op jit(solution)/shard_map/ppermute | solution.py:579
  77.9 18.0 %collective-permute-start.6 = (bf16[256,768]{1,0:T(8,128)(2,1)}, bf16[256,768]{1,0:T(8,128)(2,1)}, u32[]{:S(2)}, u32[]{:S(2)}) collective-permute-start(bf16[256,768]{1,0:T(8,128)(2,1)} %get-tuple-element.87), channel_id=1, source_target_pairs={{0,7},{1,6},{2,5},{3,4},{4,3},{5,2},{6,1},{7,0},{8,15},{9,14},{10,... | collective-permute-start | bytes 1179656 | tf_op jit(solution)/shard_map/ppermute | solution.py:579
  137.9 42.4 %all-to-all-start.1 = ((bf16[8,256,768]{2,1,0:T(8,128)(2,1)}), bf16[8,256,768]{2,1,0:T(8,128)(2,1)}, u32[]{:S(2)}, u32[]{:S(2)}) async-start(bf16[8,256,768]{2,1,0:T(8,128)(2,1)} %shard_map.168), calls=%async_computation.1 | async-start | bytes 6291456 | tf_op jit(solution)/shard_map/all_to_all | solution.py:736
  142.4 181.5 %reduce-scatter.5.cloned.1.call-start = ((), (), s32[]{:S(2)}) async-start(), calls=%async_computation.6 | async-start | bytes 5898240 | tf_op jit(solution)/shard_map/reduce_scatter | solution.py:768
  180.3 59.6 %all-to-all-start.2 = ((bf16[8,256,768]{2,1,0:T(8,128)(2,1)}), bf16[8,256,768]{2,1,0:T(8,128)(2,1)}, u32[]{:S(2)}, u32[]{:S(2)}) async-start(bf16[8,256,768]{2,1,0:T(8,128)(2,1)} %shard_map.170), calls=%async_computation.2 | async-start | bytes 6291456 | tf_op jit(solution)/shard_map/all_to_all | solution.py:736
  234.9 4.9 %collective-permute-start.7 = (bf16[768,1536]{1,0:T(8,128)(2,1)}, bf16[768,1536]{1,0:T(8,128)(2,1)}, u32[]{:S(2)}, u32[]{:S(2)}) collective-permute-start(bf16[768,1536]{1,0:T(8,128)(2,1)} %get-tuple-element.110), channel_id=1, source_target_pairs={{0,1},{1,0},{2,3},{3,2},{4,5},{5,4},{6,7},{7,6},{8,9},{9,8},{10,11... | collective-permute-start | bytes 7077896 | tf_op jit(solution)/shard_map/ppermute | solution.py:540
  243.0 22.4 %collective-permute-start.8 = (bf16[192,1536]{1,0:T(8,128)(2,1)}, bf16[192,1536]{1,0:T(8,128)(2,1)S(1)}, u32[]{:S(2)}, u32[]{:S(2)}) collective-permute-start(bf16[192,1536]{1,0:T(8,128)(2,1)} %get-tuple-element.114), channel_id=1, source_target_pairs={{0,2},{2,0},{1,3},{3,1},{4,6},{6,4},{5,7},{7,5},{8,10},{10,8},{9,1... | collective-permute-start | bytes 1769480 | tf_op jit(solution)/shard_map/ppermute | solution.py:540
  244.9 20.6 %collective-permute-start.9 = (bf16[192,1536]{1,0:T(8,128)(2,1)}, bf16[192,1536]{1,0:T(8,128)(2,1)S(1)}, u32[]{:S(2)}, u32[]{:S(2)}) collective-permute-start(bf16[192,1536]{1,0:T(8,128)(2,1)} %get-tuple-element.116), channel_id=1, source_target_pairs={{0,4},{4,0},{1,5},{5,1},{2,6},{6,2},{3,7},{7,3},{8,12},{12,8},{9,1... | collective-permute-start | bytes 1769480 | tf_op jit(solution)/shard_map/ppermute | solution.py:540
  246.4 9.8 %copy-start.9 = (f32[1,768]{1,0:T(1,128)S(1)}, f32[1,768]{1,0:T(1,128)}, u32[]{:S(2)}) copy-start(f32[1,768]{1,0:T(1,128)} %get-tuple-element.125) | copy-start | bytes 9220
  256.9 1.2 collective-permute-start.12
  258.2 3.7 %collective-permute-start.13 = (f32[12,128]{1,0:T(8,128)S(1)}, f32[12,128]{1,0:T(8,128)S(1)}, u32[]{:S(2)}, u32[]{:S(2)}) collective-permute-start(f32[12,128]{1,0:T(8,128)S(1)} %add.218), channel_id=1, source_target_pairs={{0,2},{2,0},{1,3},{3,1},{4,6},{6,4},{5,7},{7,5},{8,10},{10,8},{9,1... | collective-permute-start | bytes 18440 | tf_op jit(solution)/shard_map/ppermute | solution.py:540
  261.8 3.7 %collective-permute-start.14 = (f32[12,128]{1,0:T(8,128)S(1)}, f32[12,128]{1,0:T(8,128)S(1)}, u32[]{:S(2)}, u32[]{:S(2)}) collective-permute-start(f32[12,128]{1,0:T(8,128)S(1)} %add.219), channel_id=1, source_target_pairs={{0,4},{4,0},{1,5},{5,1},{2,6},{6,2},{3,7},{7,3},{8,12},{12,8},{9,1... | collective-permute-start | bytes 18440 | tf_op jit(solution)/shard_map/ppermute | solution.py:540
  265.7 7.6 %collective-permute-start.11 = (bf16[96,1536]{1,0:T(8,128)(2,1)S(1)}, bf16[96,1536]{1,0:T(8,128)(2,1)S(1)}, u32[]{:S(2)}, u32[]{:S(2)}) collective-permute-start(bf16[96,1536]{1,0:T(8,128)(2,1)S(1)} %constant_dynamic-slice_fusion.4), channel_id=1, source_target_pairs={{0,2},{2,0},{1,3},{3,1},{4,6},{6,4},{5,7},{7,5},{8,10},{10,8},{9,1... | collective-permute-start | bytes 884744 | tf_op jit(solution)/shard_map/ppermute | solution.py:540
  266.5 7.4 %collective-permute-start.10 = (bf16[96,1536]{1,0:T(8,128)(2,1)S(1)}, bf16[96,1536]{1,0:T(8,128)(2,1)S(1)}, u32[]{:S(2)}, u32[]{:S(2)}) collective-permute-start(bf16[96,1536]{1,0:T(8,128)(2,1)S(1)} %constant_dynamic-slice_fusion.5), channel_id=1, source_target_pairs={{0,4},{4,0},{1,5},{5,1},{2,6},{6,2},{3,7},{7,3},{8,12},{12,8},{9,1... | collective-permute-start | bytes 884744 | tf_op jit(solution)/shard_map/ppermute | solution.py:540
  274.1 13.5 %collective-permute-start.15 = (bf16[2,24,1664]{2,1,0:T(8,128)(2,1)S(1)}, bf16[2,24,1664]{2,1,0:T(8,128)(2,1)S(1)}, u32[]{:S(2)}, u32[]{:S(2)}) collective-permute-start(bf16[2,24,1664]{2,1,0:T(8,128)(2,1)S(1)} %get-tuple-element.142), channel_id=1, source_target_pairs={{0,8},{8,16},{16,24},{24,0},{1,9},{9,17},{17,25},{25,1},{2,10},{10... | collective-permute-start | bytes 479240 | tf_op jit(solution)/shard_map/ppermute | solution.py:540
  276.2 22.8 %collective-permute-start.16 = (bf16[2,24,1664]{2,1,0:T(8,128)(2,1)S(1)}, bf16[2,24,1664]{2,1,0:T(8,128)(2,1)S(1)}, u32[]{:S(2)}, u32[]{:S(2)}) collective-permute-start(bf16[2,24,1664]{2,1,0:T(8,128)(2,1)S(1)} %get-tuple-element.141), channel_id=1, source_target_pairs={{0,16},{8,24},{16,0},{24,8},{1,17},{9,25},{17,1},{25,9},{2,18},{10... | collective-permute-start | bytes 479240 | tf_op jit(solution)/shard_map/ppermute | solution.py:540
  278.9 20.1 %collective-permute-start.17 = (bf16[2,24,1664]{2,1,0:T(8,128)(2,1)S(1)}, bf16[2,24,1664]{2,1,0:T(8,128)(2,1)S(1)}, u32[]{:S(2)}, u32[]{:S(2)}) collective-permute-start(bf16[2,24,1664]{2,1,0:T(8,128)(2,1)S(1)} %get-tuple-element.140), channel_id=1, source_target_pairs={{0,24},{8,0},{16,8},{24,16},{1,25},{9,1},{17,9},{25,17},{2,26},{10... | collective-permute-start | bytes 479240 | tf_op jit(solution)/shard_map/ppermute | solution.py:540
  299.1 17.2 %collective-permute-start.18 = (bf16[2,24,1664]{2,1,0:T(8,128)(2,1)S(1)}, bf16[2,24,1664]{2,1,0:T(8,128)(2,1)S(1)}, u32[]{:S(2)}, u32[]{:S(2)}) collective-permute-start(bf16[2,24,1664]{2,1,0:T(8,128)(2,1)S(1)} %get-tuple-element.137), channel_id=1, source_target_pairs={{0,8},{8,16},{16,24},{24,0},{1,9},{9,17},{17,25},{25,1},{2,10},{10... | collective-permute-start | bytes 479240 | tf_op jit(solution)/shard_map/ppermute | solution.py:540
  309.2 11.2 %collective-permute-start.19 = (bf16[2,24,1664]{2,1,0:T(8,128)(2,1)S(1)}, bf16[2,24,1664]{2,1,0:T(8,128)(2,1)S(1)}, u32[]{:S(2)}, u32[]{:S(2)}) collective-permute-start(bf16[2,24,1664]{2,1,0:T(8,128)(2,1)S(1)} %get-tuple-element.137), channel_id=1, source_target_pairs={{0,16},{8,24},{16,0},{24,8},{1,17},{9,25},{17,1},{25,9},{2,18},{10... | collective-permute-start | bytes 479240 | tf_op jit(solution)/shard_map/ppermute | solution.py:540
  311.8 8.6 %collective-permute-start.20 = (bf16[2,24,1664]{2,1,0:T(8,128)(2,1)S(1)}, bf16[2,24,1664]{2,1,0:T(8,128)(2,1)S(1)}, u32[]{:S(2)}, u32[]{:S(2)}) collective-permute-start(bf16[2,24,1664]{2,1,0:T(8,128)(2,1)S(1)} %get-tuple-element.137), channel_id=1, source_target_pairs={{0,24},{8,0},{16,8},{24,16},{1,25},{9,1},{17,9},{25,17},{2,26},{10... | collective-permute-start | bytes 479240 | tf_op jit(solution)/shard_map/ppermute | solution.py:540
  320.5 9.1 %collective-permute-start.21 = (bf16[96,1536]{1,0:T(8,128)(2,1)S(1)}, bf16[96,1536]{1,0:T(8,128)(2,1)S(1)}, u32[]{:S(2)}, u32[]{:S(2)}) collective-permute-start(bf16[96,1536]{1,0:T(8,128)(2,1)S(1)} %get-tuple-element.139), channel_id=1, source_target_pairs={{0,4},{4,0},{1,5},{5,1},{2,6},{6,2},{3,7},{7,3},{8,12},{12,8},{9,1... | collective-permute-start | bytes 884744 | tf_op jit(solution)/shard_map/ppermute | solution.py:540
  322.3 8.6 %collective-permute-start.22 = (bf16[96,1536]{1,0:T(8,128)(2,1)S(1)}, bf16[96,1536]{1,0:T(8,128)(2,1)S(1)}, u32[]{:S(2)}, u32[]{:S(2)}) collective-permute-start(bf16[96,1536]{1,0:T(8,128)(2,1)S(1)} %get-tuple-element.138), channel_id=1, source_target_pairs={{0,2},{2,0},{1,3},{3,1},{4,6},{6,4},{5,7},{7,5},{8,10},{10,8},{9,1... | collective-permute-start | bytes 884744 | tf_op jit(solution)/shard_map/ppermute | solution.py:540
  330.9 14.0 %collective-permute-start.24 = (bf16[192,1536]{1,0:T(8,128)(2,1)S(1)}, bf16[192,1536]{1,0:T(8,128)(2,1)S(1)}, u32[]{:S(2)}, u32[]{:S(2)}) collective-permute-start(bf16[192,1536]{1,0:T(8,128)(2,1)S(1)} %constant_dynamic-update-slice_fusion.4), channel_id=1, source_target_pairs={{0,4},{4,0},{1,5},{5,1},{2,6},{6,2},{3,7},{7,3},{8,12},{12,8},{9,1... | collective-permute-start | bytes 1769480 | tf_op jit(solution)/shard_map/ppermute | solution.py:540
  331.4 13.9 %collective-permute-start.23 = (bf16[192,1536]{1,0:T(8,128)(2,1)S(1)}, bf16[192,1536]{1,0:T(8,128)(2,1)S(1)}, u32[]{:S(2)}, u32[]{:S(2)}) collective-permute-start(bf16[192,1536]{1,0:T(8,128)(2,1)S(1)} %constant_dynamic-update-slice_fusion.6), channel_id=1, source_target_pairs={{0,2},{2,0},{1,3},{3,1},{4,6},{6,4},{5,7},{7,5},{8,10},{10,8},{9,1... | collective-permute-start | bytes 1769480 | tf_op jit(solution)/shard_map/ppermute | solution.py:540
  345.6 4.7 %collective-permute-start.25 = (bf16[768,1536]{1,0:T(8,128)(2,1)S(1)}, bf16[768,1536]{1,0:T(8,128)(2,1)}, u32[]{:S(2)}, u32[]{:S(2)}) collective-permute-start(bf16[768,1536]{1,0:T(8,128)(2,1)S(1)} %pad_maximum_fusion.mine_ref), channel_id=1, source_target_pairs={{0,1},{1,0},{2,3},{3,2},{4,5},{5,4},{6,7},{7,6},{8,9},{9,8},{10,11... | collective-permute-start | bytes 7077896 | tf_op jit(solution)/shard_map/ppermute | solution.py:540
  (10 other events, 42.3 us)
Sparse Core Ops, SparseCore 0:
  121.5 87.2 reduce-scatter.2
  211.2 96.0 reduce-scatter.4

commit v5 on v4

--- a/solution.py
+++ b/solution.py
@@ -43,6 +43,9 @@
         ),
         **kw,
     )
+
+
+ANY = pl.BlockSpec(memory_space=pl.ANY)
 
 
 def whole(shape):
@@ -322,27 +325,27 @@
     )(source, *xs, *[g] * parts, w, out_w, *earlier)
 
 
-def weight_share_body(g_ref, act_ref, out_ref):
-    out_ref[...] = tn(g_ref[...], act_ref[...]).astype(BF)
-
-
-def weight_share(g, act, shares, begin, size):
+def weight_share_body(g_ref, act_ref, *out_refs):
+    out = tn(g_ref[...], act_ref[...]).astype(BF)
+    at = 0
+    for out_ref in out_refs:
+        out_ref[...] = out[at : at + out_ref.shape[0]]
+        at += out_ref.shape[0]
+
+
+def weight_share(g, act, *heights):
     rows, width = g.shape
-    share = act.shape[1] // shares
-    block = math.gcd(768, size)
-    per = size // block
-    pick = pl.BlockSpec(
-        (pl.Element(rows), pl.Element(block)),
-        lambda i: (0, pl.multiple_of(i // per * share + begin + i % per * block, 128)),
-    )
+    units = act.shape[1]
+    block = math.gcd(768, units)
+    column = lambda height: pl.BlockSpec((height, block), lambda i: (0, i))
     return call(
         weight_share_body,
-        flops=2 * rows * width * shares * size,
-        moved=2 * (rows * width + rows * shares * size + width * shares * size),
-        grid=(shares * per,),
-        in_specs=[whole(g.shape), pick],
-        out_specs=pl.BlockSpec((width, block), lambda i: (0, i)),
-        out_shape=jax.ShapeDtypeStruct((width, shares * size), BF),
+        flops=2 * rows * width * units,
+        moved=2 * (rows * width + rows * units + width * units),
+        grid=(units // block,),
+        in_specs=[whole(g.shape), column(rows)],
+        out_specs=[column(height) for height in heights],
+        out_shape=[jax.ShapeDtypeStruct((height, units), BF) for height in heights],
     )(g, act)
 
 
@@ -457,21 +460,42 @@
 def weight_grad_body(normed_ref, g_ref, att_ref, gattn_ref, keep_ref, send_ref):
     step = pl.program_id(0)
     width = g_ref.shape[2]
-    last = step == pl.num_programs(0) - 1
-    rows = jnp.where(last, gattn_ref[...], g_ref[0])
-    left = jnp.where(last, att_ref[...], normed_ref[...])
-    out = tn(left, rows).astype(BF)
-    mine = step // 2 == lax.axis_index("core")
-    for half in range(2):
-        columns = slice(half * width, (half + 1) * width)
-
-        @pl.when((step % 2 == half) & mine)
+    half = width // 2
+    core = lax.axis_index("core")
+
+    def put(owner, at, value):
+        columns = slice(at, at + value.shape[1])
+
+        @pl.when(core == owner)
         def _():
-            keep_ref[:, columns] = out
-
-        @pl.when((step % 2 == half) & jnp.logical_not(mine))
+            keep_ref[:, columns] = value
+
+        @pl.when(core != owner)
         def _():
-            send_ref[:, columns] = out
+            send_ref[:, columns] = value
+
+    def packed_part():
+        return tn(normed_ref[...], g_ref[0]).astype(BF)
+
+    @pl.when(step == 0)
+    def _():
+        put(0, 0, packed_part())
+
+    @pl.when(step == 1)
+    def _():
+        out = packed_part()
+        put(0, width, out[:, :half])
+        put(1, 0, out[:, half:])
+
+    @pl.when(step == 2)
+    def _():
+        put(1, half, packed_part())
+
+    @pl.when(step == 3)
+    def _():
+        out = tn(att_ref[...], gattn_ref[...]).astype(BF)
+        put(0, width + half, out[:, :half])
+        put(1, width + half, out[:, half:])
 
 
 def weight_grads(normed, g, attended, gattn):
@@ -664,60 +688,54 @@
     return mine, shift(mine, "core", 1)
 
 
-def unpack_body(mine_ref, other_ref, qkv_ref, proj_ref):
-    width = proj_ref.shape[1]
-    first = lax.axis_index("core") == 0
-
-    @pl.when(first)
-    def _():
-        qkv_ref[:, : 2 * width] = mine_ref[...].astype(F32)
-        qkv_ref[:, 2 * width :] = other_ref[:, :width].astype(F32)
-        proj_ref[...] = other_ref[:, width:].astype(F32)
-
-    @pl.when(jnp.logical_not(first))
-    def _():
-        qkv_ref[:, : 2 * width] = other_ref[...].astype(F32)
-        qkv_ref[:, 2 * width :] = mine_ref[:, :width].astype(F32)
-        proj_ref[...] = mine_ref[:, width:].astype(F32)
-
-
-def unpack(mine, other):
-    width = mine.shape[0]
+def unpack_body(core_ref, in_ref, *refs):
+    qkv_ref, proj_ref = refs[-2:]
+    wide = qkv_ref.shape[1]
+    qkv_ref[...] = in_ref[:, :wide].astype(F32)
+    proj_ref[...] = in_ref[:, wide:].astype(F32)
+
+
+def unpack(core, half, earlier):
+    width = half.shape[0]
     block = min(192, width)
-    row = lambda wide: pl.BlockSpec((block, wide), lambda i: (i, 0))
-    return call(
+    shapes = [(width, 3 * width), (width, width)]
+    return pl.pallas_call(
         unpack_body,
-        limit=60,
-        grid=(width // block,),
-        in_specs=[row(2 * width)] * 2,
-        out_specs=[row(3 * width), row(width)],
-        out_shape=[
-            jax.ShapeDtypeStruct((width, 3 * width), F32),
-            jax.ShapeDtypeStruct((width, width), F32),
-        ],
-    )(mine, other)
-
-
-def widen_body(*refs):
-    at = 0
-    for ref in refs[:-1]:
-        refs[-1][:, :, at : at + ref.shape[2]] = ref[...].astype(F32)
-        at += ref.shape[2]
-
-
-def widen(*parts):
-    rows = parts[0].shape[1]
-    wide = sum(a.shape[2] for a in parts)
-    block = lambda columns: pl.BlockSpec((1, rows // 2, columns), lambda i: (0, i, 0))
+        grid_spec=pltpu.PrefetchScalarGridSpec(
+            num_scalar_prefetch=1,
+            grid=(width // block,),
+            in_specs=[pl.BlockSpec((block, 2 * width), lambda i, s: (i, 0))]
+            + [pl.BlockSpec(memory_space=pl.ANY)] * len(earlier),
+            out_specs=[
+                pl.BlockSpec((block, wide // 2), lambda i, s: (i, s[0])) for _, wide in shapes
+            ],
+        ),
+        out_shape=[jax.ShapeDtypeStruct(shape, F32) for shape in shapes],
+        input_output_aliases={2 + i: i for i in range(len(earlier))},
+        compiler_params=pltpu.CompilerParams(vmem_limit_bytes=60 << 20),
+        cost_estimate=pl.CostEstimate(
+            flops=0, bytes_accessed=12 * width * width, transcendentals=0
+        ),
+    )(core, half, *earlier)
+
+
+def widen_body(in_ref, *refs):
+    refs[-1][...] = in_ref[...].astype(F32)
+
+
+def widen(a, at, rows, *earlier):
+    _, height, wide = a.shape
+    block = math.gcd(height, 384)
     return call(
         widen_body,
         limit=60,
-        moved=6 * rows * wide,
-        grid=(2,),
-        in_specs=[block(a.shape[2]) for a in parts],
-        out_specs=block(wide),
+        moved=6 * height * wide,
+        grid=(height // block,),
+        in_specs=[pl.BlockSpec((1, block, wide), lambda i: (0, i, 0))] + [ANY] * len(earlier),
+        out_specs=pl.BlockSpec((1, block, wide), lambda i: (0, at // block + i, 0)),
         out_shape=jax.ShapeDtypeStruct((1, rows, wide), F32),
-    )(*parts)
+        input_output_aliases={1: 0} if earlier else {},
+    )(a, *earlier)
 
 
 def local(tokens, token_ids, hash_table, gain_one, w_qkv, w_proj, gain_two, w_in, w_out, cotangent):
@@ -767,11 +785,14 @@
     def scatter(a):
         return lax.psum_scatter(a[None], "dp", scatter_dimension=2, tiled=True)
 
-    grad_outer = weight_share(rows_grad, active, shares, 0, share)
+    (grad_outer,) = weight_share(rows_grad, active, width)
     grad_w_out = scatter(grad_outer)
     grad_flat = make_result(chips, after(grad_hidden, grad_outer), inner, experts)
     grad_back = exchange_all(grad_flat).reshape(-1, width)
-    grad_inner = weight_share(after(rows_in, grad_flat), grad_hidden, shares, 0, share)
+    most = width * 3 // 4
+    grad_inner, grad_later = weight_share(
+        after(rows_in, grad_flat), grad_hidden, most, width - most
+    )
     grad_w_in = scatter(grad_inner)
     results = make_result(chips, after(active, grad_inner), outer, experts)
     returned = exchange_all(after(results, grad_back))
@@ -782,7 +803,7 @@
     grad_packed = attend_back(packed, attended, totals, grad_attended)
     keep, send = weight_grads(normed, grad_packed, attended, grad_attn)
     got = shift(send, "core", 1)
-    grad_w_out = widen(after(grad_w_out, keep))
+    grad_w_out = widen(after(grad_w_out, keep), 0, width)
     top, low = split(keep, after(got, grad_w_out, returned), sides)
     grad_tokens, grad_gain_one = grad_in(
         x, first_gain, w_qkv, after(grad_packed, top, low), grad_residual
@@ -792,7 +813,7 @@
     top, low = after((add_up(top, "x"), add_up(low, "y")), grad_tokens)
     top, low = pieces_of(total(top), "y", 0), pieces_of(total(low), "x", 0)
     small = sum_over(sum_over(small, "x"), "y")
-    top, low = add_up(top, "y"), add_up(low, "x")
+    top, low = after((add_up(top, "y"), add_up(low, "x")), grad_w_in)
     both = jnp.stack([total(top), total(low)])
     pad = both.shape[0] * both.shape[1] - small.shape[0]
     small = jnp.concatenate([small, jnp.zeros((pad, 128), F32)], 0).astype(BF)
@@ -802,9 +823,22 @@
     both = gather_planes(after(add_up(pieces, "dp"), outputs))
     small = both[:, :, 2 * width :].reshape(-1, 128)[: 2 * width // 128]
     gains = small.astype(F32).reshape(2, width)
-    grad_w_in = widen(after(grad_w_in, both))
-    mine, other = gather_plane(both[:, :, : 2 * width], (grad_w_in,))
-    grad_qkv, grad_proj = unpack(mine, other)
+    grad_w_in = widen(after(grad_w_in, both), 0, width)
+    later = scatter(after(grad_later, both))
+    core = lax.axis_index("core").reshape(1).astype(jnp.int32)
+
+    def spread(both):
+        mine, other = gather_plane(both, ())
+        grads = unpack(core, mine, ())
+        return tuple(unpack(1 - core, other, after(grads, other)))
+
+    def skip(both):
+        return tuple(jnp.zeros((width, wide), F32) for wide in (3 * width, width))
+
+    grad_qkv, grad_proj = lax.cond(
+        core[0] < 2, spread, skip, after(both[:, :, : 2 * width], grad_w_in)
+    )
+    grad_w_in = widen(after(later, grad_qkv), most, width, grad_w_in)
     return (
         outputs.reshape(tokens.shape),
         grad_tokens.reshape(tokens.shape),

time: 369 us -> 361 us (0.978)
  waiting for transfers between devices: 69.8 us -> 61.9 us
  starting transfers between devices: 51.4 us -> 46.5 us
  Pallas kernels: 222 us -> 226 us
    ppermute x19, waiting for transfers between devices: 56.4 us -> 44.1 us  [shift(): return lax.ppermute(a, axis, [(i, (i + k) % n) for i in range(n)])]
    ppermute x19, starting transfers between devices: 30 us -> 25.1 us  [shift(): return lax.ppermute(a, axis, [(i, (i + k) % n) for i in range(n)])]
    pallas_call x5 -> x7, Pallas kernels: 41.2 us -> 45.4 us  [the longest x2 29.1 us: weight_share(): call(weight_share_body, flops=2 * rows * width * units, moved=2 * (rows *...]
    reduce_scatter x2 -> x3, waiting for transfers between devices: 0.02 us -> 3.84 us  [scatter(): return lax.psum_scatter(a[None], 'dp', scatter_dimension=2, tiled=True)]
  transfers between devices with their start and end apart: 31 -> 32, of which waited for: 18 -> 18; matrix products, arithmetic and copies ran while one was open for 1% -> 1% of each run, Pallas kernels for 50% -> 54%
where the time goes in v5:
time: 361 us; the launch traced here: 356 us
  Pallas kernels  226 us (63%)
  waiting for transfers between devices  61.9 us (17%)
  starting transfers between devices  46.5 us (13%)
  between operations  14.2 us (4%)
  local copies, waits for them, and re-layouts  5.49 us (2%)
    ppermute x19, waiting for transfers between devices, shift(): return lax.ppermute(a, axis, [(i, (i + k) % n) for i in range(n)])  44.1 us
    pallas_call x3, Pallas kernels, expert(): pl.pallas_call(functools.partial(expert_body, parts=parts, kept=len(earli...  38.4 us
    pallas_call x2, Pallas kernels, make_result(): pl.pallas_call(result_body, grid_spec=pltpu.PrefetchScalarGridSpec(num_sc...  31.7 us
    pallas_call x2, Pallas kernels, weight_share(): call(weight_share_body, flops=2 * rows * width * units, moved=2 * (rows *...  29.1 us
    pallas_call x1, Pallas kernels, attend_back(): call(functools.partial(attend_back_body, block=min(256, length)), flops=3...  25.7 us
    ppermute x19, starting transfers between devices, shift(): return lax.ppermute(a, axis, [(i, (i + k) % n) for i in range(n)])  25.1 us
    pallas_call x1, Pallas kernels, attend(): call(functools.partial(attend_body, block=min(512, length)), flops=120000...  24.3 us
    all_to_all x3, starting transfers between devices, exchange_all(): return lax.all_to_all(a, PLANE, split_axis=0, concat_axis=0, tiled=True)  14.2 us
  transfers between devices with their start and end apart: 32, of which 18 were waited for; matrix products, arithmetic and copies ran while one was open for 1% of the time, Pallas kernels for 54%

profile of v5, /device:TPU:0, one launch (start us, length us, event | category | flops | bytes accessed | tf_op | source)
XLA Modules:
  0.0 355.8 jit_solution(9784059285181906911)
XLA Ops:
  7.2 7.1 %shard_map.161 = (s32[1,1024]{1,0:T(1,128)}, s32[1024,1]{1,0:T(8,128)}, bf16[8,256,768]{2,1,0:T(8,128)(2,1)}) custom-call(s32[1,1024]{1,0:T(1,128)} %ids_ref.1, s32[64,128]{1,0:T(8,128)} %bitcast.61, bf16[1024,768]{1,0:T(8,128)(2,1)} %bitcast.56), custom_call_target="tpu_custom_call" | custom-call | flops 3221225472 | bytes 4718592 | tf_op jit(solution)/shard_map/pallas_call | solution.py:111
  14.2 5.3 %all-to-all-start = ((bf16[8,256,768]{2,1,0:T(8,128)(2,1)}), bf16[8,256,768]{2,1,0:T(8,128)(2,1)}, u32[]{:S(2)}, u32[]{:S(2)}) async-start(bf16[8,256,768]{2,1,0:T(8,128)(2,1)} %get-tuple-element.104), calls=%async_computation | async-start | bytes 6291456 | tf_op jit(solution)/shard_map/all_to_all | solution.py:754
  20.9 24.3 %shard_map.162 = (bf16[3,1024,768]{2,1,0:T(8,128)(2,1)}, bf16[1024,768]{1,0:T(8,128)(2,1)}, bf16[1024,768]{1,0:T(8,128)(2,1)}, f32[6,2,1024]{2,1,0:T(2,128)}) custom-call(bf16[1024,768]{1,0:T(8,128)(2,1)} %bitcast.58, f32[1,768]{1,0:T(1,128)} %reshape.64.gain_ref, bf16[768,2304]{1,0:T(8,128)(2,1)} %w_ref.5, bf16[768,2304]{1,0:T(8,128)(2,1)} %w_ref.5, ...), custom_call_target="tpu_custom_call" | custom-call | flops 15623878656 | bytes 12976128 | tf_op jit(solution)/shard_map/pallas_call | solution.py:164
  45.3 8.4 %shard_map.163 = (f32[1024,768]{1,0:T(8,128)}, bf16[256,768]{1,0:T(8,128)(2,1)}, bf16[256,768]{1,0:T(8,128)(2,1)}, bf16[256,768]{1,0:T(8,128)(2,1)}, bf16[256,76...) custom-call(bf16[1024,768]{1,0:T(8,128)(2,1)} %get-tuple-element.93., ...), custom_call_target="tpu_custom_call" | custom-call | flops 4429185024 | bytes 11010048 | tf_op jit(solution)/shard_map/pallas_call | solution.py:258
  59.2 10.7 %shard_map.164 = (bf16[2048,3072]{1,0:T(8,128)(2,1)}, bf16[2048,3072]{1,0:T(8,128)(2,1)}, bf16[2048,768]{1,0:T(8,128)(2,1)}, bf16[2048,768]{1,0:T(8,128)(2,1)}) custom-call(s32[8]{0:T(128)} %stack.64.from_ref, bf16[256,768]{1,0:T(8,128)(2,1)} %get-tuple-element.102.refs_0_, bf16[256,768]{1,0:T(8,128)(2,1)} %copy-done.11, ...), custom_call_target="tpu_custom_call" | custom-call | flops 4831838208 | bytes 18874368 | tf_op jit(solution)/shard_map/pallas_call | solution.py:305
  69.9 3.9 %collective-permute-done.6.refs_1_ = bf16[256,768]{1,0:T(8,128)(2,1)S(1)} collective-permute-done((bf16[256,768]{1,0:T(8,128)(2,1)}, bf16[256,768]{1,0:T(8,128)(2,1)S(1)}, u32[]{:S(2)}, u32[]{:S(2)}) %collective-permute-start.6) | collective-permute-done | bytes 393248 | tf_op jit(solution)/shard_map/ppermute | solution.py:603
  78.1 16.8 %shard_map.165 = (bf16[2048,3072]{1,0:T(8,128)(2,1)}, bf16[2048,3072]{1,0:T(8,128)(2,1)}, bf16[2048,768]{1,0:T(8,128)(2,1)}, bf16[2048,768]{1,0:T(8,128)(2,1)}) custom-call(s32[8]{0:T(128)} %stack.64.from_ref, bf16[256,768]{1,0:T(8,128)(2,1)} %copy-done.2, ...), custom_call_target="tpu_custom_call", output_to_operand_aliasing={{0}: (11, {}), {1}: (12, {}), {2}: (13, {}), {3}: (14, {})} | custom-call | flops 9663676416 | bytes 28311552 | tf_op jit(solution)/shard_map/pallas_call | solution.py:305
  96.0 10.8 %shard_map.166 = (bf16[2048,3072]{1,0:T(8,128)(2,1)}, bf16[2048,3072]{1,0:T(8,128)(2,1)}, bf16[2048,768]{1,0:T(8,128)(2,1)}, bf16[2048,768]{1,0:T(8,128)(2,1)}) custom-call(s32[8]{0:T(128)} %stack.64.from_ref, bf16[256,768]{1,0:T(8,128)(2,1)} %copy-done.6, ...), custom_call_target="tpu_custom_call", output_to_operand_aliasing={{0}: (7, {}), {1}: (8, {}), {2}: (9, {}), {3}: (10, {})} | custom-call | flops 4831838208 | bytes 18874368 | tf_op jit(solution)/shard_map/pallas_call | solution.py:305
  106.8 14.6 %shard_map.167 = bf16[768,3072]{1,0:T(8,128)(2,1)} custom-call(bf16[2048,768]{1,0:T(8,128)(2,1)} %get-tuple-element.118.g_ref, bf16[2048,3072]{1,0:T(8,128)(2,1)} %get-tuple-element.122.act_ref), custom_call_target="tpu_custom_call" | custom-call | flops 9663676416 | bytes 20447232 | tf_op jit(solution)/shard_map/pallas_call | solution.py:341
  122.2 15.9 %shard_map.168 = bf16[8,256,768]{2,1,0:T(8,128)(2,1)} custom-call(s32[4]{0:T(128)} %pad_add_fusion.chip_ref, bf16[2048,3072]{1,0:T(8,128)(2,1)} %get-tuple-element.119.act_ref, bf16[768,3072]{1,0:T(8,128)(2,1)} %bitcast.46), custom_call_target="tpu_custom_call" | custom-call | flops 9663676416 | bytes 20447232 | tf_op jit(solution)/shard_map/pallas_call | solution.py:372
  138.0 4.5 %all-to-all-start.1 = ((bf16[8,256,768]{2,1,0:T(8,128)(2,1)}), bf16[8,256,768]{2,1,0:T(8,128)(2,1)}, u32[]{:S(2)}, u32[]{:S(2)}) async-start(bf16[8,256,768]{2,1,0:T(8,128)(2,1)} %shard_map.168), calls=%async_computation.1 | async-start | bytes 6291456 | tf_op jit(solution)/shard_map/all_to_all | solution.py:754
  142.6 14.5 %shard_map.169 = (bf16[576,3072]{1,0:T(8,128)(2,1)}, bf16[192,3072]{1,0:T(8,128)(2,1)}) custom-call(bf16[2048,768]{1,0:T(8,128)(2,1)} %get-tuple-element.120.g_ref, bf16[2048,3072]{1,0:T(8,128)(2,1)} %get-tuple-element.119.act_ref), custom_call_target="tpu_custom_call" | custom-call | flops 9663676416 | bytes 20447232 | tf_op jit(solution)/shard_map/pallas_call | solution.py:341
  157.1 15.8 %shard_map.170 = bf16[8,256,768]{2,1,0:T(8,128)(2,1)} custom-call(s32[4]{0:T(128)} %pad_add_fusion.chip_ref, bf16[2048,3072]{1,0:T(8,128)(2,1)} %get-tuple-element.122.act_ref, bf16[768,3072]{1,0:T(8,128)(2,1)} %bitcast.50), custom_call_target="tpu_custom_call" | custom-call | flops 9663676416 | bytes 20447232 | tf_op jit(solution)/shard_map/pallas_call | solution.py:372
  172.9 7.5 %all-to-all-done.1 = bf16[8,256,768]{2,1,0:T(8,128)(2,1)} async-done(((bf16[8,256,768]{2,1,0:T(8,128)(2,1)}), bf16[8,256,768]{2,1,0:T(8,128)(2,1)}, u32[]{:S(2)}, u32[]{:S(2)}) %all-to-all-start.1) | async-done | bytes 3145760 | tf_op jit(solution)/shard_map/all_to_all | solution.py:754
  180.4 4.5 %all-to-all-start.2 = ((bf16[8,256,768]{2,1,0:T(8,128)(2,1)}), bf16[8,256,768]{2,1,0:T(8,128)(2,1)}, u32[]{:S(2)}, u32[]{:S(2)}) async-start(bf16[8,256,768]{2,1,0:T(8,128)(2,1)} %shard_map.170), calls=%async_computation.2 | async-start | bytes 6291456 | tf_op jit(solution)/shard_map/all_to_all | solution.py:754
  184.9 13.3 %shard_map.171 = (f32[1024,768]{1,0:T(8,128)}, bf16[1024,768]{1,0:T(8,128)(2,1)}, bf16[1024,768]{1,0:T(8,128)(2,1)}, f32[1,768]{1,0:T(1,128)}) custom-call(s32[1024,1]{1,0:T(8,128)} %get-tuple-element.92.col_ref, f32[1024,768]{1,0:T(8,128)} %get-tuple-element.95.res_ref, bf16[1024,768]{1,0:T(8,128)(2,1)} %bitcast.57, f32[1,768]{1,0:T(1,128)} %reshape.65.gain_ref, ...), custom_call_target="tpu_custom_call" | custom-call | flops 5637144576 | bytes 15728640 | tf_op jit(solution)/shard_map/pallas_call | solution.py:420
  198.2 25.7 %shard_map.172.g_ref = bf16[3,1024,768]{2,1,0:T(8,128)(2,1)} custom-call(bf16[3,1024,768]{2,1,0:T(8,128)(2,1)} %get-tuple-element.125.packed_ref, bf16[1024,768]{1,0:T(8,128)(2,1)} %get-tuple-element.93.att_ref.o_ref, bf16[1024,768]{1,0:T(8,128)(2,1)} %get-tuple-element.127.up_ref, f32[6,2,1024]{2,1,0:T(2,128)} %get-tuple-element.128.total_ref), custom_call_target="tpu_custom_call" | custom-call | flops 30000001024 | bytes 12582912 | tf_op jit(solution)/shard_map/pallas_call | solution.py:229
  223.9 11.5 %shard_map.173 = (bf16[768,1536]{1,0:T(8,128)(2,1)}, bf16[768,1536]{1,0:T(8,128)(2,1)}) custom-call(bf16[1024,768]{1,0:T(8,128)(2,1)} %get-tuple-element.124.normed_ref, bf16[3,1024,768]{2,1,0:T(8,128)(2,1)} %shard_map.172.g_ref, bf16[1024,768]{1,0:T(8,128)(2,1)} %get-tuple-element.93.att_ref.o_ref, bf16[1024,768]{1,0:T(8,128)(2,1)} %get-tuple-element.129.gattn_ref), custom_call_target="tpu_custom_call" | custom-call | flops 4831838208 | bytes 14155776 | tf_op jit(solution)/shard_map/pallas_call | solution.py:504
  240.3 3.1 shard_map.175
  246.7 10.0 %shard_map.176 = (f32[1024,768]{1,0:T(8,128)}, f32[1,768]{1,0:T(1,128)}) custom-call(bf16[1024,768]{1,0:T(8,128)(2,1)} %bitcast.60, f32[1,768]{1,0:T(1,128)} %reshape.64.gain_ref, bf16[768,2304]{1,0:T(8,128)(2,1)} %w_ref.5, bf16[3,1024,768]{2,1,0:T(8,128)(2,1)} %shard_map.172.g_ref, f32[1024,768]{1,0:T(8,128)} %get-tuple-element.139.gres_ref), custom_call_target="tpu_custom_call" | custom-call | flops 3623878656 | bytes 14155776 | tf_op jit(solution)/shard_map/pallas_call | solution.py:544
  265.9 4.6 %collective-permute-done.18 = f32[12,128]{1,0:T(8,128)S(1)} collective-permute-done((f32[12,128]{1,0:T(8,128)S(1)}, f32[12,128]{1,0:T(8,128)S(1)}, u32[]{:S(2)}, u32[]{:S(2)}) %collective-permute-start.18) | collective-permute-done | bytes 6176 | tf_op jit(solution)/shard_map/ppermute | solution.py:564
  271.0 3.1 collective-permute-done.19
  274.1 3.8 %reduce-scatter.6.cloned.1.call-done.in_ref = bf16[1,576,768]{2,1,0:T(8,128)(2,1)} async-done(((bf16[1,576,3072]{2,1,0:T(8,128)(2,1)}), bf16[1,576,768]{2,1,0:T(8,128)(2,1)}) %reduce-scatter.6.cloned.1.call-update) | async-done | bytes 884752 | tf_op jit(solution)/shard_map/reduce_scatter | solution.py:786
  284.0 7.4 %shard_map.177 = bf16[1024,768]{1,0:T(8,128)(2,1)} custom-call(s32[1024,1]{1,0:T(8,128)} %get-tuple-element.92.col_ref, f32[1024,768]{1,0:T(8,128)} %get-tuple-element.95.res_ref, bf16[2048,768]{1,0:T(8,128)(2,1)} %bitcast.21.back_ref), custom_call_target="tpu_custom_call" | custom-call | flops 3221225472 | bytes 7864320 | tf_op jit(solution)/shard_map/pallas_call | solution.py:448
  292.9 3.9 %collective-permute-start.23 = (bf16[2,24,1664]{2,1,0:T(8,128)(2,1)S(1)}, bf16[2,24,1664]{2,1,0:T(8,128)(2,1)S(1)}, u32[]{:S(2)}, u32[]{:S(2)}) collective-permute-start(bf16[2,24,1664]{2,1,0:T(8,128)(2,1)S(1)} %get-tuple-element.164), channel_id=1, source_target_pairs={{0,8},{8,16},{16,24},{24,0},{1,9},{9,17},{17,25},{25,1},{2,10},{10... | collective-permute-start | bytes 479240 | tf_op jit(solution)/shard_map/ppermute | solution.py:564
  299.3 4.2 %collective-permute-done.23 = bf16[2,24,1664]{2,1,0:T(8,128)(2,1)S(1)} collective-permute-done((bf16[2,24,1664]{2,1,0:T(8,128)(2,1)S(1)}, bf16[2,24,1664]{2,1,0:T(8,128)(2,1)S(1)}, u32[]{:S(2)}, u32[]{:S(2)}) %collective-permute-start.23) | collective-permute-done | bytes 159776 | tf_op jit(solution)/shard_map/ppermute | solution.py:564
  303.5 5.1 %collective-permute-done.24 = bf16[2,24,1664]{2,1,0:T(8,128)(2,1)S(1)} collective-permute-done((bf16[2,24,1664]{2,1,0:T(8,128)(2,1)S(1)}, bf16[2,24,1664]{2,1,0:T(8,128)(2,1)S(1)}, u32[]{:S(2)}, u32[]{:S(2)}) %collective-permute-start.24) | collective-permute-done | bytes 159776 | tf_op jit(solution)/shard_map/ppermute | solution.py:564
  311.8 34.9 %conditional.1 = ((f32[768,2304]{1,0:T(8,128)}, f32[768,768]{1,0:T(8,128)})) conditional(s32[]{:T(128)} %convert_element_type.76, () %tuple.47, (s32[]{:T(128)}, bf16[2,96,1536]{2,1,0:T(8,128)(2,1)S(1)}) %tuple.50), branch_computations={%region_2.3_spmd, %region_3.4_spmd} | conditional | flops 4718645 | bytes 56623972 | solution.py:838
  315.0 5.8 %collective-permute-done = bf16[96,1536]{1,0:T(8,128)(2,1)S(1)} collective-permute-done((bf16[96,1536]{1,0:T(8,128)(2,1)S(1)}, bf16[96,1536]{1,0:T(8,128)(2,1)S(1)}, u32[]{:S(2)}, u32[]{:S(2)}) %collective-permute-start) | collective-permute-done | bytes 294944 | tf_op jit(solution)/shard_map/cond/branch_1_fun/ppermute | solution.py:564
  324.4 11.8 %collective-permute-done.3 = bf16[192,1536]{1,0:T(8,128)(2,1)S(1)} collective-permute-done((bf16[192,1536]{1,0:T(8,128)(2,1)S(1)}, bf16[192,1536]{1,0:T(8,128)(2,1)S(1)}, u32[]{:S(2)}, u32[]{:S(2)}) %collective-permute-start.3) | collective-permute-done | bytes 589856 | tf_op jit(solution)/shard_map/cond/branch_1_fun/ppermute | solution.py:564
  338.0 4.3 %branch_1_fun.2 = (f32[768,2304]{1,0:T(8,128)}, f32[768,768]{1,0:T(8,128)}) custom-call(s32[1]{0:T(128)} %bitcast.core_ref, bf16[768,1536]{1,0:T(8,128)(2,1)} %copy-done.1), custom_call_target="tpu_custom_call" | custom-call | bytes 7077888 | tf_op jit(solution)/shard_map/cond/branch_1_fun/pallas_call | solution.py:702
  342.4 4.3 %branch_1_fun.3 = (f32[768,2304]{1,0:T(8,128)}, f32[768,768]{1,0:T(8,128)}) custom-call(s32[1]{0:T(128)S(6)} %sub.5.core_ref, bf16[768,1536]{1,0:T(8,128)(2,1)} %collective-permute-done.4.in_ref, f32[768,2304]{1,0:T(8,128)} %get-tuple-element.11.refs_0_, f32[768,768]{1,0:T(8,128)} %get-tuple-element.12.refs_1_), custom_call_target="tpu_custom_call", output_to_operand_aliasing={{0}: (2, {}), {1}: (3, {})} | custom-call | bytes 7077888 | tf_op jit(solution)/shard_map/cond/branch_1_fun/pallas_call | solution.py:702
  (121 shorter events, 54.9 us)
Async XLA Ops:
  14.2 44.2 %all-to-all-start = ((bf16[8,256,768]{2,1,0:T(8,128)(2,1)}), bf16[8,256,768]{2,1,0:T(8,128)(2,1)}, u32[]{:S(2)}, u32[]{:S(2)}) async-start(bf16[8,256,768]{2,1,0:T(8,128)(2,1)} %get-tuple-element.104), calls=%async_computation | async-start | bytes 6291456 | tf_op jit(solution)/shard_map/all_to_all | solution.py:754
  19.5 216.2 %reduce-scatter.4.cloned.1.call-start = ((), (), s32[]{:S(2)}) async-start(), calls=%async_computation.6 | async-start | bytes 5898240 | tf_op jit(solution)/shard_map/reduce_scatter | solution.py:786
  53.6 4.8 %collective-permute-start.9 = (bf16[256,768]{1,0:T(8,128)(2,1)}, bf16[256,768]{1,0:T(8,128)(2,1)S(1)}, u32[]{:S(2)}, u32[]{:S(2)}) collective-permute-start(bf16[256,768]{1,0:T(8,128)(2,1)} %get-tuple-element.103), channel_id=1, source_target_pairs={{0,1},{1,0},{2,3},{3,2},{4,5},{5,4},{6,7},{7,6},{8,9},{9,8},{10,11... | collective-permute-start | bytes 1179656 | tf_op jit(solution)/shard_map/ppermute | solution.py:603
  54.1 15.8 %collective-permute-start.5 = (bf16[256,768]{1,0:T(8,128)(2,1)}, bf16[256,768]{1,0:T(8,128)(2,1)S(1)}, u32[]{:S(2)}, u32[]{:S(2)}) collective-permute-start(bf16[256,768]{1,0:T(8,128)(2,1)} %get-tuple-element.98), channel_id=1, source_target_pairs={{0,2},{1,3},{2,0},{3,1},{4,6},{5,7},{6,4},{7,5},{8,10},{9,11},{10,... | collective-permute-start | bytes 1179656 | tf_op jit(solution)/shard_map/ppermute | solution.py:603
  55.8 18.0 %collective-permute-start.6 = (bf16[256,768]{1,0:T(8,128)(2,1)}, bf16[256,768]{1,0:T(8,128)(2,1)S(1)}, u32[]{:S(2)}, u32[]{:S(2)}) collective-permute-start(bf16[256,768]{1,0:T(8,128)(2,1)} %get-tuple-element.99), channel_id=1, source_target_pairs={{0,3},{1,2},{2,1},{3,0},{4,7},{5,6},{6,5},{7,4},{8,11},{9,10},{10,... | collective-permute-start | bytes 1179656 | tf_op jit(solution)/shard_map/ppermute | solution.py:603
  56.0 17.9 %collective-permute-start.7 = (bf16[256,768]{1,0:T(8,128)(2,1)}, bf16[256,768]{1,0:T(8,128)(2,1)S(1)}, u32[]{:S(2)}, u32[]{:S(2)}) collective-permute-start(bf16[256,768]{1,0:T(8,128)(2,1)} %get-tuple-element.100), channel_id=1, source_target_pairs={{0,4},{1,5},{2,6},{3,7},{4,0},{5,1},{6,2},{7,3},{8,12},{9,13},{10,... | collective-permute-start | bytes 1179656 | tf_op jit(solution)/shard_map/ppermute | solution.py:603
  57.7 17.6 %collective-permute-start.8 = (bf16[256,768]{1,0:T(8,128)(2,1)}, bf16[256,768]{1,0:T(8,128)(2,1)S(1)}, u32[]{:S(2)}, u32[]{:S(2)}) collective-permute-start(bf16[256,768]{1,0:T(8,128)(2,1)} %get-tuple-element.101), channel_id=1, source_target_pairs={{0,5},{1,4},{2,7},{3,6},{4,1},{5,0},{6,3},{7,2},{8,13},{9,12},{10,... | collective-permute-start | bytes 1179656 | tf_op jit(solution)/shard_map/ppermute | solution.py:603
  75.3 19.6 %collective-permute-start.10 = (bf16[256,768]{1,0:T(8,128)(2,1)}, bf16[256,768]{1,0:T(8,128)(2,1)S(1)}, u32[]{:S(2)}, u32[]{:S(2)}) collective-permute-start(bf16[256,768]{1,0:T(8,128)(2,1)} %get-tuple-element.106), channel_id=1, source_target_pairs={{0,6},{1,7},{2,4},{3,5},{4,2},{5,3},{6,0},{7,1},{8,14},{9,15},{10,... | collective-permute-start | bytes 1179656 | tf_op jit(solution)/shard_map/ppermute | solution.py:603
  77.9 18.0 %collective-permute-start.11 = (bf16[256,768]{1,0:T(8,128)(2,1)}, bf16[256,768]{1,0:T(8,128)(2,1)}, u32[]{:S(2)}, u32[]{:S(2)}) collective-permute-start(bf16[256,768]{1,0:T(8,128)(2,1)} %get-tuple-element.107), channel_id=1, source_target_pairs={{0,7},{1,6},{2,5},{3,4},{4,3},{5,2},{6,1},{7,0},{8,15},{9,14},{10,... | collective-permute-start | bytes 1179656 | tf_op jit(solution)/shard_map/ppermute | solution.py:603
  138.0 42.4 %all-to-all-start.1 = ((bf16[8,256,768]{2,1,0:T(8,128)(2,1)}), bf16[8,256,768]{2,1,0:T(8,128)(2,1)}, u32[]{:S(2)}, u32[]{:S(2)}) async-start(bf16[8,256,768]{2,1,0:T(8,128)(2,1)} %shard_map.168), calls=%async_computation.1 | async-start | bytes 6291456 | tf_op jit(solution)/shard_map/all_to_all | solution.py:754
  142.5 135.4 %reduce-scatter.6.cloned.1.call-start = ((), (), s32[]{:S(2)}) async-start(), calls=%async_computation.7 | async-start | bytes 4423680 | tf_op jit(solution)/shard_map/reduce_scatter | solution.py:786
  180.4 59.8 %all-to-all-start.2 = ((bf16[8,256,768]{2,1,0:T(8,128)(2,1)}), bf16[8,256,768]{2,1,0:T(8,128)(2,1)}, u32[]{:S(2)}, u32[]{:S(2)}) async-start(bf16[8,256,768]{2,1,0:T(8,128)(2,1)} %shard_map.170), calls=%async_computation.2 | async-start | bytes 6291456 | tf_op jit(solution)/shard_map/all_to_all | solution.py:754
  184.9 162.4 %reduce-scatter.8.cloned.1.call-start = ((), (), s32[]{:S(2)}) async-start(), calls=%async_computation.8 | async-start | bytes 1474560 | tf_op jit(solution)/shard_map/reduce_scatter | solution.py:786
  235.4 4.9 %collective-permute-start.12 = (bf16[768,1536]{1,0:T(8,128)(2,1)}, bf16[768,1536]{1,0:T(8,128)(2,1)}, u32[]{:S(2)}, u32[]{:S(2)}) collective-permute-start(bf16[768,1536]{1,0:T(8,128)(2,1)} %get-tuple-element.131), channel_id=1, source_target_pairs={{0,1},{1,0},{2,3},{3,2},{4,5},{5,4},{6,7},{7,6},{8,9},{9,8},{10,11... | collective-permute-start | bytes 7077896 | tf_op jit(solution)/shard_map/ppermute | solution.py:564
  243.4 15.8 %collective-permute-start.13 = (bf16[192,1536]{1,0:T(8,128)(2,1)}, bf16[192,1536]{1,0:T(8,128)(2,1)S(1)}, u32[]{:S(2)}, u32[]{:S(2)}) collective-permute-start(bf16[192,1536]{1,0:T(8,128)(2,1)} %get-tuple-element.135), channel_id=1, source_target_pairs={{0,2},{2,0},{1,3},{3,1},{4,6},{6,4},{5,7},{7,5},{8,10},{10,8},{9,1... | collective-permute-start | bytes 1769480 | tf_op jit(solution)/shard_map/ppermute | solution.py:564
  245.3 15.3 %collective-permute-start.14 = (bf16[192,1536]{1,0:T(8,128)(2,1)}, bf16[192,1536]{1,0:T(8,128)(2,1)S(1)}, u32[]{:S(2)}, u32[]{:S(2)}) collective-permute-start(bf16[192,1536]{1,0:T(8,128)(2,1)} %get-tuple-element.137), channel_id=1, source_target_pairs={{0,4},{4,0},{1,5},{5,1},{2,6},{6,2},{3,7},{7,3},{8,12},{12,8},{9,1... | collective-permute-start | bytes 1769480 | tf_op jit(solution)/shard_map/ppermute | solution.py:564
  260.9 17.1 %collective-permute-start.15 = (bf16[96,1536]{1,0:T(8,128)(2,1)S(1)}, bf16[96,1536]{1,0:T(8,128)(2,1)S(1)}, u32[]{:S(2)}, u32[]{:S(2)}) collective-permute-start(bf16[96,1536]{1,0:T(8,128)(2,1)S(1)} %get-tuple-element.173), channel_id=1, source_target_pairs={{0,4},{4,0},{1,5},{5,1},{2,6},{6,2},{3,7},{7,3},{8,12},{12,8},{9,1... | collective-permute-start | bytes 884744 | tf_op jit(solution)/shard_map/ppermute | solution.py:564
  262.5 15.5 %collective-permute-start.16 = (bf16[96,1536]{1,0:T(8,128)(2,1)S(1)}, bf16[96,1536]{1,0:T(8,128)(2,1)S(1)}, u32[]{:S(2)}, u32[]{:S(2)}) collective-permute-start(bf16[96,1536]{1,0:T(8,128)(2,1)S(1)} %get-tuple-element.171), channel_id=1, source_target_pairs={{0,2},{2,0},{1,3},{3,1},{4,6},{6,4},{5,7},{7,5},{8,10},{10,8},{9,1... | collective-permute-start | bytes 884744 | tf_op jit(solution)/shard_map/ppermute | solution.py:564
  263.2 1.2 collective-permute-start.17
  264.4 6.1 %collective-permute-start.18 = (f32[12,128]{1,0:T(8,128)S(1)}, f32[12,128]{1,0:T(8,128)S(1)}, u32[]{:S(2)}, u32[]{:S(2)}) collective-permute-start(f32[12,128]{1,0:T(8,128)S(1)} %add.228), channel_id=1, source_target_pairs={{0,2},{2,0},{1,3},{3,1},{4,6},{6,4},{5,7},{7,5},{8,10},{10,8},{9,1... | collective-permute-start | bytes 18440 | tf_op jit(solution)/shard_map/ppermute | solution.py:564
  270.5 3.7 %collective-permute-start.19 = (f32[12,128]{1,0:T(8,128)S(1)}, f32[12,128]{1,0:T(8,128)S(1)}, u32[]{:S(2)}, u32[]{:S(2)}) collective-permute-start(f32[12,128]{1,0:T(8,128)S(1)} %add.229), channel_id=1, source_target_pairs={{0,4},{4,0},{1,5},{5,1},{2,6},{6,2},{3,7},{7,3},{8,12},{12,8},{9,1... | collective-permute-start | bytes 18440 | tf_op jit(solution)/shard_map/ppermute | solution.py:564
  278.3 13.2 %collective-permute-start.20 = (bf16[2,24,1664]{2,1,0:T(8,128)(2,1)S(1)}, bf16[2,24,1664]{2,1,0:T(8,128)(2,1)S(1)}, u32[]{:S(2)}, u32[]{:S(2)}) collective-permute-start(bf16[2,24,1664]{2,1,0:T(8,128)(2,1)S(1)} %get-tuple-element.169), channel_id=1, source_target_pairs={{0,8},{8,16},{16,24},{24,0},{1,9},{9,17},{17,25},{25,1},{2,10},{10... | collective-permute-start | bytes 479240 | tf_op jit(solution)/shard_map/ppermute | solution.py:564
  279.6 13.2 %collective-permute-start.21 = (bf16[2,24,1664]{2,1,0:T(8,128)(2,1)S(1)}, bf16[2,24,1664]{2,1,0:T(8,128)(2,1)S(1)}, u32[]{:S(2)}, u32[]{:S(2)}) collective-permute-start(bf16[2,24,1664]{2,1,0:T(8,128)(2,1)S(1)} %get-tuple-element.168), channel_id=1, source_target_pairs={{0,16},{8,24},{16,0},{24,8},{1,17},{9,25},{17,1},{25,9},{2,18},{10... | collective-permute-start | bytes 479240 | tf_op jit(solution)/shard_map/ppermute | solution.py:564
  281.3 11.5 %collective-permute-start.22 = (bf16[2,24,1664]{2,1,0:T(8,128)(2,1)S(1)}, bf16[2,24,1664]{2,1,0:T(8,128)(2,1)S(1)}, u32[]{:S(2)}, u32[]{:S(2)}) collective-permute-start(bf16[2,24,1664]{2,1,0:T(8,128)(2,1)S(1)} %get-tuple-element.167), channel_id=1, source_target_pairs={{0,24},{8,0},{16,8},{24,16},{1,25},{9,1},{17,9},{25,17},{2,26},{10... | collective-permute-start | bytes 479240 | tf_op jit(solution)/shard_map/ppermute | solution.py:564
  292.9 10.6 %collective-permute-start.23 = (bf16[2,24,1664]{2,1,0:T(8,128)(2,1)S(1)}, bf16[2,24,1664]{2,1,0:T(8,128)(2,1)S(1)}, u32[]{:S(2)}, u32[]{:S(2)}) collective-permute-start(bf16[2,24,1664]{2,1,0:T(8,128)(2,1)S(1)} %get-tuple-element.164), channel_id=1, source_target_pairs={{0,8},{8,16},{16,24},{24,0},{1,9},{9,17},{17,25},{25,1},{2,10},{10... | collective-permute-start | bytes 479240 | tf_op jit(solution)/shard_map/ppermute | solution.py:564
  296.9 11.7 %collective-permute-start.24 = (bf16[2,24,1664]{2,1,0:T(8,128)(2,1)S(1)}, bf16[2,24,1664]{2,1,0:T(8,128)(2,1)S(1)}, u32[]{:S(2)}, u32[]{:S(2)}) collective-permute-start(bf16[2,24,1664]{2,1,0:T(8,128)(2,1)S(1)} %get-tuple-element.164), channel_id=1, source_target_pairs={{0,16},{8,24},{16,0},{24,8},{1,17},{9,25},{17,1},{25,9},{2,18},{10... | collective-permute-start | bytes 479240 | tf_op jit(solution)/shard_map/ppermute | solution.py:564
  298.9 9.7 %collective-permute-start.25 = (bf16[2,24,1664]{2,1,0:T(8,128)(2,1)S(1)}, bf16[2,24,1664]{2,1,0:T(8,128)(2,1)S(1)}, u32[]{:S(2)}, u32[]{:S(2)}) collective-permute-start(bf16[2,24,1664]{2,1,0:T(8,128)(2,1)S(1)} %get-tuple-element.164), channel_id=1, source_target_pairs={{0,24},{8,0},{16,8},{24,16},{1,25},{9,1},{17,9},{25,17},{2,26},{10... | collective-permute-start | bytes 479240 | tf_op jit(solution)/shard_map/ppermute | solution.py:564
  311.9 8.9 %collective-permute-start = (bf16[96,1536]{1,0:T(8,128)(2,1)S(1)}, bf16[96,1536]{1,0:T(8,128)(2,1)S(1)}, u32[]{:S(2)}, u32[]{:S(2)}) collective-permute-start(bf16[96,1536]{1,0:T(8,128)(2,1)S(1)} %get-tuple-element.166), channel_id=1, source_target_pairs={{0,4},{4,0},{1,5},{5,1},{2,6},{6,2},{3,7},{7,3},{8,12},{12,8},{9,1... | collective-permute-start | bytes 884744 | tf_op jit(solution)/shard_map/cond/branch_1_fun/ppermute | solution.py:564
  313.4 8.6 %collective-permute-start.1 = (bf16[96,1536]{1,0:T(8,128)(2,1)S(1)}, bf16[96,1536]{1,0:T(8,128)(2,1)S(1)}, u32[]{:S(2)}, u32[]{:S(2)}) collective-permute-start(bf16[96,1536]{1,0:T(8,128)(2,1)S(1)} %get-tuple-element.165), channel_id=1, source_target_pairs={{0,2},{2,0},{1,3},{3,1},{4,6},{6,4},{5,7},{7,5},{8,10},{10,8},{9,1... | collective-permute-start | bytes 884744 | tf_op jit(solution)/shard_map/cond/branch_1_fun/ppermute | solution.py:564
  322.0 14.1 %collective-permute-start.3 = (bf16[192,1536]{1,0:T(8,128)(2,1)S(1)}, bf16[192,1536]{1,0:T(8,128)(2,1)S(1)}, u32[]{:S(2)}, u32[]{:S(2)}) collective-permute-start(bf16[192,1536]{1,0:T(8,128)(2,1)S(1)} %constant_dynamic-update-slice_fusion.4), channel_id=1, source_target_pairs={{0,4},{4,0},{1,5},{5,1},{2,6},{6,2},{3,7},{7,3},{8,12},{12,8},{9,1... | collective-permute-start | bytes 1769480 | tf_op jit(solution)/shard_map/cond/branch_1_fun/ppermute | solution.py:564
  322.6 13.8 %collective-permute-start.2 = (bf16[192,1536]{1,0:T(8,128)(2,1)S(1)}, bf16[192,1536]{1,0:T(8,128)(2,1)S(1)}, u32[]{:S(2)}, u32[]{:S(2)}) collective-permute-start(bf16[192,1536]{1,0:T(8,128)(2,1)S(1)} %constant_dynamic-update-slice_fusion.6), channel_id=1, source_target_pairs={{0,2},{2,0},{1,3},{3,1},{4,6},{6,4},{5,7},{7,5},{8,10},{10,8},{9,1... | collective-permute-start | bytes 1769480 | tf_op jit(solution)/shard_map/cond/branch_1_fun/ppermute | solution.py:564
  336.6 5.8 %collective-permute-start.4 = (bf16[768,1536]{1,0:T(8,128)(2,1)S(1)}, bf16[768,1536]{1,0:T(8,128)(2,1)}, u32[]{:S(2)}, u32[]{:S(2)}) collective-permute-start(bf16[768,1536]{1,0:T(8,128)(2,1)S(1)} %pad_maximum_fusion.in_ref), channel_id=1, source_target_pairs={{0,1},{1,0},{2,3},{3,2},{4,5},{5,4},{6,7},{7,6},{8,9},{9,8},{10,11... | collective-permute-start | bytes 7077896 | tf_op jit(solution)/shard_map/cond/branch_1_fun/ppermute | solution.py:564
  (12 other events, 44.1 us)
Sparse Core Ops, SparseCore 0:
  121.5 87.1 reduce-scatter.3
  211.1 66.8 reduce-scatter.5
  308.8 31.9 reduce-scatter.7

commit v6 on v5

--- a/solution.py
+++ b/solution.py
@@ -725,7 +725,7 @@
 
 def widen(a, at, rows, *earlier):
     _, height, wide = a.shape
-    block = math.gcd(height, 384)
+    block = math.gcd(height, 256)
     return call(
         widen_body,
         limit=60,
@@ -789,7 +789,7 @@
     grad_w_out = scatter(grad_outer)
     grad_flat = make_result(chips, after(grad_hidden, grad_outer), inner, experts)
     grad_back = exchange_all(grad_flat).reshape(-1, width)
-    most = width * 3 // 4
+    most = width * 2 // 3
     grad_inner, grad_later = weight_share(
         after(rows_in, grad_flat), grad_hidden, most, width - most
     )
@@ -820,10 +820,10 @@
     both = jnp.concatenate([both, small.reshape(both.shape[:2] + (128,))], 2)
     pieces = pieces_of(both, "dp", 1)
     outputs = collect(after(returned.reshape(-1, width), pieces), col, residual)
-    both = gather_planes(after(add_up(pieces, "dp"), outputs))
+    grad_w_in = widen(after(grad_w_in, pieces), 0, width)
+    both = gather_planes(after(add_up(pieces, "dp"), outputs, grad_w_in))
     small = both[:, :, 2 * width :].reshape(-1, 128)[: 2 * width // 128]
     gains = small.astype(F32).reshape(2, width)
-    grad_w_in = widen(after(grad_w_in, both), 0, width)
     later = scatter(after(grad_later, both))
     core = lax.axis_index("core").reshape(1).astype(jnp.int32)
 
@@ -836,7 +836,7 @@
         return tuple(jnp.zeros((width, wide), F32) for wide in (3 * width, width))
 
     grad_qkv, grad_proj = lax.cond(
-        core[0] < 2, spread, skip, after(both[:, :, : 2 * width], grad_w_in)
+        core[0] < 2, spread, skip, both[:, :, : 2 * width]
     )
     grad_w_in = widen(after(later, grad_qkv), most, width, grad_w_in)
     return (

time: 361 us -> 354 us (0.981)
  waiting for transfers between devices: 61.9 us -> 57.7 us
  transfers between devices with their start and end apart: 32 -> 32, of which waited for: 18 -> 17; matrix products, arithmetic and copies ran while one was open for 1% -> 1% of each run, Pallas kernels for 54% -> 55%
where the time goes in v6:
time: 354 us; the launch traced here: 349 us
  Pallas kernels  226 us (64%)
  waiting for transfers between devices  57.7 us (16%)
  starting transfers between devices  44.2 us (12%)
  between operations  14.2 us (4%)
  local copies, waits for them, and re-layouts  5.46 us (2%)
    ppermute x19, waiting for transfers between devices, shift(): return lax.ppermute(a, axis, [(i, (i + k) % n) for i in range(n)])  41 us
    pallas_call x3, Pallas kernels, expert(): pl.pallas_call(functools.partial(expert_body, parts=parts, kept=len(earli...  38.4 us
    pallas_call x2, Pallas kernels, make_result(): pl.pallas_call(result_body, grid_spec=pltpu.PrefetchScalarGridSpec(num_sc...  31.7 us
    pallas_call x2, Pallas kernels, weight_share(): call(weight_share_body, flops=2 * rows * width * units, moved=2 * (rows *...  29.1 us
    pallas_call x1, Pallas kernels, attend_back(): call(functools.partial(attend_back_body, block=min(256, length)), flops=3...  25.7 us
    pallas_call x1, Pallas kernels, attend(): call(functools.partial(attend_body, block=min(512, length)), flops=120000...  24.3 us
    ppermute x19, starting transfers between devices, shift(): return lax.ppermute(a, axis, [(i, (i + k) % n) for i in range(n)])  22.9 us
    all_to_all x3, starting transfers between devices, exchange_all(): return lax.all_to_all(a, PLANE, split_axis=0, concat_axis=0, tiled=True)  14.2 us
  transfers between devices with their start and end apart: 32, of which 17 were waited for; matrix products, arithmetic and copies ran while one was open for 1% of the time, Pallas kernels for 55%

profile of v6, /device:TPU:0, one launch (start us, length us, event | category | flops | bytes accessed | tf_op | source)
XLA Modules:
  0.0 349.4 jit_solution(1125729713376210554)
XLA Ops:
  7.2 7.1 %shard_map.161 = (s32[1,1024]{1,0:T(1,128)}, s32[1024,1]{1,0:T(8,128)}, bf16[8,256,768]{2,1,0:T(8,128)(2,1)}) custom-call(s32[1,1024]{1,0:T(1,128)} %ids_ref.1, s32[64,128]{1,0:T(8,128)} %bitcast.61, bf16[1024,768]{1,0:T(8,128)(2,1)} %bitcast.56), custom_call_target="tpu_custom_call" | custom-call | flops 3221225472 | bytes 4718592 | tf_op jit(solution)/shard_map/pallas_call | solution.py:111
  14.2 5.3 %all-to-all-start = ((bf16[8,256,768]{2,1,0:T(8,128)(2,1)}), bf16[8,256,768]{2,1,0:T(8,128)(2,1)}, u32[]{:S(2)}, u32[]{:S(2)}) async-start(bf16[8,256,768]{2,1,0:T(8,128)(2,1)} %get-tuple-element.104), calls=%async_computation | async-start | bytes 6291456 | tf_op jit(solution)/shard_map/all_to_all | solution.py:754
  20.9 24.3 %shard_map.162 = (bf16[3,1024,768]{2,1,0:T(8,128)(2,1)}, bf16[1024,768]{1,0:T(8,128)(2,1)}, bf16[1024,768]{1,0:T(8,128)(2,1)}, f32[6,2,1024]{2,1,0:T(2,128)}) custom-call(bf16[1024,768]{1,0:T(8,128)(2,1)} %bitcast.58, f32[1,768]{1,0:T(1,128)} %reshape.64.gain_ref, bf16[768,2304]{1,0:T(8,128)(2,1)} %w_ref.5, bf16[768,2304]{1,0:T(8,128)(2,1)} %w_ref.5, ...), custom_call_target="tpu_custom_call" | custom-call | flops 15623878656 | bytes 12976128 | tf_op jit(solution)/shard_map/pallas_call | solution.py:164
  45.3 8.4 %shard_map.163 = (f32[1024,768]{1,0:T(8,128)}, bf16[256,768]{1,0:T(8,128)(2,1)}, bf16[256,768]{1,0:T(8,128)(2,1)}, bf16[256,768]{1,0:T(8,128)(2,1)}, bf16[256,76...) custom-call(bf16[1024,768]{1,0:T(8,128)(2,1)} %get-tuple-element.93., ...), custom_call_target="tpu_custom_call" | custom-call | flops 4429185024 | bytes 11010048 | tf_op jit(solution)/shard_map/pallas_call | solution.py:258
  59.2 10.7 %shard_map.164 = (bf16[2048,3072]{1,0:T(8,128)(2,1)}, bf16[2048,3072]{1,0:T(8,128)(2,1)}, bf16[2048,768]{1,0:T(8,128)(2,1)}, bf16[2048,768]{1,0:T(8,128)(2,1)}) custom-call(s32[8]{0:T(128)} %stack.64.from_ref, bf16[256,768]{1,0:T(8,128)(2,1)} %get-tuple-element.102.refs_0_, bf16[256,768]{1,0:T(8,128)(2,1)} %copy-done.11, ...), custom_call_target="tpu_custom_call" | custom-call | flops 4831838208 | bytes 18874368 | tf_op jit(solution)/shard_map/pallas_call | solution.py:305
  70.0 3.9 %collective-permute-done.6.refs_1_ = bf16[256,768]{1,0:T(8,128)(2,1)S(1)} collective-permute-done((bf16[256,768]{1,0:T(8,128)(2,1)}, bf16[256,768]{1,0:T(8,128)(2,1)S(1)}, u32[]{:S(2)}, u32[]{:S(2)}) %collective-permute-start.6) | collective-permute-done | bytes 393248 | tf_op jit(solution)/shard_map/ppermute | solution.py:603
  78.1 16.8 %shard_map.165 = (bf16[2048,3072]{1,0:T(8,128)(2,1)}, bf16[2048,3072]{1,0:T(8,128)(2,1)}, bf16[2048,768]{1,0:T(8,128)(2,1)}, bf16[2048,768]{1,0:T(8,128)(2,1)}) custom-call(s32[8]{0:T(128)} %stack.64.from_ref, bf16[256,768]{1,0:T(8,128)(2,1)} %copy-done.2, ...), custom_call_target="tpu_custom_call", output_to_operand_aliasing={{0}: (11, {}), {1}: (12, {}), {2}: (13, {}), {3}: (14, {})} | custom-call | flops 9663676416 | bytes 28311552 | tf_op jit(solution)/shard_map/pallas_call | solution.py:305
  96.0 10.8 %shard_map.166 = (bf16[2048,3072]{1,0:T(8,128)(2,1)}, bf16[2048,3072]{1,0:T(8,128)(2,1)}, bf16[2048,768]{1,0:T(8,128)(2,1)}, bf16[2048,768]{1,0:T(8,128)(2,1)}) custom-call(s32[8]{0:T(128)} %stack.64.from_ref, bf16[256,768]{1,0:T(8,128)(2,1)} %copy-done.6, ...), custom_call_target="tpu_custom_call", output_to_operand_aliasing={{0}: (7, {}), {1}: (8, {}), {2}: (9, {}), {3}: (10, {})} | custom-call | flops 4831838208 | bytes 18874368 | tf_op jit(solution)/shard_map/pallas_call | solution.py:305
  106.8 14.6 %shard_map.167 = bf16[768,3072]{1,0:T(8,128)(2,1)} custom-call(bf16[2048,768]{1,0:T(8,128)(2,1)} %get-tuple-element.118.g_ref, bf16[2048,3072]{1,0:T(8,128)(2,1)} %get-tuple-element.122.act_ref), custom_call_target="tpu_custom_call" | custom-call | flops 9663676416 | bytes 20447232 | tf_op jit(solution)/shard_map/pallas_call | solution.py:341
  122.2 15.8 %shard_map.168 = bf16[8,256,768]{2,1,0:T(8,128)(2,1)} custom-call(s32[4]{0:T(128)} %pad_add_fusion.chip_ref, bf16[2048,3072]{1,0:T(8,128)(2,1)} %get-tuple-element.119.act_ref, bf16[768,3072]{1,0:T(8,128)(2,1)} %bitcast.46), custom_call_target="tpu_custom_call" | custom-call | flops 9663676416 | bytes 20447232 | tf_op jit(solution)/shard_map/pallas_call | solution.py:372
  138.0 4.5 %all-to-all-start.1 = ((bf16[8,256,768]{2,1,0:T(8,128)(2,1)}), bf16[8,256,768]{2,1,0:T(8,128)(2,1)}, u32[]{:S(2)}, u32[]{:S(2)}) async-start(bf16[8,256,768]{2,1,0:T(8,128)(2,1)} %shard_map.168), calls=%async_computation.1 | async-start | bytes 6291456 | tf_op jit(solution)/shard_map/all_to_all | solution.py:754
  142.6 14.5 %shard_map.169 = (bf16[512,3072]{1,0:T(8,128)(2,1)}, bf16[256,3072]{1,0:T(8,128)(2,1)}) custom-call(bf16[2048,768]{1,0:T(8,128)(2,1)} %get-tuple-element.120.g_ref, bf16[2048,3072]{1,0:T(8,128)(2,1)} %get-tuple-element.119.act_ref), custom_call_target="tpu_custom_call" | custom-call | flops 9663676416 | bytes 20447232 | tf_op jit(solution)/shard_map/pallas_call | solution.py:341
  157.1 15.8 %shard_map.170 = bf16[8,256,768]{2,1,0:T(8,128)(2,1)} custom-call(s32[4]{0:T(128)} %pad_add_fusion.chip_ref, bf16[2048,3072]{1,0:T(8,128)(2,1)} %get-tuple-element.122.act_ref, bf16[768,3072]{1,0:T(8,128)(2,1)} %bitcast.50), custom_call_target="tpu_custom_call" | custom-call | flops 9663676416 | bytes 20447232 | tf_op jit(solution)/shard_map/pallas_call | solution.py:372
  173.0 7.5 %all-to-all-done.1 = bf16[8,256,768]{2,1,0:T(8,128)(2,1)} async-done(((bf16[8,256,768]{2,1,0:T(8,128)(2,1)}), bf16[8,256,768]{2,1,0:T(8,128)(2,1)}, u32[]{:S(2)}, u32[]{:S(2)}) %all-to-all-start.1) | async-done | bytes 3145760 | tf_op jit(solution)/shard_map/all_to_all | solution.py:754
  180.4 4.5 %all-to-all-start.2 = ((bf16[8,256,768]{2,1,0:T(8,128)(2,1)}), bf16[8,256,768]{2,1,0:T(8,128)(2,1)}, u32[]{:S(2)}, u32[]{:S(2)}) async-start(bf16[8,256,768]{2,1,0:T(8,128)(2,1)} %shard_map.170), calls=%async_computation.2 | async-start | bytes 6291456 | tf_op jit(solution)/shard_map/all_to_all | solution.py:754
  184.9 13.3 %shard_map.171 = (f32[1024,768]{1,0:T(8,128)}, bf16[1024,768]{1,0:T(8,128)(2,1)}, bf16[1024,768]{1,0:T(8,128)(2,1)}, f32[1,768]{1,0:T(1,128)}) custom-call(s32[1024,1]{1,0:T(8,128)} %get-tuple-element.92.col_ref, f32[1024,768]{1,0:T(8,128)} %get-tuple-element.95.res_ref, bf16[1024,768]{1,0:T(8,128)(2,1)} %bitcast.57, f32[1,768]{1,0:T(1,128)} %reshape.65.gain_ref, ...), custom_call_target="tpu_custom_call" | custom-call | flops 5637144576 | bytes 15728640 | tf_op jit(solution)/shard_map/pallas_call | solution.py:420
  198.2 25.7 %shard_map.172.g_ref = bf16[3,1024,768]{2,1,0:T(8,128)(2,1)} custom-call(bf16[3,1024,768]{2,1,0:T(8,128)(2,1)} %get-tuple-element.125.packed_ref, bf16[1024,768]{1,0:T(8,128)(2,1)} %get-tuple-element.93.att_ref.o_ref, bf16[1024,768]{1,0:T(8,128)(2,1)} %get-tuple-element.127.up_ref, f32[6,2,1024]{2,1,0:T(2,128)} %get-tuple-element.128.total_ref), custom_call_target="tpu_custom_call" | custom-call | flops 30000001024 | bytes 12582912 | tf_op jit(solution)/shard_map/pallas_call | solution.py:229
  223.9 11.5 %shard_map.173 = (bf16[768,1536]{1,0:T(8,128)(2,1)}, bf16[768,1536]{1,0:T(8,128)(2,1)}) custom-call(bf16[1024,768]{1,0:T(8,128)(2,1)} %get-tuple-element.124.normed_ref, bf16[3,1024,768]{2,1,0:T(8,128)(2,1)} %shard_map.172.g_ref, bf16[1024,768]{1,0:T(8,128)(2,1)} %get-tuple-element.93.att_ref.o_ref, bf16[1024,768]{1,0:T(8,128)(2,1)} %get-tuple-element.129.gattn_ref), custom_call_target="tpu_custom_call" | custom-call | flops 4831838208 | bytes 14155776 | tf_op jit(solution)/shard_map/pallas_call | solution.py:504
  235.6 3.4 shard_map.174
  240.2 3.1 shard_map.175
  246.7 10.0 %shard_map.176 = (f32[1024,768]{1,0:T(8,128)}, f32[1,768]{1,0:T(1,128)}) custom-call(bf16[1024,768]{1,0:T(8,128)(2,1)} %bitcast.60, f32[1,768]{1,0:T(1,128)} %reshape.64.gain_ref, bf16[768,2304]{1,0:T(8,128)(2,1)} %w_ref.5, bf16[3,1024,768]{2,1,0:T(8,128)(2,1)} %shard_map.172.g_ref, f32[1024,768]{1,0:T(8,128)} %get-tuple-element.139.gres_ref), custom_call_target="tpu_custom_call" | custom-call | flops 3623878656 | bytes 14155776 | tf_op jit(solution)/shard_map/pallas_call | solution.py:544
  265.8 4.6 %collective-permute-done.18 = f32[12,128]{1,0:T(8,128)S(1)} collective-permute-done((f32[12,128]{1,0:T(8,128)S(1)}, f32[12,128]{1,0:T(8,128)S(1)}, u32[]{:S(2)}, u32[]{:S(2)}) %collective-permute-start.18) | collective-permute-done | bytes 6176 | tf_op jit(solution)/shard_map/ppermute | solution.py:564
  271.0 3.1 collective-permute-done.19
  282.5 7.4 %shard_map.177 = bf16[1024,768]{1,0:T(8,128)(2,1)} custom-call(s32[1024,1]{1,0:T(8,128)} %get-tuple-element.92.col_ref, f32[1024,768]{1,0:T(8,128)} %get-tuple-element.95.res_ref, bf16[2048,768]{1,0:T(8,128)(2,1)} %bitcast.21.back_ref), custom_call_target="tpu_custom_call" | custom-call | flops 3221225472 | bytes 7864320 | tf_op jit(solution)/shard_map/pallas_call | solution.py:448
  294.1 4.3 %collective-permute-done.23 = bf16[2,24,1664]{2,1,0:T(8,128)(2,1)S(1)} collective-permute-done((bf16[2,24,1664]{2,1,0:T(8,128)(2,1)S(1)}, bf16[2,24,1664]{2,1,0:T(8,128)(2,1)S(1)}, u32[]{:S(2)}, u32[]{:S(2)}) %collective-permute-start.23) | collective-permute-done | bytes 159776 | tf_op jit(solution)/shard_map/ppermute | solution.py:564
  298.3 4.1 %collective-permute-done.24 = bf16[2,24,1664]{2,1,0:T(8,128)(2,1)S(1)} collective-permute-done((bf16[2,24,1664]{2,1,0:T(8,128)(2,1)S(1)}, bf16[2,24,1664]{2,1,0:T(8,128)(2,1)S(1)}, u32[]{:S(2)}, u32[]{:S(2)}) %collective-permute-start.24) | collective-permute-done | bytes 159776 | tf_op jit(solution)/shard_map/ppermute | solution.py:564
  302.5 34.9 %conditional.1 = ((f32[768,2304]{1,0:T(8,128)}, f32[768,768]{1,0:T(8,128)})) conditional(s32[]{:T(128)} %convert_element_type.76, () %tuple.47, (s32[]{:T(128)}, bf16[2,96,1664]{2,1,0:T(8,128)(2,1)S(1)}) %tuple.48), branch_computations={%region_2.3_spmd, %region_3.4_spmd} | conditional | flops 4718645 | bytes 56623972 | solution.py:838
  305.8 5.4 %collective-permute-done = bf16[96,1536]{1,0:T(8,128)(2,1)S(1)} collective-permute-done((bf16[96,1536]{1,0:T(8,128)(2,1)S(1)}, bf16[96,1536]{1,0:T(8,128)(2,1)S(1)}, u32[]{:S(2)}, u32[]{:S(2)}) %collective-permute-start) | collective-permute-done | bytes 294944 | tf_op jit(solution)/shard_map/cond/branch_1_fun/ppermute | solution.py:564
  315.1 11.7 %collective-permute-done.3 = bf16[192,1536]{1,0:T(8,128)(2,1)S(1)} collective-permute-done((bf16[192,1536]{1,0:T(8,128)(2,1)S(1)}, bf16[192,1536]{1,0:T(8,128)(2,1)S(1)}, u32[]{:S(2)}, u32[]{:S(2)}) %collective-permute-start.3) | collective-permute-done | bytes 589856 | tf_op jit(solution)/shard_map/cond/branch_1_fun/ppermute | solution.py:564
  328.8 4.3 %branch_1_fun.2 = (f32[768,2304]{1,0:T(8,128)}, f32[768,768]{1,0:T(8,128)}) custom-call(s32[1]{0:T(128)} %bitcast.core_ref, bf16[768,1536]{1,0:T(8,128)(2,1)} %copy-done.1), custom_call_target="tpu_custom_call" | custom-call | bytes 7077888 | tf_op jit(solution)/shard_map/cond/branch_1_fun/pallas_call | solution.py:702
  333.1 4.3 %branch_1_fun.3 = (f32[768,2304]{1,0:T(8,128)}, f32[768,768]{1,0:T(8,128)}) custom-call(s32[1]{0:T(128)S(6)} %sub.5.core_ref, bf16[768,1536]{1,0:T(8,128)(2,1)} %collective-permute-done.4.in_ref, f32[768,2304]{1,0:T(8,128)} %get-tuple-element.12.refs_0_, f32[768,768]{1,0:T(8,128)} %get-tuple-element.13.refs_1_), custom_call_target="tpu_custom_call", output_to_operand_aliasing={{0}: (2, {}), {1}: (3, {})} | custom-call | bytes 7077888 | tf_op jit(solution)/shard_map/cond/branch_1_fun/pallas_call | solution.py:702
  338.0 2.8 reduce-scatter.8.cloned.1.call-done.in_ref
  (120 shorter events, 51.4 us)
Async XLA Ops:
  14.2 44.2 %all-to-all-start = ((bf16[8,256,768]{2,1,0:T(8,128)(2,1)}), bf16[8,256,768]{2,1,0:T(8,128)(2,1)}, u32[]{:S(2)}, u32[]{:S(2)}) async-start(bf16[8,256,768]{2,1,0:T(8,128)(2,1)} %get-tuple-element.104), calls=%async_computation | async-start | bytes 6291456 | tf_op jit(solution)/shard_map/all_to_all | solution.py:754
  19.5 216.1 %reduce-scatter.4.cloned.1.call-start = ((), (), s32[]{:S(2)}) async-start(), calls=%async_computation.6 | async-start | bytes 5898240 | tf_op jit(solution)/shard_map/reduce_scatter | solution.py:786
  53.7 4.8 %collective-permute-start.9 = (bf16[256,768]{1,0:T(8,128)(2,1)}, bf16[256,768]{1,0:T(8,128)(2,1)S(1)}, u32[]{:S(2)}, u32[]{:S(2)}) collective-permute-start(bf16[256,768]{1,0:T(8,128)(2,1)} %get-tuple-element.103), channel_id=1, source_target_pairs={{0,1},{1,0},{2,3},{3,2},{4,5},{5,4},{6,7},{7,6},{8,9},{9,8},{10,11... | collective-permute-start | bytes 1179656 | tf_op jit(solution)/shard_map/ppermute | solution.py:603
  54.1 15.8 %collective-permute-start.5 = (bf16[256,768]{1,0:T(8,128)(2,1)}, bf16[256,768]{1,0:T(8,128)(2,1)S(1)}, u32[]{:S(2)}, u32[]{:S(2)}) collective-permute-start(bf16[256,768]{1,0:T(8,128)(2,1)} %get-tuple-element.98), channel_id=1, source_target_pairs={{0,2},{1,3},{2,0},{3,1},{4,6},{5,7},{6,4},{7,5},{8,10},{9,11},{10,... | collective-permute-start | bytes 1179656 | tf_op jit(solution)/shard_map/ppermute | solution.py:603
  55.9 18.0 %collective-permute-start.6 = (bf16[256,768]{1,0:T(8,128)(2,1)}, bf16[256,768]{1,0:T(8,128)(2,1)S(1)}, u32[]{:S(2)}, u32[]{:S(2)}) collective-permute-start(bf16[256,768]{1,0:T(8,128)(2,1)} %get-tuple-element.99), channel_id=1, source_target_pairs={{0,3},{1,2},{2,1},{3,0},{4,7},{5,6},{6,5},{7,4},{8,11},{9,10},{10,... | collective-permute-start | bytes 1179656 | tf_op jit(solution)/shard_map/ppermute | solution.py:603
  56.0 17.9 %collective-permute-start.7 = (bf16[256,768]{1,0:T(8,128)(2,1)}, bf16[256,768]{1,0:T(8,128)(2,1)S(1)}, u32[]{:S(2)}, u32[]{:S(2)}) collective-permute-start(bf16[256,768]{1,0:T(8,128)(2,1)} %get-tuple-element.100), channel_id=1, source_target_pairs={{0,4},{1,5},{2,6},{3,7},{4,0},{5,1},{6,2},{7,3},{8,12},{9,13},{10,... | collective-permute-start | bytes 1179656 | tf_op jit(solution)/shard_map/ppermute | solution.py:603
  57.8 17.6 %collective-permute-start.8 = (bf16[256,768]{1,0:T(8,128)(2,1)}, bf16[256,768]{1,0:T(8,128)(2,1)S(1)}, u32[]{:S(2)}, u32[]{:S(2)}) collective-permute-start(bf16[256,768]{1,0:T(8,128)(2,1)} %get-tuple-element.101), channel_id=1, source_target_pairs={{0,5},{1,4},{2,7},{3,6},{4,1},{5,0},{6,3},{7,2},{8,13},{9,12},{10,... | collective-permute-start | bytes 1179656 | tf_op jit(solution)/shard_map/ppermute | solution.py:603
  75.3 19.6 %collective-permute-start.10 = (bf16[256,768]{1,0:T(8,128)(2,1)}, bf16[256,768]{1,0:T(8,128)(2,1)S(1)}, u32[]{:S(2)}, u32[]{:S(2)}) collective-permute-start(bf16[256,768]{1,0:T(8,128)(2,1)} %get-tuple-element.106), channel_id=1, source_target_pairs={{0,6},{1,7},{2,4},{3,5},{4,2},{5,3},{6,0},{7,1},{8,14},{9,15},{10,... | collective-permute-start | bytes 1179656 | tf_op jit(solution)/shard_map/ppermute | solution.py:603
  78.0 18.0 %collective-permute-start.11 = (bf16[256,768]{1,0:T(8,128)(2,1)}, bf16[256,768]{1,0:T(8,128)(2,1)}, u32[]{:S(2)}, u32[]{:S(2)}) collective-permute-start(bf16[256,768]{1,0:T(8,128)(2,1)} %get-tuple-element.107), channel_id=1, source_target_pairs={{0,7},{1,6},{2,5},{3,4},{4,3},{5,2},{6,1},{7,0},{8,15},{9,14},{10,... | collective-permute-start | bytes 1179656 | tf_op jit(solution)/shard_map/ppermute | solution.py:603
  138.0 42.4 %all-to-all-start.1 = ((bf16[8,256,768]{2,1,0:T(8,128)(2,1)}), bf16[8,256,768]{2,1,0:T(8,128)(2,1)}, u32[]{:S(2)}, u32[]{:S(2)}) async-start(bf16[8,256,768]{2,1,0:T(8,128)(2,1)} %shard_map.168), calls=%async_computation.1 | async-start | bytes 6291456 | tf_op jit(solution)/shard_map/all_to_all | solution.py:754
  142.5 131.6 %reduce-scatter.6.cloned.1.call-start = ((), (), s32[]{:S(2)}) async-start(), calls=%async_computation.7 | async-start | bytes 3932160 | tf_op jit(solution)/shard_map/reduce_scatter | solution.py:786
  180.4 59.8 %all-to-all-start.2 = ((bf16[8,256,768]{2,1,0:T(8,128)(2,1)}), bf16[8,256,768]{2,1,0:T(8,128)(2,1)}, u32[]{:S(2)}, u32[]{:S(2)}) async-start(bf16[8,256,768]{2,1,0:T(8,128)(2,1)} %shard_map.170), calls=%async_computation.2 | async-start | bytes 6291456 | tf_op jit(solution)/shard_map/all_to_all | solution.py:754
  184.9 155.9 %reduce-scatter.8.cloned.1.call-start = ((), (), s32[]{:S(2)}) async-start(), calls=%async_computation.8 | async-start | bytes 1966080 | tf_op jit(solution)/shard_map/reduce_scatter | solution.py:786
  235.4 4.9 %collective-permute-start.12 = (bf16[768,1536]{1,0:T(8,128)(2,1)}, bf16[768,1536]{1,0:T(8,128)(2,1)}, u32[]{:S(2)}, u32[]{:S(2)}) collective-permute-start(bf16[768,1536]{1,0:T(8,128)(2,1)} %get-tuple-element.131), channel_id=1, source_target_pairs={{0,1},{1,0},{2,3},{3,2},{4,5},{5,4},{6,7},{7,6},{8,9},{9,8},{10,11... | collective-permute-start | bytes 7077896 | tf_op jit(solution)/shard_map/ppermute | solution.py:564
  243.4 15.7 %collective-permute-start.13 = (bf16[192,1536]{1,0:T(8,128)(2,1)}, bf16[192,1536]{1,0:T(8,128)(2,1)S(1)}, u32[]{:S(2)}, u32[]{:S(2)}) collective-permute-start(bf16[192,1536]{1,0:T(8,128)(2,1)} %get-tuple-element.135), channel_id=1, source_target_pairs={{0,2},{2,0},{1,3},{3,1},{4,6},{6,4},{5,7},{7,5},{8,10},{10,8},{9,1... | collective-permute-start | bytes 1769480 | tf_op jit(solution)/shard_map/ppermute | solution.py:564
  245.2 15.3 %collective-permute-start.14 = (bf16[192,1536]{1,0:T(8,128)(2,1)}, bf16[192,1536]{1,0:T(8,128)(2,1)S(1)}, u32[]{:S(2)}, u32[]{:S(2)}) collective-permute-start(bf16[192,1536]{1,0:T(8,128)(2,1)} %get-tuple-element.137), channel_id=1, source_target_pairs={{0,4},{4,0},{1,5},{5,1},{2,6},{6,2},{3,7},{7,3},{8,12},{12,8},{9,1... | collective-permute-start | bytes 1769480 | tf_op jit(solution)/shard_map/ppermute | solution.py:564
  260.9 13.3 %collective-permute-start.15 = (bf16[96,1536]{1,0:T(8,128)(2,1)S(1)}, bf16[96,1536]{1,0:T(8,128)(2,1)S(1)}, u32[]{:S(2)}, u32[]{:S(2)}) collective-permute-start(bf16[96,1536]{1,0:T(8,128)(2,1)S(1)} %get-tuple-element.172), channel_id=1, source_target_pairs={{0,4},{4,0},{1,5},{5,1},{2,6},{6,2},{3,7},{7,3},{8,12},{12,8},{9,1... | collective-permute-start | bytes 884744 | tf_op jit(solution)/shard_map/ppermute | solution.py:564
  262.5 11.7 %collective-permute-start.16 = (bf16[96,1536]{1,0:T(8,128)(2,1)S(1)}, bf16[96,1536]{1,0:T(8,128)(2,1)S(1)}, u32[]{:S(2)}, u32[]{:S(2)}) collective-permute-start(bf16[96,1536]{1,0:T(8,128)(2,1)S(1)} %get-tuple-element.170), channel_id=1, source_target_pairs={{0,2},{2,0},{1,3},{3,1},{4,6},{6,4},{5,7},{7,5},{8,10},{10,8},{9,1... | collective-permute-start | bytes 884744 | tf_op jit(solution)/shard_map/ppermute | solution.py:564
  263.1 1.2 collective-permute-start.17
  264.4 6.1 %collective-permute-start.18 = (f32[12,128]{1,0:T(8,128)S(1)}, f32[12,128]{1,0:T(8,128)S(1)}, u32[]{:S(2)}, u32[]{:S(2)}) collective-permute-start(f32[12,128]{1,0:T(8,128)S(1)} %add.228), channel_id=1, source_target_pairs={{0,2},{2,0},{1,3},{3,1},{4,6},{6,4},{5,7},{7,5},{8,10},{10,8},{9,1... | collective-permute-start | bytes 18440 | tf_op jit(solution)/shard_map/ppermute | solution.py:564
  270.4 3.7 %collective-permute-start.19 = (f32[12,128]{1,0:T(8,128)S(1)}, f32[12,128]{1,0:T(8,128)S(1)}, u32[]{:S(2)}, u32[]{:S(2)}) collective-permute-start(f32[12,128]{1,0:T(8,128)S(1)} %add.229), channel_id=1, source_target_pairs={{0,4},{4,0},{1,5},{5,1},{2,6},{6,2},{3,7},{7,3},{8,12},{12,8},{9,1... | collective-permute-start | bytes 18440 | tf_op jit(solution)/shard_map/ppermute | solution.py:564
  274.4 15.5 %collective-permute-start.20 = (bf16[2,24,1664]{2,1,0:T(8,128)(2,1)S(1)}, bf16[2,24,1664]{2,1,0:T(8,128)(2,1)S(1)}, u32[]{:S(2)}, u32[]{:S(2)}) collective-permute-start(bf16[2,24,1664]{2,1,0:T(8,128)(2,1)S(1)} %get-tuple-element.168), channel_id=1, source_target_pairs={{0,8},{8,16},{16,24},{24,0},{1,9},{9,17},{17,25},{25,1},{2,10},{10... | collective-permute-start | bytes 479240 | tf_op jit(solution)/shard_map/ppermute | solution.py:564
  276.5 13.5 %collective-permute-start.21 = (bf16[2,24,1664]{2,1,0:T(8,128)(2,1)S(1)}, bf16[2,24,1664]{2,1,0:T(8,128)(2,1)S(1)}, u32[]{:S(2)}, u32[]{:S(2)}) collective-permute-start(bf16[2,24,1664]{2,1,0:T(8,128)(2,1)S(1)} %get-tuple-element.167), channel_id=1, source_target_pairs={{0,16},{8,24},{16,0},{24,8},{1,17},{9,25},{17,1},{25,9},{2,18},{10... | collective-permute-start | bytes 479240 | tf_op jit(solution)/shard_map/ppermute | solution.py:564
  279.1 10.9 %collective-permute-start.22 = (bf16[2,24,1664]{2,1,0:T(8,128)(2,1)S(1)}, bf16[2,24,1664]{2,1,0:T(8,128)(2,1)S(1)}, u32[]{:S(2)}, u32[]{:S(2)}) collective-permute-start(bf16[2,24,1664]{2,1,0:T(8,128)(2,1)S(1)} %get-tuple-element.166), channel_id=1, source_target_pairs={{0,24},{8,0},{16,8},{24,16},{1,25},{9,1},{17,9},{25,17},{2,26},{10... | collective-permute-start | bytes 479240 | tf_op jit(solution)/shard_map/ppermute | solution.py:564
  290.2 8.1 %collective-permute-start.23 = (bf16[2,24,1664]{2,1,0:T(8,128)(2,1)S(1)}, bf16[2,24,1664]{2,1,0:T(8,128)(2,1)S(1)}, u32[]{:S(2)}, u32[]{:S(2)}) collective-permute-start(bf16[2,24,1664]{2,1,0:T(8,128)(2,1)S(1)} %get-tuple-element.163), channel_id=1, source_target_pairs={{0,8},{8,16},{16,24},{24,0},{1,9},{9,17},{17,25},{25,1},{2,10},{10... | collective-permute-start | bytes 479240 | tf_op jit(solution)/shard_map/ppermute | solution.py:564
  291.0 11.4 %collective-permute-start.24 = (bf16[2,24,1664]{2,1,0:T(8,128)(2,1)S(1)}, bf16[2,24,1664]{2,1,0:T(8,128)(2,1)S(1)}, u32[]{:S(2)}, u32[]{:S(2)}) collective-permute-start(bf16[2,24,1664]{2,1,0:T(8,128)(2,1)S(1)} %get-tuple-element.163), channel_id=1, source_target_pairs={{0,16},{8,24},{16,0},{24,8},{1,17},{9,25},{17,1},{25,9},{2,18},{10... | collective-permute-start | bytes 479240 | tf_op jit(solution)/shard_map/ppermute | solution.py:564
  292.5 9.9 %collective-permute-start.25 = (bf16[2,24,1664]{2,1,0:T(8,128)(2,1)S(1)}, bf16[2,24,1664]{2,1,0:T(8,128)(2,1)S(1)}, u32[]{:S(2)}, u32[]{:S(2)}) collective-permute-start(bf16[2,24,1664]{2,1,0:T(8,128)(2,1)S(1)} %get-tuple-element.163), channel_id=1, source_target_pairs={{0,24},{8,0},{16,8},{24,16},{1,25},{9,1},{17,9},{25,17},{2,26},{10... | collective-permute-start | bytes 479240 | tf_op jit(solution)/shard_map/ppermute | solution.py:564
  302.5 8.7 %collective-permute-start = (bf16[96,1536]{1,0:T(8,128)(2,1)S(1)}, bf16[96,1536]{1,0:T(8,128)(2,1)S(1)}, u32[]{:S(2)}, u32[]{:S(2)}) collective-permute-start(bf16[96,1536]{1,0:T(8,128)(2,1)S(1)} %get-tuple-element.165), channel_id=1, source_target_pairs={{0,4},{4,0},{1,5},{5,1},{2,6},{6,2},{3,7},{7,3},{8,12},{12,8},{9,1... | collective-permute-start | bytes 884744 | tf_op jit(solution)/shard_map/cond/branch_1_fun/ppermute | solution.py:564
  304.1 8.6 %collective-permute-start.1 = (bf16[96,1536]{1,0:T(8,128)(2,1)S(1)}, bf16[96,1536]{1,0:T(8,128)(2,1)S(1)}, u32[]{:S(2)}, u32[]{:S(2)}) collective-permute-start(bf16[96,1536]{1,0:T(8,128)(2,1)S(1)} %get-tuple-element.164), channel_id=1, source_target_pairs={{0,2},{2,0},{1,3},{3,1},{4,6},{6,4},{5,7},{7,5},{8,10},{10,8},{9,1... | collective-permute-start | bytes 884744 | tf_op jit(solution)/shard_map/cond/branch_1_fun/ppermute | solution.py:564
  312.7 14.0 %collective-permute-start.3 = (bf16[192,1536]{1,0:T(8,128)(2,1)S(1)}, bf16[192,1536]{1,0:T(8,128)(2,1)S(1)}, u32[]{:S(2)}, u32[]{:S(2)}) collective-permute-start(bf16[192,1536]{1,0:T(8,128)(2,1)S(1)} %constant_dynamic-update-slice_fusion.4), channel_id=1, source_target_pairs={{0,4},{4,0},{1,5},{5,1},{2,6},{6,2},{3,7},{7,3},{8,12},{12,8},{9,1... | collective-permute-start | bytes 1769480 | tf_op jit(solution)/shard_map/cond/branch_1_fun/ppermute | solution.py:564
  313.1 14.0 %collective-permute-start.2 = (bf16[192,1536]{1,0:T(8,128)(2,1)S(1)}, bf16[192,1536]{1,0:T(8,128)(2,1)S(1)}, u32[]{:S(2)}, u32[]{:S(2)}) collective-permute-start(bf16[192,1536]{1,0:T(8,128)(2,1)S(1)} %constant_dynamic-update-slice_fusion.6), channel_id=1, source_target_pairs={{0,2},{2,0},{1,3},{3,1},{4,6},{6,4},{5,7},{7,5},{8,10},{10,8},{9,1... | collective-permute-start | bytes 1769480 | tf_op jit(solution)/shard_map/cond/branch_1_fun/ppermute | solution.py:564
  327.3 5.8 %collective-permute-start.4 = (bf16[768,1536]{1,0:T(8,128)(2,1)S(1)}, bf16[768,1536]{1,0:T(8,128)(2,1)}, u32[]{:S(2)}, u32[]{:S(2)}) collective-permute-start(bf16[768,1536]{1,0:T(8,128)(2,1)S(1)} %pad_maximum_fusion.in_ref), channel_id=1, source_target_pairs={{0,1},{1,0},{2,3},{3,2},{4,5},{5,4},{6,7},{7,6},{8,9},{9,8},{10,11... | collective-permute-start | bytes 7077896 | tf_op jit(solution)/shard_map/cond/branch_1_fun/ppermute | solution.py:564
  (12 other events, 44.1 us)
Sparse Core Ops, SparseCore 0:
  121.6 87.1 reduce-scatter.3
  211.1 60.7 reduce-scatter.5
  302.6 38.1 reduce-scatter.7
